TPU v7x, 128 devices: a whole 4x4x4 slice. The times are simulated.
128 devices in a mesh: row: 4 (over z), col: 16 (over x, y), depth: 2 (over core).
Axes of the slice: x: 4, y: 4, z: 4, core: 2. Of those that a mesh axis runs over, the one named last changes fastest.
Arguments:
- tiles: float32 [4, 16, 96, 256, 256], P('row', 'col', 'depth'), as said below
- tile_rows: int32 [4, 16, 96], P('row', 'col', 'depth'), may hold values from 0 to 127, as said below
- tile_cols: int32 [4, 16, 96], P('row', 'col', 'depth'), may hold values from 0 to 127
- tile_count: int32 [4, 16, 2], P('row', 'col', 'depth'), may hold values from 16 to 48, as said below
Outputs:
- row_scale: float32 [131072], P('row')
- col_scale: float32 [524288], P('col')
- scaled_tiles: float32 [4, 16, 96, 256, 256], P('row', 'col', 'depth')
Inputs may be any that keep to these rules, and one draw needn't show every extreme that they name: `tile_rows`: every block row and every block column of the matrix holds a live tile; no block is listed twice among the live tiles of the two depth lists of one row and col index. `tile_count`: some device's list is full in every draw. `tiles`: entries in empty slots are ignored.
All inputs are finite; a program needn't handle non-finite values.
Results may differ from a plain program's by a relative error of at most 0.0001.
Values sent between devices are 32-bit elements; how exact they have to be, the bound alone decides.
No kernel may reach another device: no remote copies, remote signals or barrier semaphores. Data moves between devices by JAX's collectives and lax.ppermute only.
A program may use at most 128 MiB of HBM per device.

v0:
```python
import math

import jax
import jax.numpy as jnp
from jax import lax
from jax.sharding import PartitionSpec as P

RB_DEV = 128
ANCHORS = 16
SWEEPS = 4


EPS = 1e-06


def shards(tiles, tile_rows, tile_cols, tile_count):
    all_values = tiles[0, 0]
    row_index = tile_rows[0, 0]
    col_index = tile_cols[0, 0]
    live_count = tile_count[0, 0, 0]
    slot_count = all_values.shape[0]
    tile_size = all_values.shape[1]
    col_blocks = lax.axis_size("row") * lax.axis_size("depth") * ANCHORS
    group_size = math.gcd(slot_count, 8)
    block_count = (live_count + group_size - 1) // group_size
    row_ids = jnp.arange(RB_DEV, dtype=jnp.int32)
    col_ids = jnp.arange(col_blocks, dtype=jnp.int32)

    def partials(row_now, col_now, summed):

        def step_block(position, carry):
            row_acc, col_acc = carry
            first_slot = position * group_size
            block_values = lax.dynamic_slice_in_dim(all_values, first_slot, group_size, 0)
            block_rows = lax.dynamic_slice_in_dim(row_index, first_slot, group_size, 0)
            block_cols = lax.dynamic_slice_in_dim(col_index, first_slot, group_size, 0)
            live_mask = first_slot + jnp.arange(group_size, dtype=jnp.int32) < live_count
            scaled = (
                block_values * row_now[block_rows][:, :, None] * col_now[block_cols][:, None, :]
            )
            magnitude = jnp.where(live_mask[:, None, None], jnp.abs(scaled), jnp.float32(0.0))
            row_hit = row_ids[:, None] == block_rows[None, :]
            col_hit = col_ids[:, None] == block_cols[None, :]
            if summed:
                row_acc = row_acc + jnp.dot(
                    row_hit.astype(jnp.float32),
                    magnitude.sum(axis=2),
                    precision=lax.Precision.HIGHEST,
                )
                col_acc = col_acc + jnp.dot(
                    col_hit.astype(jnp.float32),
                    magnitude.sum(axis=1),
                    precision=lax.Precision.HIGHEST,
                )
            else:
                row_acc = jnp.maximum(
                    row_acc,
                    jnp.where(
                        row_hit[:, :, None], magnitude.max(axis=2)[None], jnp.float32(0.0)
                    ).max(axis=1),
                )
                col_acc = jnp.maximum(
                    col_acc,
                    jnp.where(
                        col_hit[:, :, None], magnitude.max(axis=1)[None], jnp.float32(0.0)
                    ).max(axis=1),
                )
            return (row_acc, col_acc)

        initial = (
            jnp.zeros((RB_DEV, tile_size), jnp.float32),
            jnp.zeros((col_blocks, tile_size), jnp.float32),
        )
        return lax.fori_loop(0, block_count, step_block, initial)

    row_factor = jnp.ones((RB_DEV, tile_size), jnp.float32)
    col_factor = jnp.ones((col_blocks, tile_size), jnp.float32)
    for sweep_index in range(SWEEPS):
        row_part, col_part = partials(row_factor, col_factor, False)
        row_peak = lax.pmax(row_part, ("col", "depth"))
        col_peak = lax.pmax(col_part, ("row", "depth"))
        row_factor = row_factor * lax.rsqrt(row_peak + EPS)
        col_factor = col_factor * lax.rsqrt(col_peak + EPS)
    row_part, col_part = partials(row_factor, col_factor, True)
    row_mass = lax.psum(row_part, ("col", "depth"))
    col_mass = lax.psum(col_part, ("row", "depth"))
    row_factor = row_factor * lax.rsqrt(row_mass + EPS)
    col_factor = col_factor * lax.rsqrt(col_mass + EPS)
    live_all = jnp.arange(slot_count, dtype=jnp.int32) < live_count
    scaled_all = all_values * row_factor[row_index][:, :, None] * col_factor[col_index][:, None, :]
    scaled_all = jnp.where(live_all[:, None, None], scaled_all, jnp.float32(0.0))
    return (row_factor.reshape(-1), col_factor.reshape(-1), scaled_all[None, None])


def solution(mesh):
    in_specs = (
        P("row", "col", "depth", None, None),
        P("row", "col", "depth"),
        P("row", "col", "depth"),
        P("row", "col", "depth"),
    )
    out_specs = (P("row"), P("col"), P("row", "col", "depth", None, None))
    return jax.shard_map(shards, mesh=mesh, in_specs=in_specs, out_specs=out_specs, check_vma=False)
```

profile of v0, /device:TPU:1, one launch (start us, length us, event | category | flops | bytes accessed | tf_op | source)
XLA Modules:
  0.0 1013.1 jit_solution(7620673832992945533)
XLA Ops:
  7.9 29.2 %while.75 = (s32[]{:T(128)}, f32[128,256]{1,0:T(8,128)S(1)}, f32[128,256]{1,0:T(8,128)S(1)}, s32[]{:T(128)}, s32[48]{0:T(128)}, /*index=5*/s32[]{:T(128)}, f32[4...) while((s32[]{:T(128)}, f32[128,256]{1,0:T(8,128)S(1)}, ...), condition=%wide.region_5.6_spmd.clone.clone, body=%wide.region_0.5_spmd.clone.clone.sunk | while | flops 4194374 | bytes 3371599 | solution.py:74
  10.6 2.3 fusion.33
  16.4 2.3 fusion.33
  22.3 2.3 fusion.33
  28.1 2.3 fusion.33
  34.0 2.3 fusion.33
  39.3 106.7 %all-reduce.11.cloned.1.call-done = f32[128,256]{1,0:T(8,128)} async-done(((f32[128,256]{1,0:T(8,128)}), f32[128,256]{1,0:T(8,128)}) %all-reduce.11.cloned.1.call-update) | async-done | bytes 131088 | tf_op jit(solution)/shard_map/pmax | solution.py:80
  146.9 59.1 %all-reduce.13.cloned.1.call-done = f32[128,256]{1,0:T(8,128)} async-done(((f32[128,256]{1,0:T(8,128)}), f32[128,256]{1,0:T(8,128)}) %all-reduce.13.cloned.1.call-update) | async-done | bytes 131088 | tf_op jit(solution)/shard_map/pmax | solution.py:81
  207.0 29.2 %while.76 = (s32[]{:T(128)}, f32[128,256]{1,0:T(8,128)S(1)}, f32[128,256]{1,0:T(8,128)S(1)}, s32[]{:T(128)}, s32[48]{0:T(128)}, /*index=5*/s32[]{:T(128)}, f32[4...) while((s32[]{:T(128)}, f32[128,256]{1,0:T(8,128)S(1)}, ...), condition=%wide.region_13.14_spmd.clone.clone, body=%wide.region_8.13_spmd.clone.clone.sunk | while | flops 4194374 | bytes 3240531 | solution.py:74
  209.7 2.3 fusion.34
  215.5 2.3 fusion.34
  221.3 2.3 fusion.34
  227.2 2.3 fusion.34
  233.0 2.3 fusion.34
  237.7 63.0 %all-reduce.17.cloned.1.call-done = f32[128,256]{1,0:T(8,128)} async-done(((f32[128,256]{1,0:T(8,128)}), f32[128,256]{1,0:T(8,128)}) %all-reduce.17.cloned.1.call-update) | async-done | bytes 131088 | tf_op jit(solution)/shard_map/pmax | solution.py:81
  301.7 103.3 %all-reduce.15.cloned.1.call-done = f32[128,256]{1,0:T(8,128)} async-done(((f32[128,256]{1,0:T(8,128)}), f32[128,256]{1,0:T(8,128)}) %all-reduce.15.cloned.1.call-update) | async-done | bytes 131088 | tf_op jit(solution)/shard_map/pmax | solution.py:80
  406.0 29.1 %while.77 = (s32[]{:T(128)}, f32[128,256]{1,0:T(8,128)S(1)}, f32[128,256]{1,0:T(8,128)S(1)}, s32[]{:T(128)}, s32[48]{0:T(128)}, /*index=5*/s32[]{:T(128)}, f32[4...) while((s32[]{:T(128)}, f32[128,256]{1,0:T(8,128)S(1)}, ...), condition=%wide.region_21.22_spmd.clone.clone, body=%wide.region_16.21_spmd.clone.clone.sunk | while | flops 4194374 | bytes 3240531 | solution.py:74
  408.6 2.3 fusion.35
  436.4 61.8 %all-reduce.21.cloned.1.call-done = f32[128,256]{1,0:T(8,128)} async-done(((f32[128,256]{1,0:T(8,128)}), f32[128,256]{1,0:T(8,128)}) %all-reduce.21.cloned.1.call-update) | async-done | bytes 131088 | tf_op jit(solution)/shard_map/pmax | solution.py:81
  499.2 103.7 %all-reduce.19.cloned.1.call-done = f32[128,256]{1,0:T(8,128)} async-done(((f32[128,256]{1,0:T(8,128)}), f32[128,256]{1,0:T(8,128)}) %all-reduce.19.cloned.1.call-update) | async-done | bytes 131088 | tf_op jit(solution)/shard_map/pmax | solution.py:80
  603.8 29.1 %while.78 = (s32[]{:T(128)}, f32[128,256]{1,0:T(8,128)S(1)}, f32[128,256]{1,0:T(8,128)S(1)}, s32[]{:T(128)}, s32[48]{0:T(128)}, /*index=5*/s32[]{:T(128)}, f32[4...) while((s32[]{:T(128)}, f32[128,256]{1,0:T(8,128)S(1)}, ...), condition=%wide.region_29.30_spmd.clone.clone, body=%wide.region_24.29_spmd.clone.clone.sunk | while | flops 4194374 | bytes 3240531 | solution.py:74
  634.4 61.7 %all-reduce.25.cloned.1.call-done = f32[128,256]{1,0:T(8,128)} async-done(((f32[128,256]{1,0:T(8,128)}), f32[128,256]{1,0:T(8,128)}) %all-reduce.25.cloned.1.call-update) | async-done | bytes 131088 | tf_op jit(solution)/shard_map/pmax | solution.py:81
  697.0 103.5 %all-reduce.23.cloned.1.call-done = f32[128,256]{1,0:T(8,128)} async-done(((f32[128,256]{1,0:T(8,128)}), f32[128,256]{1,0:T(8,128)}) %all-reduce.23.cloned.1.call-update) | async-done | bytes 131088 | tf_op jit(solution)/shard_map/pmax | solution.py:80
  801.5 26.9 %while.79 = (s32[]{:T(128)}, f32[128,256]{1,0:T(8,128)S(1)}, f32[128,256]{1,0:T(8,128)S(1)}, s32[]{:T(128)}, s32[48]{0:T(128)}, /*index=5*/s32[]{:T(128)}, f32[4...) while((s32[]{:T(128)}, f32[128,256]{1,0:T(8,128)S(1)}, ...), condition=%wide.region_35.36_spmd.clone.clone, body=%wide.region_32.35_spmd.clone.clone.sunk | while | flops 9502790 | bytes 2712147 | solution.py:74
  804.1 2.3 fusion.39
  809.4 2.3 fusion.39
  814.8 2.3 fusion.39
  820.2 2.3 fusion.39
  825.6 2.3 fusion.39
  829.6 103.5 %all-reduce.27.cloned.1.call-done = f32[128,256]{1,0:T(8,128)} async-done(((f32[128,256]{1,0:T(8,128)}), f32[128,256]{1,0:T(8,128)}) %all-reduce.27.cloned.1.call-update) | async-done | bytes 131088 | tf_op jit(solution)/shard_map/psum | solution.py:85
  935.5 57.8 %all-reduce.29.cloned.1.call-done = f32[128,256]{1,0:T(8,128)} async-done(((f32[128,256]{1,0:T(8,128)}), f32[128,256]{1,0:T(8,128)}) %all-reduce.29.cloned.1.call-update) | async-done | bytes 131088 | tf_op jit(solution)/shard_map/psum | solution.py:86
  995.5 10.7 %multiply_select_fusion = f32[1,1,48,256,256]{4,3,2,1,0:T(8,128)} fusion(f32[1,1,48,256,256]{4,3,2,1,0:T(8,128)} %bitcast.25, f32[48,256]{1,0:T(8,128)S(1)} %gather_fusion.11, f32[48,256]{1,0:T(8,128)S(1)} %gather_fusion.10, pred[48]{0:T(512)(128)(4,1)S(1)} %iota_compare_fusion.12), kind=kLoop, calls=%fused_computation.79 | loop fusion | flops 9437184 | bytes 25264176 | tf_op jit(solution)/shard_map/jit(_where)/select_n | solution.py:91
  (367 shorter events, 123.5 us)
Async XLA Ops:
  7.2 138.8 %all-reduce.11.cloned.1.call-start = ((), (), s32[]{:S(2)}) async-start(), calls=%async_computation | async-start | bytes 262144 | tf_op jit(solution)/shard_map/pmax | solution.py:80
  37.2 0.7 copy-start.1
  37.2 0.7 copy-start
  37.8 168.2 %all-reduce.13.cloned.1.call-start = ((), (), s32[]{:S(2)}) async-start(), calls=%async_computation.1 | async-start | bytes 262144 | tf_op jit(solution)/shard_map/pmax | solution.py:81
  38.6 262.1 %all-reduce.17.cloned.1.call-start = ((), (), s32[]{:S(2)}) async-start(), calls=%async_computation.3 | async-start | bytes 262144 | tf_op jit(solution)/shard_map/pmax | solution.py:81
  207.0 93.7 %copy-start.11 = (f32[128,256]{1,0:T(8,128)S(1)}, f32[128,256]{1,0:T(8,128)}, u32[]{:S(2)}) copy-start(f32[128,256]{1,0:T(8,128)} %all-reduce.13.cloned.1.call-done) | copy-start | bytes 393220
  207.0 198.0 %copy-start.10 = (f32[128,256]{1,0:T(8,128)S(1)}, f32[128,256]{1,0:T(8,128)}, u32[]{:S(2)}) copy-start(f32[128,256]{1,0:T(8,128)} %all-reduce.11.cloned.1.call-done) | copy-start | bytes 393220
  236.2 0.7 copy-start.2
  236.2 1.4 copy-start.3
  236.9 168.1 %all-reduce.15.cloned.1.call-start = ((), (), s32[]{:S(2)}) async-start(), calls=%async_computation.2 | async-start | bytes 262144 | tf_op jit(solution)/shard_map/pmax | solution.py:80
  237.7 260.6 %all-reduce.21.cloned.1.call-start = ((), (), s32[]{:S(2)}) async-start(), calls=%async_computation.5 | async-start | bytes 262144 | tf_op jit(solution)/shard_map/pmax | solution.py:81
  435.1 0.7 copy-start.4
  435.1 0.7 copy-start.5
  435.8 167.1 %all-reduce.19.cloned.1.call-start = ((), (), s32[]{:S(2)}) async-start(), calls=%async_computation.4 | async-start | bytes 262144 | tf_op jit(solution)/shard_map/pmax | solution.py:80
  436.4 259.7 %all-reduce.25.cloned.1.call-start = ((), (), s32[]{:S(2)}) async-start(), calls=%async_computation.7 | async-start | bytes 262144 | tf_op jit(solution)/shard_map/pmax | solution.py:81
  632.9 0.7 copy-start.6
  633.0 0.7 copy-start.7
  633.6 166.9 %all-reduce.23.cloned.1.call-start = ((), (), s32[]{:S(2)}) async-start(), calls=%async_computation.6 | async-start | bytes 262144 | tf_op jit(solution)/shard_map/pmax | solution.py:80
  634.4 298.8 %all-reduce.27.cloned.1.call-start = ((), (), s32[]{:S(2)}) async-start(), calls=%async_computation.8 | async-start | bytes 262144 | tf_op jit(solution)/shard_map/psum | solution.py:85
  828.4 0.7 copy-start.9
  828.4 0.7 copy-start.8
  829.1 164.2 %all-reduce.29.cloned.1.call-start = ((), (), s32[]{:S(2)}) async-start(), calls=%async_computation.9 | async-start | bytes 262144 | tf_op jit(solution)/shard_map/psum | solution.py:86
Sparse Core Ops, SparseCore 0:
  38.0 107.9 all-reduce.10
  148.9 57.1 all-reduce.12
  237.0 63.6 all-reduce.16
  304.4 100.5 all-reduce.14
  435.9 62.2 all-reduce.20
  502.2 100.5 all-reduce.18
  633.7 62.3 all-reduce.24
  699.9 100.5 all-reduce.22
  829.2 103.9 all-reduce.26
  936.0 57.1 all-reduce.28
where the time goes:
time: 1020 us; the launch traced here: 1010 us
  waiting for transfers between devices  827 us (81%)
  other arithmetic  132 us (13%)
  local copies, waits for them, and re-layouts  34.2 us (3%)
  between operations  15.1 us (1%)
    pmax x4, waiting for transfers between devices, shards(): row_peak = lax.pmax(row_part, ('col', 'depth'))  417 us
    pmax x4, waiting for transfers between devices, shards(): col_peak = lax.pmax(col_part, ('row', 'depth'))  246 us
    psum x1, waiting for transfers between devices, shards(): row_mass = lax.psum(row_part, ('col', 'depth'))  104 us
    psum x1, waiting for transfers between devices, shards(): col_mass = lax.psum(col_part, ('row', 'depth'))  57.8 us
    reduce_max x20, other arithmetic, step_block(): magnitude.max(axis=1)[None]  46.8 us
  transfers between devices with their start and end apart: 10, of which 10 were waited for; matrix products, arithmetic and copies ran while one was open for 1% of the time, Pallas kernels for 0%

commit v1 on v0

v1 whole, which is shorter than its diff:
```python
import functools

import jax
import jax.numpy as jnp
from jax import lax
from jax.experimental import pallas as pl
from jax.experimental.pallas import tpu as pltpu
from jax.sharding import PartitionSpec as P

BLOCKS = 128
EPS = 1e-06
AXES = ("row", "col", "depth")
GROUP = 4
VMEM_LIMIT = 40 * 1024 * 1024


def scale_row(meta_ref, slots, t):
    return meta_ref[t], meta_ref[slots + t]


def fold(summed):
    return (lambda a, b: a + b) if summed else jnp.maximum


def tile_partials(values, row_vec, col_vec, want_row, want_col, summed):
    join = fold(summed)
    reduce = jnp.sum if summed else jnp.max
    row_halves = []
    col_acc = None
    for h in range(2):
        rows = slice(h * 128, (h + 1) * 128)
        left = jnp.abs(values[rows, 0:128])
        right = jnp.abs(values[rows, 128:256])
        if want_row:
            if col_vec is None:
                part = join(left, right)
            else:
                part = join(left * col_vec[:, 0:128], right * col_vec[:, 128:256])
            row_halves.append(reduce(part.T, axis=0, keepdims=True))
        if want_col:
            if row_vec is not None:
                factor = jnp.broadcast_to(row_vec[:, rows], (128, 128)).T
                left = left * factor
                right = right * factor
            both = [reduce(x.reshape(16, 8, 128), axis=0) for x in (left, right)]
            col_acc = both if col_acc is None else [join(a, b) for a, b in zip(col_acc, both)]
    row_out = jnp.concatenate(row_halves, axis=1) if want_row else None
    col_out = None
    if want_col:
        col_out = jnp.concatenate([reduce(a, axis=0, keepdims=True) for a in col_acc], axis=1)
    return row_out, col_out


def sweep(slots, meta_ref, tiles_ref, row_ref, col_ref, row_acc, col_acc, summed, before=None):
    want_row, want_col = row_acc is not None, col_acc is not None
    join = fold(summed)
    count = meta_ref[2 * slots]
    for acc in (row_acc, col_acc):
        if acc is not None:
            acc[...] = jnp.zeros_like(acc)

    def body(g, carry):
        found = []
        if before is not None:
            for k in range(GROUP):
                before(g * GROUP + k)
        for k in range(GROUP):
            t = g * GROUP + k
            row, col = meta_ref[t], meta_ref[slots + t]
            row_vec = None if row_ref is None else row_ref[pl.ds(row, 1), :]
            col_vec = None if col_ref is None else col_ref[pl.ds(col, 1), :]
            values = tiles_ref.at[t]
            row_out, col_out = tile_partials(values, row_vec, col_vec, want_row, want_col, summed)
            live = t < count
            if want_row:
                row_out = jnp.where(live, row_out, 0.0)
            if want_col:
                col_out = jnp.where(live, col_out, 0.0)
            found.append((row, col, row_out, col_out))
        for row, col, row_out, col_out in found:
            if want_row:
                row_acc[pl.ds(row, 1), :] = join(row_acc[pl.ds(row, 1), :], row_out)
            if want_col:
                col_acc[pl.ds(col, 1), :] = join(col_acc[pl.ds(col, 1), :], col_out)
        return carry

    lax.fori_loop(0, (count + GROUP - 1) // GROUP, body, 0)


def split(core, row_acc, col_acc, mine_ref, other_ref):
    first = core == 0
    mine_ref[...] = jnp.where(first, row_acc[...], col_acc[...])
    other_ref[...] = jnp.where(first, col_acc[...], row_acc[...])


def load_kernel(slots, meta_ref, hbm_ref, tiles_ref, mine_ref, other_ref, row_acc, col_acc, sem):
    count = meta_ref[2 * slots]

    def copy(t):
        return pltpu.make_async_copy(hbm_ref.at[t], tiles_ref.at[t], sem.at[t])

    def start(t, carry):
        copy(t).start()
        return carry

    lax.fori_loop(0, count, start, 0)

    def before(t):
        @pl.when(t < count)
        def _():
            copy(t).wait()

    sweep(slots, meta_ref, tiles_ref, None, None, row_acc, col_acc, False, before)
    split(meta_ref[2 * slots + 1], row_acc, col_acc, mine_ref, other_ref)


def row_kernel(slots, meta_ref, tiles_ref, s_ref, g_ref, part_ref, col_ref):
    first = meta_ref[2 * slots + 1] == 0
    col_ref[...] = jnp.where(first, g_ref[...], s_ref[...])
    sweep(slots, meta_ref, tiles_ref, None, col_ref, part_ref, None, False)


def col_kernel(slots, meta_ref, tiles_ref, s_ref, g_ref, part_ref, row_ref):
    first = meta_ref[2 * slots + 1] == 0
    row_ref[...] = jnp.where(first, s_ref[...], g_ref[...])
    sweep(slots, meta_ref, tiles_ref, row_ref, None, None, part_ref, False)


def both_kernel(
    slots, summed, meta_ref, tiles_ref, s_ref, g_ref, mine_ref, other_ref, row_ref, col_ref, row_acc, col_acc
):
    first = meta_ref[2 * slots + 1] == 0
    col_ref[...] = jnp.where(first, s_ref[...], g_ref[...])
    row_ref[...] = jnp.where(first, g_ref[...], s_ref[...])
    sweep(slots, meta_ref, tiles_ref, row_ref, col_ref, row_acc, col_acc, summed)
    split(meta_ref[2 * slots + 1], row_acc, col_acc, mine_ref, other_ref)


def final_kernel(slots, meta_ref, tiles_ref, row_ref, col_ref, out_ref):
    count = meta_ref[2 * slots]
    base = pl.program_id(0) * GROUP
    for k in range(GROUP):
        t = base + k

        @pl.when(t < count)
        def _():
            row_vec = row_ref[pl.ds(meta_ref[t], 1), :]
            col_vec = col_ref[pl.ds(meta_ref[slots + t], 1), :]
            for h in range(2):
                rows = slice(h * 128, (h + 1) * 128)
                factor = jnp.broadcast_to(row_vec[:, rows], (128, 128)).T
                for w in range(2):
                    cols = slice(w * 128, (w + 1) * 128)
                    out_ref[k, rows, cols] = tiles_ref[t, rows, cols] * factor * col_vec[:, cols]

        @pl.when(t >= count)
        def _():
            out_ref[k] = jnp.zeros(out_ref.shape[1:], jnp.float32)


def shards(sizes, tiles, tile_rows, tile_cols, tile_count):
    zs, xs, ys = sizes
    values = tiles[0, 0]
    slots, size = values.shape[0], values.shape[1]
    core = lax.axis_index("depth")
    is_first = core == 0
    meta = jnp.concatenate(
        [tile_rows[0, 0], tile_cols[0, 0], tile_count[0, 0], core[None].astype(jnp.int32)]
    )

    smem = pl.BlockSpec(memory_space=pltpu.SMEM)
    vmem = pl.BlockSpec(memory_space=pltpu.VMEM)
    params = pltpu.CompilerParams(vmem_limit_bytes=VMEM_LIMIT)
    vec = jax.ShapeDtypeStruct((BLOCKS, size), jnp.float32)
    acc = pltpu.VMEM((BLOCKS, size), jnp.float32)
    kept = pltpu.VMEM((slots, size, size), jnp.float32)

    def spots(move):
        pairs = []
        for z in range(zs):
            for x in range(xs):
                for y in range(ys):
                    for d in range(2):
                        to = move(z, x, y, d)
                        if to is not None:
                            pairs.append((index(z, x, y, d), index(*to)))
        return pairs

    def index(z, x, y, d):
        return ((z % zs * xs + x % xs) * ys + y % ys) * 2 + d

    steps = {
        "x": lambda z, x, y, d, s: (z, x + s, y, d),
        "y": lambda z, x, y, d, s: (z, x, y + s, d),
        "z": lambda z, x, y, d, s: (z + s, x, y, d),
    }

    def slot(v, first_axis, second_axis):
        parts = [v]
        for s in (2, 1, 3):
            def move(z, x, y, d, s=s):
                axis = first_axis if d == 0 else second_axis
                return None if axis is None else steps[axis](z, x, y, d, s)
            parts.append(lax.ppermute(v, AXES, spots(move)))
        return parts

    def top(parts):
        return jnp.maximum(jnp.maximum(parts[0], parts[1]), jnp.maximum(parts[2], parts[3]))

    def total(parts):
        return (parts[0] + parts[1]) + (parts[2] + parts[3])

    def next_factor(old, partial):
        return old * lax.rsqrt(old * partial + EPS)

    swap = lambda v: lax.ppermute(v, "depth", [(0, 1), (1, 0)])
    up = lambda v: lax.ppermute(v, "depth", [(0, 1)])
    down = lambda v: lax.ppermute(v, "depth", [(1, 0)])

    def pick(a, b):
        return jnp.where(is_first, a, b)

    held, mine, other = pl.pallas_call(
        functools.partial(load_kernel, slots),
        out_shape=(kept, vec, vec),
        in_specs=[smem, pl.BlockSpec(memory_space=pl.ANY)],
        out_specs=(vmem, vmem, vmem),
        scratch_shapes=[acc, acc, pltpu.SemaphoreType.DMA((slots,))],
        compiler_params=params,
        name="load",
    )(meta, values)
    held = pltpu.with_memory_space_constraint(held, pltpu.VMEM)

    def call(kernel, outs, scratch, name):
        def run(*args):
            return pl.pallas_call(
                kernel,
                out_shape=(vec,) * outs,
                in_specs=[smem] + [vmem] * (1 + len(args)),
                out_specs=(vmem,) * outs,
                scratch_shapes=[acc] * scratch,
                compiler_params=params,
                name=name,
            )(meta, held, *args)
        return run

    run_row = call(functools.partial(row_kernel, slots), 2, 0, "rows")
    run_col = call(functools.partial(col_kernel, slots), 2, 0, "cols")
    run_both = call(functools.partial(both_kernel, slots, False), 4, 2, "both")
    run_sums = call(functools.partial(both_kernel, slots, True), 4, 2, "sums")

    one = jnp.ones((BLOCKS, size), jnp.float32)
    row_now, col_now = one, one
    m = jnp.maximum(mine, swap(other))
    for pair in range(2):
        u = top(slot(m, "x", "z"))
        s = pick(u, next_factor(col_now, u))
        part, col_now = run_row(s, down(s))
        m = pick(s, jnp.maximum(part, up(part)))
        u = top(slot(m, "y", "x"))
        s = pick(next_factor(row_now, u), u)
        part, row_now = run_col(s, up(s))
        m = pick(jnp.maximum(part, down(part)), s)
        u = top(slot(m, "z", "y"))
        s = next_factor(pick(col_now, row_now), u)
        if pair == 0:
            mine, other, row_now, col_now = run_both(s, swap(s))
            m = jnp.maximum(mine, swap(other))
        else:
            mine, other, row_now, col_now = run_sums(s, swap(s))
            m = mine + swap(other)
    u = total(slot(m, "x", "z"))
    s = pick(u, next_factor(col_now, u))
    col_last = pick(down(s), s)
    u = total(slot(s, "y", None))
    s = next_factor(row_now, u)
    row_last = pick(s, up(s))

    scaled = pl.pallas_call(
        functools.partial(final_kernel, slots),
        out_shape=jax.ShapeDtypeStruct((slots, size, size), jnp.float32),
        grid=(slots // GROUP,),
        in_specs=[smem, vmem, vmem, vmem],
        out_specs=pl.BlockSpec((GROUP, size, size), lambda i: (i, 0, 0)),
        compiler_params=params,
        name="scaled",
    )(meta, held, row_last, col_last)
    return row_last.reshape(-1), col_last.reshape(-1), scaled[None, None]


def solution(mesh):
    zs, cs, ds = (mesh.shape[a] for a in AXES)
    xs = 4
    sizes = (zs, xs, cs // xs)
    in_specs = (
        P("row", "col", "depth", None, None),
        P("row", "col", "depth"),
        P("row", "col", "depth"),
        P("row", "col", "depth"),
    )
    out_specs = (P("row"), P("col"), P("row", "col", "depth", None, None))
    return jax.shard_map(
        functools.partial(shards, sizes), mesh=mesh, in_specs=in_specs, out_specs=out_specs, check_vma=False
    )
```

time: 1020 us -> 157 us (0.15)
  waiting for transfers between devices: 827 us -> 48.1 us
  other arithmetic: 132 us -> 1.33 us
  starting transfers between devices: 0.41 us -> 71.8 us
  local copies, waits for them, and re-layouts: 34.2 us -> 10.8 us
  Pallas kernels: 0 us -> 23.4 us
  between operations: 15.1 us -> 1.56 us
    pmax x8 -> x0, waiting for transfers between devices: 663 us -> none  [the longest x4 417 us: shards(): row_peak = lax.pmax(row_part, ('col', 'depth'))]
    psum x2 -> x0, waiting for transfers between devices: 161 us -> none  [the longest x1 104 us: shards(): row_mass = lax.psum(row_part, ('col', 'depth'))]
    ppermute x0 -> x39, starting transfers between devices: none -> 71.8 us  [the longest x24 36.4 us: slot(): parts.append(lax.ppermute(v, AXES, spots(move)))]
    reduce_max x60 -> x0, other arithmetic: 62 us -> none  [the longest x20 46.8 us: step_block(): magnitude.max(axis=1)[None]]
    ppermute x0 -> x39, waiting for transfers between devices: none -> 48.1 us  [the longest x24 22.1 us: slot(): parts.append(lax.ppermute(v, AXES, spots(move)))]
    select_n x28 -> x11, other arithmetic: 30.9 us -> 0.41 us  [pick(): return jnp.where(is_first, a, b)]
    gather x52 -> x0, local copies, waits for them, and re-layouts: 29.4 us -> none  [the longest x25 14.1 us: step_block(): col_now[block_cols][:, None, :]]
    pallas_call x0 -> x8, Pallas kernels: none -> 23.4 us  [the longest x6 11.6 us: run(): pl.pallas_call(kernel, out_shape=(vec,) * outs, in_specs=[smem] + [vmem]...]
  transfers between devices with their start and end apart: 10 -> 39, of which waited for: 10 -> 30; matrix products, arithmetic and copies ran while one was open for 1% -> 0% of each run, Pallas kernels for 0% -> 0%
where the time goes in v1:
time: 157 us
  starting transfers between devices  71.8 us (46%)
  waiting for transfers between devices  48.1 us (31%)
  Pallas kernels  23.4 us (15%)
  local copies, waits for them, and re-layouts  10.8 us (7%)
    ppermute x24, starting transfers between devices, slot(): parts.append(lax.ppermute(v, AXES, spots(move)))  36.4 us
    ppermute x5, starting transfers between devices, shards(): down = lambda v: lax.ppermute(v, 'depth', [(1, 0)])  25 us
    ppermute x24, waiting for transfers between devices, slot(): parts.append(lax.ppermute(v, AXES, spots(move)))  22.1 us
    ppermute x5, waiting for transfers between devices, shards(): up = lambda v: lax.ppermute(v, 'depth', [(0, 1)])  15.6 us
    pallas_call x6, Pallas kernels, run(): pl.pallas_call(kernel, out_shape=(vec,) * outs, in_specs=[smem] + [vmem]...  11.6 us
    unnamed x6, local copies, waits for them, and re-layouts  10.8 us
    pallas_call x1, Pallas kernels, shards(): pl.pallas_call(functools.partial(final_kernel, slots), out_shape=jax.Shap...  8.19 us
    ppermute x5, starting transfers between devices, shards(): up = lambda v: lax.ppermute(v, 'depth', [(0, 1)])  6.46 us
  transfers between devices with their start and end apart: 39, of which 30 were waited for; matrix products, arithmetic and copies ran while one was open for 0% of the time, Pallas kernels for 0%

profile of v1, /device:TPU:1, one launch (start us, length us, event | category | flops | bytes accessed | tf_op | source)
XLA Modules:
  0.0 156.9 jit_solution(11615910897382620632)
XLA Ops:
  2.0 3.6 %load.1 = (f32[48,256,256]{2,1,0:T(8,128)S(1)}, f32[128,256]{1,0:T(8,128)S(1)}, f32[128,256]{1,0:T(8,128)S(1)}) custom-call(s32[98]{0:T(128)S(1)} %pad_add_fusion.meta_ref, f32[48,256,256]{2,1,0:T(8,128)} %bitcast.13), custom_call_target="tpu_custom_call" | custom-call | tf_op jit(solution)/shard_map/load/pallas_call | solution.py:223
  5.7 4.8 %copy-done = f32[48,256,256]{2,1,0:T(8,128)} copy-done((f32[48,256,256]{2,1,0:T(8,128)}, f32[48,256,256]{2,1,0:T(8,128)S(1)}, u32[]{:S(2)}) %copy-start) | copy-done | bytes 12582936
  12.6 4.6 %collective-permute-start.1 = (f32[128,256]{1,0:T(8,128)S(1)}, f32[128,256]{1,0:T(8,128)S(1)}, u32[]{:S(2)}, u32[]{:S(2)}) collective-permute-start(f32[128,256]{1,0:T(8,128)S(1)} %max.72), channel_id=1, source_target_pairs={{0,16},{1,65},{2,18},{3,67},{4,20},{5,69},{6,22},{7,71},{8,24},{9,... | collective-permute-start | bytes 393224 | tf_op jit(solution)/shard_map/ppermute | solution.py:204
  17.7 2.2 %collective-permute-start.3 = (f32[128,256]{1,0:T(8,128)S(1)}, f32[128,256]{1,0:T(8,128)S(1)}, u32[]{:S(2)}, u32[]{:S(2)}) collective-permute-start(f32[128,256]{1,0:T(8,128)S(1)} %max.72), channel_id=1, source_target_pairs={{0,24},{1,97},{2,26},{3,99},{4,28},{5,101},{6,30},{7,103},{8,0},{9... | collective-permute-start | bytes 393224 | tf_op jit(solution)/shard_map/ppermute | solution.py:204
  19.9 2.3 %collective-permute-done.2 = f32[128,256]{1,0:T(8,128)S(1)} collective-permute-done((f32[128,256]{1,0:T(8,128)S(1)}, f32[128,256]{1,0:T(8,128)S(1)}, u32[]{:S(2)}, u32[]{:S(2)}) %collective-permute-start.2) | collective-permute-done | bytes 131104 | tf_op jit(solution)/shard_map/ppermute | solution.py:204
  22.3 2.0 %collective-permute-start.4 = (f32[128,256]{1,0:T(8,128)S(1)}, f32[128,256]{1,0:T(8,128)S(1)}, u32[]{:S(2)}, u32[]{:S(2)}) collective-permute-start(f32[128,256]{1,0:T(8,128)S(1)} %rsqrt_select_fusion.1.s_ref), channel_id=1, source_target_pairs={{1,0},{3,2},{5,4},{7,6},{9,8},{11,10},{13,12},{15,14},{17,16},{19,... | collective-permute-start | bytes 393224 | tf_op jit(solution)/shard_map/ppermute | solution.py:218
  25.3 4.6 %copy-done.1 = f32[48,256,256]{2,1,0:T(8,128)S(1)} copy-done((f32[48,256,256]{2,1,0:T(8,128)S(1)}, f32[48,256,256]{2,1,0:T(8,128)}, u32[]{:S(2)}) %copy-start.1) | copy-done | bytes 12582936
  29.9 1.7 %rows.2 = (f32[128,256]{1,0:T(8,128)S(1)}, f32[128,256]{1,0:T(8,128)S(1)}) custom-call(s32[98]{0:T(128)S(1)} %pad_add_fusion.meta_ref, f32[48,256,256]{2,1,0:T(8,128)S(1)} %copy-done.1, f32[128,256]{1,0:T(8,128)S(1)} %rsqrt_select_fusion.1.s_ref, f32[128,256]{1,0:T(8,128)S(1)} %collective-permute-done.4.g_ref), custom_call_target="tpu_custom_call" | custom-call | tf_op jit(solution)/shard_map/rows/pallas_call | solution.py:236
  32.8 1.9 %collective-permute-done.5 = f32[128,256]{1,0:T(8,128)S(1)} collective-permute-done((f32[128,256]{1,0:T(8,128)S(1)}, f32[128,256]{1,0:T(8,128)S(1)}, u32[]{:S(2)}, u32[]{:S(2)}) %collective-permute-start.5) | collective-permute-done | bytes 131104 | tf_op jit(solution)/shard_map/ppermute | solution.py:217
  34.8 2.2 %collective-permute-start.6 = (f32[128,256]{1,0:T(8,128)S(1)}, f32[128,256]{1,0:T(8,128)S(1)}, u32[]{:S(2)}, u32[]{:S(2)}) collective-permute-start(f32[128,256]{1,0:T(8,128)S(1)} %maximum_select_fusion.3), channel_id=1, source_target_pairs={{0,4},{1,17},{2,6},{3,19},{4,0},{5,21},{6,2},{7,23},{8,12},{9,25},... | collective-permute-start | bytes 393224 | tf_op jit(solution)/shard_map/ppermute | solution.py:204
  40.2 2.1 %collective-permute-done.7 = f32[128,256]{1,0:T(8,128)S(1)} collective-permute-done((f32[128,256]{1,0:T(8,128)S(1)}, f32[128,256]{1,0:T(8,128)S(1)}, u32[]{:S(2)}, u32[]{:S(2)}) %collective-permute-start.7) | collective-permute-done | bytes 131104 | tf_op jit(solution)/shard_map/ppermute | solution.py:204
  43.7 4.7 %collective-permute-done.9.g_ref = f32[128,256]{1,0:T(8,128)S(1)} collective-permute-done((f32[128,256]{1,0:T(8,128)S(1)}, f32[128,256]{1,0:T(8,128)S(1)}, u32[]{:S(2)}, u32[]{:S(2)}) %collective-permute-start.9) | collective-permute-done | bytes 131104 | tf_op jit(solution)/shard_map/ppermute | solution.py:217
  48.4 1.7 %cols.2 = (f32[128,256]{1,0:T(8,128)S(1)}, f32[128,256]{1,0:T(8,128)S(1)}) custom-call(s32[98]{0:T(128)S(1)} %pad_add_fusion.meta_ref, f32[48,256,256]{2,1,0:T(8,128)S(1)} %copy-done.1, f32[128,256]{1,0:T(8,128)S(1)} %rsqrt_select_fusion.s_ref, f32[128,256]{1,0:T(8,128)S(1)} %collective-permute-done.9.g_ref), custom_call_target="tpu_custom_call" | custom-call | tf_op jit(solution)/shard_map/cols/pallas_call | solution.py:236
  50.1 1.8 %collective-permute-start.10 = (f32[128,256]{1,0:T(8,128)S(1)}, f32[128,256]{1,0:T(8,128)S(1)}, u32[]{:S(2)}, u32[]{:S(2)}) collective-permute-start(f32[128,256]{1,0:T(8,128)S(1)} %get-tuple-element.28), channel_id=1, source_target_pairs={{1,0},{3,2},{5,4},{7,6},{9,8},{11,10},{13,12},{15,14},{17,16},{19,... | collective-permute-start | bytes 393224 | tf_op jit(solution)/shard_map/ppermute | solution.py:218
  52.9 2.1 %collective-permute-start.11 = (f32[128,256]{1,0:T(8,128)S(1)}, f32[128,256]{1,0:T(8,128)S(1)}, u32[]{:S(2)}, u32[]{:S(2)}) collective-permute-start(f32[128,256]{1,0:T(8,128)S(1)} %maximum_select_fusion.2), channel_id=1, source_target_pairs={{0,64},{1,5},{2,66},{3,7},{4,68},{5,1},{6,70},{7,3},{8,72},{9,13},... | collective-permute-start | bytes 393224 | tf_op jit(solution)/shard_map/ppermute | solution.py:204
  55.0 3.2 %collective-permute-start.12 = (f32[128,256]{1,0:T(8,128)S(1)}, f32[128,256]{1,0:T(8,128)S(1)}, u32[]{:S(2)}, u32[]{:S(2)}) collective-permute-start(f32[128,256]{1,0:T(8,128)S(1)} %maximum_select_fusion.2), channel_id=1, source_target_pairs={{0,32},{1,3},{2,34},{3,5},{4,36},{5,7},{6,38},{7,1},{8,40},{9,11},... | collective-permute-start | bytes 393224 | tf_op jit(solution)/shard_map/ppermute | solution.py:204
  60.2 2.2 %collective-permute-done.13 = f32[128,256]{1,0:T(8,128)S(1)} collective-permute-done((f32[128,256]{1,0:T(8,128)S(1)}, f32[128,256]{1,0:T(8,128)S(1)}, u32[]{:S(2)}, u32[]{:S(2)}) %collective-permute-start.13) | collective-permute-done | bytes 131104 | tf_op jit(solution)/shard_map/ppermute | solution.py:204
  62.4 1.8 %collective-permute-start.14 = (f32[128,256]{1,0:T(8,128)S(1)}, f32[128,256]{1,0:T(8,128)S(1)}, u32[]{:S(2)}, u32[]{:S(2)}) collective-permute-start(f32[128,256]{1,0:T(8,128)S(1)} %rsqrt_multiply_fusion.2.s_ref), channel_id=1, source_target_pairs={{0,1},{1,0},{2,3},{3,2},{4,5},{5,4},{6,7},{7,6},{8,9},{9,8},{10,11... | collective-permute-start | bytes 393224 | tf_op jit(solution)/shard_map/ppermute | solution.py:216
  65.2 2.5 %both.1 = (f32[128,256]{1,0:T(8,128)S(1)}, f32[128,256]{1,0:T(8,128)S(1)}, f32[128,256]{1,0:T(8,128)S(1)}, f32[128,256]{1,0:T(8,128)S(1)}) custom-call(s32[98]{0:T(128)S(1)} %pad_add_fusion.meta_ref, f32[48,256,256]{2,1,0:T(8,128)S(1)} %copy-done.1, f32[128,256]{1,0:T(8,128)S(1)} %rsqrt_multiply_fusion.2.s_ref, f32[128,256]{1,0:T(8,128)S(1)} %collective-permute-done.14.g_ref), custom_call_target="tpu_custom_call" | custom-call | tf_op jit(solution)/shard_map/both/pallas_call | solution.py:236
  69.2 2.0 %collective-permute-start.16 = (f32[128,256]{1,0:T(8,128)S(1)}, f32[128,256]{1,0:T(8,128)S(1)}, u32[]{:S(2)}, u32[]{:S(2)}) collective-permute-start(f32[128,256]{1,0:T(8,128)S(1)} %max.84), channel_id=1, source_target_pairs={{0,16},{1,65},{2,18},{3,67},{4,20},{5,69},{6,22},{7,71},{8,24},{9,... | collective-permute-start | bytes 393224 | tf_op jit(solution)/shard_map/ppermute | solution.py:204
  72.0 1.8 %collective-permute-start.18 = (f32[128,256]{1,0:T(8,128)S(1)}, f32[128,256]{1,0:T(8,128)S(1)}, u32[]{:S(2)}, u32[]{:S(2)}) collective-permute-start(f32[128,256]{1,0:T(8,128)S(1)} %max.84), channel_id=1, source_target_pairs={{0,24},{1,97},{2,26},{3,99},{4,28},{5,101},{6,30},{7,103},{8,0},{9... | collective-permute-start | bytes 393224 | tf_op jit(solution)/shard_map/ppermute | solution.py:204
  76.5 4.0 %collective-permute-start.19 = (f32[128,256]{1,0:T(8,128)S(1)}, f32[128,256]{1,0:T(8,128)S(1)}, u32[]{:S(2)}, u32[]{:S(2)}) collective-permute-start(f32[128,256]{1,0:T(8,128)S(1)} %multiply_select_fusion.2.s_ref), channel_id=1, source_target_pairs={{1,0},{3,2},{5,4},{7,6},{9,8},{11,10},{13,12},{15,14},{17,16},{19,... | collective-permute-start | bytes 393224 | tf_op jit(solution)/shard_map/ppermute | solution.py:218
  81.5 1.7 %rows.3 = (f32[128,256]{1,0:T(8,128)S(1)}, f32[128,256]{1,0:T(8,128)S(1)}) custom-call(s32[98]{0:T(128)S(1)} %pad_add_fusion.meta_ref, f32[48,256,256]{2,1,0:T(8,128)S(1)} %copy-done.1, f32[128,256]{1,0:T(8,128)S(1)} %multiply_select_fusion.2.s_ref, f32[128,256]{1,0:T(8,128)S(1)} %collective-permute-done.19.g_ref), custom_call_target="tpu_custom_call" | custom-call | tf_op jit(solution)/shard_map/rows/pallas_call | solution.py:236
  84.5 1.9 %collective-permute-done.20 = f32[128,256]{1,0:T(8,128)S(1)} collective-permute-done((f32[128,256]{1,0:T(8,128)S(1)}, f32[128,256]{1,0:T(8,128)S(1)}, u32[]{:S(2)}, u32[]{:S(2)}) %collective-permute-start.20) | collective-permute-done | bytes 131104 | tf_op jit(solution)/shard_map/ppermute | solution.py:217
  87.5 1.8 %collective-permute-start.22 = (f32[128,256]{1,0:T(8,128)S(1)}, f32[128,256]{1,0:T(8,128)S(1)}, u32[]{:S(2)}, u32[]{:S(2)}) collective-permute-start(f32[128,256]{1,0:T(8,128)S(1)} %maximum_select_fusion.1), channel_id=1, source_target_pairs={{0,2},{1,9},{2,4},{3,11},{4,6},{5,13},{6,0},{7,15},{8,10},{9,17},{... | collective-permute-start | bytes 393224 | tf_op jit(solution)/shard_map/ppermute | solution.py:204
  90.1 2.0 %collective-permute-done.21 = f32[128,256]{1,0:T(8,128)S(1)} collective-permute-done((f32[128,256]{1,0:T(8,128)S(1)}, f32[128,256]{1,0:T(8,128)S(1)}, u32[]{:S(2)}, u32[]{:S(2)}) %collective-permute-start.21) | collective-permute-done | bytes 131104 | tf_op jit(solution)/shard_map/ppermute | solution.py:204
  94.9 5.8 %collective-permute-done.24.g_ref = f32[128,256]{1,0:T(8,128)S(1)} collective-permute-done((f32[128,256]{1,0:T(8,128)S(1)}, f32[128,256]{1,0:T(8,128)S(1)}, u32[]{:S(2)}, u32[]{:S(2)}) %collective-permute-start.24) | collective-permute-done | bytes 131104 | tf_op jit(solution)/shard_map/ppermute | solution.py:217
  102.3 1.8 %collective-permute-start.25 = (f32[128,256]{1,0:T(8,128)S(1)}, f32[128,256]{1,0:T(8,128)S(1)}, u32[]{:S(2)}, u32[]{:S(2)}) collective-permute-start(f32[128,256]{1,0:T(8,128)S(1)} %get-tuple-element.36), channel_id=1, source_target_pairs={{1,0},{3,2},{5,4},{7,6},{9,8},{11,10},{13,12},{15,14},{17,16},{19,... | collective-permute-start | bytes 393224 | tf_op jit(solution)/shard_map/ppermute | solution.py:218
  105.9 3.5 %collective-permute-start.27 = (f32[128,256]{1,0:T(8,128)S(1)}, f32[128,256]{1,0:T(8,128)S(1)}, u32[]{:S(2)}, u32[]{:S(2)}) collective-permute-start(f32[128,256]{1,0:T(8,128)S(1)} %maximum_select_fusion), channel_id=1, source_target_pairs={{0,32},{1,3},{2,34},{3,5},{4,36},{5,7},{6,38},{7,1},{8,40},{9,11},... | collective-permute-start | bytes 393224 | tf_op jit(solution)/shard_map/ppermute | solution.py:204
  115.3 2.4 %sums.1 = (f32[128,256]{1,0:T(8,128)S(1)}, f32[128,256]{1,0:T(8,128)S(1)}, f32[128,256]{1,0:T(8,128)S(1)}, f32[128,256]{1,0:T(8,128)S(1)}) custom-call(s32[98]{0:T(128)S(1)} %pad_add_fusion.meta_ref, f32[48,256,256]{2,1,0:T(8,128)S(1)} %copy-done.1, f32[128,256]{1,0:T(8,128)S(1)} %rsqrt_multiply_fusion.1.s_ref, f32[128,256]{1,0:T(8,128)S(1)} %collective-permute-done.29.g_ref), custom_call_target="tpu_custom_call" | custom-call | tf_op jit(solution)/shard_map/sums/pallas_call | solution.py:236
  128.4 15.3 %collective-permute-start.38 = (f32[128,256]{1,0:T(8,128)S(1)}, f32[128,256]{1,0:T(8,128)S(1)}, u32[]{:S(2)}, u32[]{:S(2)}) collective-permute-start(f32[128,256]{1,0:T(8,128)S(1)} %multiply_select_fusion), channel_id=1, source_target_pairs={{1,0},{3,2},{5,4},{7,6},{9,8},{11,10},{13,12},{15,14},{17,16},{19,... | collective-permute-start | bytes 393224 | tf_op jit(solution)/shard_map/ppermute | solution.py:218
  148.0 8.2 %scaled.1 = f32[48,256,256]{2,1,0:T(8,128)} custom-call(s32[98]{0:T(128)S(1)} %pad_add_fusion.meta_ref, f32[48,256,256]{2,1,0:T(8,128)S(1)} %copy-done.1, f32[128,256]{1,0:T(8,128)S(1)} %broadcast_select_fusion.1.row_ref, f32[128,256]{1,0:T(8,128)S(1)} %get-tuple-element.41.col_ref), custom_call_target="tpu_custom_call" | custom-call | tf_op jit(solution)/shard_map/scaled/pallas_call | solution.py:279
  (77 shorter events, 50.9 us)
Async XLA Ops:
  12.6 7.3 %collective-permute-start.1 = (f32[128,256]{1,0:T(8,128)S(1)}, f32[128,256]{1,0:T(8,128)S(1)}, u32[]{:S(2)}, u32[]{:S(2)}) collective-permute-start(f32[128,256]{1,0:T(8,128)S(1)} %max.72), channel_id=1, source_target_pairs={{0,16},{1,65},{2,18},{3,67},{4,20},{5,69},{6,22},{7,71},{8,24},{9,... | collective-permute-start | bytes 393224 | tf_op jit(solution)/shard_map/ppermute | solution.py:204
  17.3 5.0 %collective-permute-start.2 = (f32[128,256]{1,0:T(8,128)S(1)}, f32[128,256]{1,0:T(8,128)S(1)}, u32[]{:S(2)}, u32[]{:S(2)}) collective-permute-start(f32[128,256]{1,0:T(8,128)S(1)} %max.72), channel_id=1, source_target_pairs={{0,8},{1,33},{2,10},{3,35},{4,12},{5,37},{6,14},{7,39},{8,16},{9,4... | collective-permute-start | bytes 393224 | tf_op jit(solution)/shard_map/ppermute | solution.py:204
  17.7 4.6 %collective-permute-start.3 = (f32[128,256]{1,0:T(8,128)S(1)}, f32[128,256]{1,0:T(8,128)S(1)}, u32[]{:S(2)}, u32[]{:S(2)}) collective-permute-start(f32[128,256]{1,0:T(8,128)S(1)} %max.72), channel_id=1, source_target_pairs={{0,24},{1,97},{2,26},{3,99},{4,28},{5,101},{6,30},{7,103},{8,0},{9... | collective-permute-start | bytes 393224 | tf_op jit(solution)/shard_map/ppermute | solution.py:204
  22.3 3.0 %collective-permute-start.4 = (f32[128,256]{1,0:T(8,128)S(1)}, f32[128,256]{1,0:T(8,128)S(1)}, u32[]{:S(2)}, u32[]{:S(2)}) collective-permute-start(f32[128,256]{1,0:T(8,128)S(1)} %rsqrt_select_fusion.1.s_ref), channel_id=1, source_target_pairs={{1,0},{3,2},{5,4},{7,6},{9,8},{11,10},{13,12},{15,14},{17,16},{19,... | collective-permute-start | bytes 393224 | tf_op jit(solution)/shard_map/ppermute | solution.py:218
  31.5 3.2 %collective-permute-start.5 = (f32[128,256]{1,0:T(8,128)S(1)}, f32[128,256]{1,0:T(8,128)S(1)}, u32[]{:S(2)}, u32[]{:S(2)}) collective-permute-start(f32[128,256]{1,0:T(8,128)S(1)} %get-tuple-element.26), channel_id=1, source_target_pairs={{0,1},{2,3},{4,5},{6,7},{8,9},{10,11},{12,13},{14,15},{16,17},{18,... | collective-permute-start | bytes 393224 | tf_op jit(solution)/shard_map/ppermute | solution.py:217
  34.8 5.4 %collective-permute-start.6 = (f32[128,256]{1,0:T(8,128)S(1)}, f32[128,256]{1,0:T(8,128)S(1)}, u32[]{:S(2)}, u32[]{:S(2)}) collective-permute-start(f32[128,256]{1,0:T(8,128)S(1)} %maximum_select_fusion.3), channel_id=1, source_target_pairs={{0,4},{1,17},{2,6},{3,19},{4,0},{5,21},{6,2},{7,23},{8,12},{9,25},... | collective-permute-start | bytes 393224 | tf_op jit(solution)/shard_map/ppermute | solution.py:204
  37.0 5.3 %collective-permute-start.7 = (f32[128,256]{1,0:T(8,128)S(1)}, f32[128,256]{1,0:T(8,128)S(1)}, u32[]{:S(2)}, u32[]{:S(2)}) collective-permute-start(f32[128,256]{1,0:T(8,128)S(1)} %maximum_select_fusion.3), channel_id=1, source_target_pairs={{0,2},{1,9},{2,4},{3,11},{4,6},{5,13},{6,0},{7,15},{8,10},{9,17},{... | collective-permute-start | bytes 393224 | tf_op jit(solution)/shard_map/ppermute | solution.py:204
  38.2 4.2 %collective-permute-start.8 = (f32[128,256]{1,0:T(8,128)S(1)}, f32[128,256]{1,0:T(8,128)S(1)}, u32[]{:S(2)}, u32[]{:S(2)}) collective-permute-start(f32[128,256]{1,0:T(8,128)S(1)} %maximum_select_fusion.3), channel_id=1, source_target_pairs={{0,6},{1,25},{2,0},{3,27},{4,2},{5,29},{6,4},{7,31},{8,14},{9,1},{... | collective-permute-start | bytes 393224 | tf_op jit(solution)/shard_map/ppermute | solution.py:204
  42.4 6.0 %collective-permute-start.9 = (f32[128,256]{1,0:T(8,128)S(1)}, f32[128,256]{1,0:T(8,128)S(1)}, u32[]{:S(2)}, u32[]{:S(2)}) collective-permute-start(f32[128,256]{1,0:T(8,128)S(1)} %rsqrt_select_fusion.s_ref), channel_id=1, source_target_pairs={{0,1},{2,3},{4,5},{6,7},{8,9},{10,11},{12,13},{14,15},{16,17},{18,... | collective-permute-start | bytes 393224 | tf_op jit(solution)/shard_map/ppermute | solution.py:217
  52.9 5.7 %collective-permute-start.11 = (f32[128,256]{1,0:T(8,128)S(1)}, f32[128,256]{1,0:T(8,128)S(1)}, u32[]{:S(2)}, u32[]{:S(2)}) collective-permute-start(f32[128,256]{1,0:T(8,128)S(1)} %maximum_select_fusion.2), channel_id=1, source_target_pairs={{0,64},{1,5},{2,66},{3,7},{4,68},{5,1},{6,70},{7,3},{8,72},{9,13},... | collective-permute-start | bytes 393224 | tf_op jit(solution)/shard_map/ppermute | solution.py:204
  55.0 5.2 %collective-permute-start.12 = (f32[128,256]{1,0:T(8,128)S(1)}, f32[128,256]{1,0:T(8,128)S(1)}, u32[]{:S(2)}, u32[]{:S(2)}) collective-permute-start(f32[128,256]{1,0:T(8,128)S(1)} %maximum_select_fusion.2), channel_id=1, source_target_pairs={{0,32},{1,3},{2,34},{3,5},{4,36},{5,7},{6,38},{7,1},{8,40},{9,11},... | collective-permute-start | bytes 393224 | tf_op jit(solution)/shard_map/ppermute | solution.py:204
  58.2 4.1 %collective-permute-start.13 = (f32[128,256]{1,0:T(8,128)S(1)}, f32[128,256]{1,0:T(8,128)S(1)}, u32[]{:S(2)}, u32[]{:S(2)}) collective-permute-start(f32[128,256]{1,0:T(8,128)S(1)} %maximum_select_fusion.2), channel_id=1, source_target_pairs={{0,96},{1,7},{2,98},{3,1},{4,100},{5,3},{6,102},{7,5},{8,104},{9,1... | collective-permute-start | bytes 393224 | tf_op jit(solution)/shard_map/ppermute | solution.py:204
  69.2 5.7 %collective-permute-start.16 = (f32[128,256]{1,0:T(8,128)S(1)}, f32[128,256]{1,0:T(8,128)S(1)}, u32[]{:S(2)}, u32[]{:S(2)}) collective-permute-start(f32[128,256]{1,0:T(8,128)S(1)} %max.84), channel_id=1, source_target_pairs={{0,16},{1,65},{2,18},{3,67},{4,20},{5,69},{6,22},{7,71},{8,24},{9,... | collective-permute-start | bytes 393224 | tf_op jit(solution)/shard_map/ppermute | solution.py:204
  71.2 5.3 %collective-permute-start.17 = (f32[128,256]{1,0:T(8,128)S(1)}, f32[128,256]{1,0:T(8,128)S(1)}, u32[]{:S(2)}, u32[]{:S(2)}) collective-permute-start(f32[128,256]{1,0:T(8,128)S(1)} %max.84), channel_id=1, source_target_pairs={{0,8},{1,33},{2,10},{3,35},{4,12},{5,37},{6,14},{7,39},{8,16},{9,4... | collective-permute-start | bytes 393224 | tf_op jit(solution)/shard_map/ppermute | solution.py:204
  72.0 4.5 %collective-permute-start.18 = (f32[128,256]{1,0:T(8,128)S(1)}, f32[128,256]{1,0:T(8,128)S(1)}, u32[]{:S(2)}, u32[]{:S(2)}) collective-permute-start(f32[128,256]{1,0:T(8,128)S(1)} %max.84), channel_id=1, source_target_pairs={{0,24},{1,97},{2,26},{3,99},{4,28},{5,101},{6,30},{7,103},{8,0},{9... | collective-permute-start | bytes 393224 | tf_op jit(solution)/shard_map/ppermute | solution.py:204
  76.5 4.9 %collective-permute-start.19 = (f32[128,256]{1,0:T(8,128)S(1)}, f32[128,256]{1,0:T(8,128)S(1)}, u32[]{:S(2)}, u32[]{:S(2)}) collective-permute-start(f32[128,256]{1,0:T(8,128)S(1)} %multiply_select_fusion.2.s_ref), channel_id=1, source_target_pairs={{1,0},{3,2},{5,4},{7,6},{9,8},{11,10},{13,12},{15,14},{17,16},{19,... | collective-permute-start | bytes 393224 | tf_op jit(solution)/shard_map/ppermute | solution.py:218
  83.2 3.2 %collective-permute-start.20 = (f32[128,256]{1,0:T(8,128)S(1)}, f32[128,256]{1,0:T(8,128)S(1)}, u32[]{:S(2)}, u32[]{:S(2)}) collective-permute-start(f32[128,256]{1,0:T(8,128)S(1)} %get-tuple-element.34), channel_id=1, source_target_pairs={{0,1},{2,3},{4,5},{6,7},{8,9},{10,11},{12,13},{14,15},{16,17},{18,... | collective-permute-start | bytes 393224 | tf_op jit(solution)/shard_map/ppermute | solution.py:217
  86.4 5.7 %collective-permute-start.21 = (f32[128,256]{1,0:T(8,128)S(1)}, f32[128,256]{1,0:T(8,128)S(1)}, u32[]{:S(2)}, u32[]{:S(2)}) collective-permute-start(f32[128,256]{1,0:T(8,128)S(1)} %maximum_select_fusion.1), channel_id=1, source_target_pairs={{0,4},{1,17},{2,6},{3,19},{4,0},{5,21},{6,2},{7,23},{8,12},{9,25},... | collective-permute-start | bytes 393224 | tf_op jit(solution)/shard_map/ppermute | solution.py:204
  87.5 6.0 %collective-permute-start.22 = (f32[128,256]{1,0:T(8,128)S(1)}, f32[128,256]{1,0:T(8,128)S(1)}, u32[]{:S(2)}, u32[]{:S(2)}) collective-permute-start(f32[128,256]{1,0:T(8,128)S(1)} %maximum_select_fusion.1), channel_id=1, source_target_pairs={{0,2},{1,9},{2,4},{3,11},{4,6},{5,13},{6,0},{7,15},{8,10},{9,17},{... | collective-permute-start | bytes 393224 | tf_op jit(solution)/shard_map/ppermute | solution.py:204
  89.2 4.2 %collective-permute-start.23 = (f32[128,256]{1,0:T(8,128)S(1)}, f32[128,256]{1,0:T(8,128)S(1)}, u32[]{:S(2)}, u32[]{:S(2)}) collective-permute-start(f32[128,256]{1,0:T(8,128)S(1)} %maximum_select_fusion.1), channel_id=1, source_target_pairs={{0,6},{1,25},{2,0},{3,27},{4,2},{5,29},{6,4},{7,31},{8,14},{9,1},{... | collective-permute-start | bytes 393224 | tf_op jit(solution)/shard_map/ppermute | solution.py:204
  93.6 7.1 %collective-permute-start.24 = (f32[128,256]{1,0:T(8,128)S(1)}, f32[128,256]{1,0:T(8,128)S(1)}, u32[]{:S(2)}, u32[]{:S(2)}) collective-permute-start(f32[128,256]{1,0:T(8,128)S(1)} %multiply_select_fusion.1.s_ref), channel_id=1, source_target_pairs={{0,1},{2,3},{4,5},{6,7},{8,9},{10,11},{12,13},{14,15},{16,17},{18,... | collective-permute-start | bytes 393224 | tf_op jit(solution)/shard_map/ppermute | solution.py:217
  105.1 5.7 %collective-permute-start.26 = (f32[128,256]{1,0:T(8,128)S(1)}, f32[128,256]{1,0:T(8,128)S(1)}, u32[]{:S(2)}, u32[]{:S(2)}) collective-permute-start(f32[128,256]{1,0:T(8,128)S(1)} %maximum_select_fusion), channel_id=1, source_target_pairs={{0,64},{1,5},{2,66},{3,7},{4,68},{5,1},{6,70},{7,3},{8,72},{9,13},... | collective-permute-start | bytes 393224 | tf_op jit(solution)/shard_map/ppermute | solution.py:204
  105.9 6.4 %collective-permute-start.27 = (f32[128,256]{1,0:T(8,128)S(1)}, f32[128,256]{1,0:T(8,128)S(1)}, u32[]{:S(2)}, u32[]{:S(2)}) collective-permute-start(f32[128,256]{1,0:T(8,128)S(1)} %maximum_select_fusion), channel_id=1, source_target_pairs={{0,32},{1,3},{2,34},{3,5},{4,36},{5,7},{6,38},{7,1},{8,40},{9,11},... | collective-permute-start | bytes 393224 | tf_op jit(solution)/shard_map/ppermute | solution.py:204
  109.4 4.1 %collective-permute-start.28 = (f32[128,256]{1,0:T(8,128)S(1)}, f32[128,256]{1,0:T(8,128)S(1)}, u32[]{:S(2)}, u32[]{:S(2)}) collective-permute-start(f32[128,256]{1,0:T(8,128)S(1)} %maximum_select_fusion), channel_id=1, source_target_pairs={{0,96},{1,7},{2,98},{3,1},{4,100},{5,3},{6,102},{7,5},{8,104},{9,1... | collective-permute-start | bytes 393224 | tf_op jit(solution)/shard_map/ppermute | solution.py:204
  119.2 5.7 %collective-permute-start.31 = (f32[128,256]{1,0:T(8,128)S(1)}, f32[128,256]{1,0:T(8,128)S(1)}, u32[]{:S(2)}, u32[]{:S(2)}) collective-permute-start(f32[128,256]{1,0:T(8,128)S(1)} %add.51), channel_id=1, source_target_pairs={{0,16},{1,65},{2,18},{3,67},{4,20},{5,69},{6,22},{7,71},{8,24},{9,... | collective-permute-start | bytes 393224 | tf_op jit(solution)/shard_map/ppermute | solution.py:204
  120.8 5.5 %collective-permute-start.32 = (f32[128,256]{1,0:T(8,128)S(1)}, f32[128,256]{1,0:T(8,128)S(1)}, u32[]{:S(2)}, u32[]{:S(2)}) collective-permute-start(f32[128,256]{1,0:T(8,128)S(1)} %add.51), channel_id=1, source_target_pairs={{0,8},{1,33},{2,10},{3,35},{4,12},{5,37},{6,14},{7,39},{8,16},{9,4... | collective-permute-start | bytes 393224 | tf_op jit(solution)/shard_map/ppermute | solution.py:204
  122.0 4.3 %collective-permute-start.33 = (f32[128,256]{1,0:T(8,128)S(1)}, f32[128,256]{1,0:T(8,128)S(1)}, u32[]{:S(2)}, u32[]{:S(2)}) collective-permute-start(f32[128,256]{1,0:T(8,128)S(1)} %add.51), channel_id=1, source_target_pairs={{0,24},{1,97},{2,26},{3,99},{4,28},{5,101},{6,30},{7,103},{8,0},{9... | collective-permute-start | bytes 393224 | tf_op jit(solution)/shard_map/ppermute | solution.py:204
  126.4 17.4 %collective-permute-start.34 = (f32[128,256]{1,0:T(8,128)S(1)}, f32[128,256]{1,0:T(8,128)S(1)}, u32[]{:S(2)}, u32[]{:S(2)}) collective-permute-start(f32[128,256]{1,0:T(8,128)S(1)} %multiply_select_fusion), channel_id=1, source_target_pairs={{0,4},{2,6},{4,0},{6,2},{8,12},{10,14},{12,8},{14,10},{16,20},{18,... | collective-permute-start | bytes 393224 | tf_op jit(solution)/shard_map/ppermute | solution.py:204
  127.0 16.7 %collective-permute-start.35 = (f32[128,256]{1,0:T(8,128)S(1)}, f32[128,256]{1,0:T(8,128)S(1)}, u32[]{:S(2)}, u32[]{:S(2)}) collective-permute-start(f32[128,256]{1,0:T(8,128)S(1)} %multiply_select_fusion), channel_id=1, source_target_pairs={{0,2},{2,4},{4,6},{6,0},{8,10},{10,12},{12,14},{14,8},{16,18},{18,... | collective-permute-start | bytes 393224 | tf_op jit(solution)/shard_map/ppermute | solution.py:204
  127.7 16.0 %collective-permute-start.36 = (f32[128,256]{1,0:T(8,128)S(1)}, f32[128,256]{1,0:T(8,128)S(1)}, u32[]{:S(2)}, u32[]{:S(2)}) collective-permute-start(f32[128,256]{1,0:T(8,128)S(1)} %multiply_select_fusion), channel_id=1, source_target_pairs={{0,6},{2,0},{4,2},{6,4},{8,14},{10,8},{12,10},{14,12},{16,22},{18,... | collective-permute-start | bytes 393224 | tf_op jit(solution)/shard_map/ppermute | solution.py:204
  128.4 16.3 %collective-permute-start.38 = (f32[128,256]{1,0:T(8,128)S(1)}, f32[128,256]{1,0:T(8,128)S(1)}, u32[]{:S(2)}, u32[]{:S(2)}) collective-permute-start(f32[128,256]{1,0:T(8,128)S(1)} %multiply_select_fusion), channel_id=1, source_target_pairs={{1,0},{3,2},{5,4},{7,6},{9,8},{11,10},{13,12},{15,14},{17,16},{19,... | collective-permute-start | bytes 393224 | tf_op jit(solution)/shard_map/ppermute | solution.py:218
  144.8 3.2 %collective-permute-start.37 = (f32[128,256]{1,0:T(8,128)S(1)}, f32[128,256]{1,0:T(8,128)S(1)}, u32[]{:S(2)}, u32[]{:S(2)}) collective-permute-start(f32[128,256]{1,0:T(8,128)S(1)} %get-tuple-element.42), channel_id=1, source_target_pairs={{0,1},{2,3},{4,5},{6,7},{8,9},{10,11},{12,13},{14,15},{16,17},{18,... | collective-permute-start | bytes 393224 | tf_op jit(solution)/shard_map/ppermute | solution.py:217
  (9 other events, 24.5 us)

commit v2 on v1

--- a/solution.py
+++ b/solution.py
@@ -11,7 +11,7 @@
 EPS = 1e-06
 AXES = ("row", "col", "depth")
 GROUP = 4
-VMEM_LIMIT = 40 * 1024 * 1024
+MIB = 1024 * 1024
 
 
 def scale_row(meta_ref, slots, t):
@@ -93,7 +93,7 @@
     other_ref[...] = jnp.where(first, col_acc[...], row_acc[...])
 
 
-def load_kernel(slots, meta_ref, hbm_ref, tiles_ref, mine_ref, other_ref, row_acc, col_acc, sem):
+def load_kernel(slots, meta_ref, hbm_ref, tiles_ref, mine_ref, other_ref, first_ref, row_acc, col_acc, sem):
     count = meta_ref[2 * slots]
 
     def copy(t):
@@ -104,6 +104,7 @@
         return carry
 
     lax.fori_loop(0, count, start, 0)
+    first_ref[...] = jnp.where(meta_ref[2 * slots + 1] == 0, jnp.ones_like(first_ref), 0.0)
 
     def before(t):
         @pl.when(t < count)
@@ -136,26 +137,41 @@
     split(meta_ref[2 * slots + 1], row_acc, col_acc, mine_ref, other_ref)
 
 
-def final_kernel(slots, meta_ref, tiles_ref, row_ref, col_ref, out_ref):
+def final_kernel(slots, meta_ref, tiles_ref, row_ref, col_ref, out_ref, row_out, col_out, done, sem):
     count = meta_ref[2 * slots]
-    base = pl.program_id(0) * GROUP
-    for k in range(GROUP):
-        t = base + k
-
-        @pl.when(t < count)
-        def _():
-            row_vec = row_ref[pl.ds(meta_ref[t], 1), :]
-            col_vec = col_ref[pl.ds(meta_ref[slots + t], 1), :]
-            for h in range(2):
-                rows = slice(h * 128, (h + 1) * 128)
-                factor = jnp.broadcast_to(row_vec[:, rows], (128, 128)).T
-                for w in range(2):
-                    cols = slice(w * 128, (w + 1) * 128)
-                    out_ref[k, rows, cols] = tiles_ref[t, rows, cols] * factor * col_vec[:, cols]
-
-        @pl.when(t >= count)
-        def _():
-            out_ref[k] = jnp.zeros(out_ref.shape[1:], jnp.float32)
+    for vec_ref, flat in ((row_ref, row_out), (col_ref, col_out)):
+        for w in range(2):
+            flat[pl.ds(w, BLOCKS, 2), :] = vec_ref[:, w * 128 : (w + 1) * 128]
+
+    def copy(t):
+        return pltpu.make_async_copy(done.at[t], out_ref.at[t], sem.at[t])
+
+    def zero(t, carry):
+        done[t] = jnp.zeros(done.shape[1:], jnp.float32)
+        copy(t).start()
+        return carry
+
+    lax.fori_loop(count, slots, zero, 0)
+
+    def fill(t, carry):
+        row_vec = row_ref[pl.ds(meta_ref[t], 1), :]
+        col_vec = col_ref[pl.ds(meta_ref[slots + t], 1), :]
+        for h in range(2):
+            rows = slice(h * 128, (h + 1) * 128)
+            factor = jnp.broadcast_to(row_vec[:, rows], (128, 128)).T
+            for w in range(2):
+                cols = slice(w * 128, (w + 1) * 128)
+                done[t, rows, cols] = tiles_ref[t, rows, cols] * factor * col_vec[:, cols]
+        copy(t).start()
+        return carry
+
+    lax.fori_loop(0, count, fill, 0)
+
+    def finish(t, carry):
+        copy(t).wait()
+        return carry
+
+    lax.fori_loop(0, slots, finish, 0)
 
 
 def shards(sizes, tiles, tile_rows, tile_cols, tile_count):
@@ -163,14 +179,13 @@
     values = tiles[0, 0]
     slots, size = values.shape[0], values.shape[1]
     core = lax.axis_index("depth")
-    is_first = core == 0
     meta = jnp.concatenate(
         [tile_rows[0, 0], tile_cols[0, 0], tile_count[0, 0], core[None].astype(jnp.int32)]
     )
 
     smem = pl.BlockSpec(memory_space=pltpu.SMEM)
     vmem = pl.BlockSpec(memory_space=pltpu.VMEM)
-    params = pltpu.CompilerParams(vmem_limit_bytes=VMEM_LIMIT)
+    params = pltpu.CompilerParams(vmem_limit_bytes=8 * MIB)
     vec = jax.ShapeDtypeStruct((BLOCKS, size), jnp.float32)
     acc = pltpu.VMEM((BLOCKS, size), jnp.float32)
     kept = pltpu.VMEM((slots, size, size), jnp.float32)
@@ -181,26 +196,23 @@
             for x in range(xs):
                 for y in range(ys):
                     for d in range(2):
-                        to = move(z, x, y, d)
-                        if to is not None:
-                            pairs.append((index(z, x, y, d), index(*to)))
+                        pairs.append((index(z, x, y, d), index(*move(z, x, y, d))))
         return pairs
 
     def index(z, x, y, d):
-        return ((z % zs * xs + x % xs) * ys + y % ys) * 2 + d
+        return ((z * xs + x) * ys + y) * 2 + d
 
     steps = {
-        "x": lambda z, x, y, d, s: (z, x + s, y, d),
-        "y": lambda z, x, y, d, s: (z, x, y + s, d),
-        "z": lambda z, x, y, d, s: (z + s, x, y, d),
+        "x": lambda z, x, y, d, s: (z, x ^ s, y, d),
+        "y": lambda z, x, y, d, s: (z, x, y ^ s, d),
+        "z": lambda z, x, y, d, s: (z ^ s, x, y, d),
     }
 
     def slot(v, first_axis, second_axis):
         parts = [v]
         for s in (2, 1, 3):
             def move(z, x, y, d, s=s):
-                axis = first_axis if d == 0 else second_axis
-                return None if axis is None else steps[axis](z, x, y, d, s)
+                return steps[first_axis if d == 0 else second_axis](z, x, y, d, s)
             parts.append(lax.ppermute(v, AXES, spots(move)))
         return parts
 
@@ -214,21 +226,19 @@
         return old * lax.rsqrt(old * partial + EPS)
 
     swap = lambda v: lax.ppermute(v, "depth", [(0, 1), (1, 0)])
-    up = lambda v: lax.ppermute(v, "depth", [(0, 1)])
-    down = lambda v: lax.ppermute(v, "depth", [(1, 0)])
 
     def pick(a, b):
-        return jnp.where(is_first, a, b)
-
-    held, mine, other = pl.pallas_call(
+        return jnp.where(is_first > 0.5, a, b)
+
+    held, mine, other, is_first = pl.pallas_call(
         functools.partial(load_kernel, slots),
-        out_shape=(kept, vec, vec),
-        in_specs=[smem, pl.BlockSpec(memory_space=pl.ANY)],
-        out_specs=(vmem, vmem, vmem),
+        out_shape=(kept, vec, vec, vec),
+        in_specs=[smem, pl.BlockSpec(memory_space=pltpu.HBM)],
+        out_specs=(vmem, vmem, vmem, vmem),
         scratch_shapes=[acc, acc, pltpu.SemaphoreType.DMA((slots,))],
         compiler_params=params,
         name="load",
-    )(meta, values)
+    )(meta, pltpu.with_memory_space_constraint(values, pltpu.HBM))
     held = pltpu.with_memory_space_constraint(held, pltpu.VMEM)
 
     def call(kernel, outs, scratch, name):
@@ -255,12 +265,12 @@
     for pair in range(2):
         u = top(slot(m, "x", "z"))
         s = pick(u, next_factor(col_now, u))
-        part, col_now = run_row(s, down(s))
-        m = pick(s, jnp.maximum(part, up(part)))
+        part, col_now = run_row(s, swap(s))
+        m = pick(s, jnp.maximum(part, swap(part)))
         u = top(slot(m, "y", "x"))
         s = pick(next_factor(row_now, u), u)
-        part, row_now = run_col(s, up(s))
-        m = pick(jnp.maximum(part, down(part)), s)
+        part, row_now = run_col(s, swap(s))
+        m = pick(jnp.maximum(part, swap(part)), s)
         u = top(slot(m, "z", "y"))
         s = next_factor(pick(col_now, row_now), u)
         if pair == 0:
@@ -271,21 +281,22 @@
             m = mine + swap(other)
     u = total(slot(m, "x", "z"))
     s = pick(u, next_factor(col_now, u))
-    col_last = pick(down(s), s)
-    u = total(slot(s, "y", None))
+    col_last = pick(swap(s), s)
+    u = total(slot(s, "y", "x"))
     s = next_factor(row_now, u)
-    row_last = pick(s, up(s))
-
-    scaled = pl.pallas_call(
+    row_last = pick(s, swap(s))
+
+    flat = jax.ShapeDtypeStruct((2 * BLOCKS, size // 2), jnp.float32)
+    scaled, row_out, col_out = pl.pallas_call(
         functools.partial(final_kernel, slots),
-        out_shape=jax.ShapeDtypeStruct((slots, size, size), jnp.float32),
-        grid=(slots // GROUP,),
+        out_shape=(jax.ShapeDtypeStruct((slots, size, size), jnp.float32), flat, flat),
         in_specs=[smem, vmem, vmem, vmem],
-        out_specs=pl.BlockSpec((GROUP, size, size), lambda i: (i, 0, 0)),
-        compiler_params=params,
+        out_specs=(pl.BlockSpec(memory_space=pltpu.HBM), vmem, vmem),
+        scratch_shapes=[pltpu.VMEM((slots, size, size), jnp.float32), pltpu.SemaphoreType.DMA((slots,))],
+        compiler_params=pltpu.CompilerParams(vmem_limit_bytes=16 * MIB),
         name="scaled",
     )(meta, held, row_last, col_last)
-    return row_last.reshape(-1), col_last.reshape(-1), scaled[None, None]
+    return row_out.reshape(-1), col_out.reshape(-1), scaled[None, None]
 
 
 def solution(mesh):

time: 157 us -> 133 us (0.85)
  local copies, waits for them, and re-layouts: 10.8 us -> 0 us
  starting transfers between devices: 71.8 us -> 64 us
  Pallas kernels: 23.4 us -> 19.7 us
  waiting for transfers between devices: 48.1 us -> 46.5 us
    ppermute x10 -> x0, starting transfers between devices: 31.4 us -> none  [the longest x5 25 us: shards(): down = lambda v: lax.ppermute(v, 'depth', [(1, 0)])]
    ppermute x5 -> x15, starting transfers between devices: 3.92 us -> 29.9 us  [shards(): swap = lambda v: lax.ppermute(v, 'depth', [(0, 1), (1, 0)])]
    ppermute x10 -> x0, waiting for transfers between devices: 20.4 us -> none  [the longest x5 15.6 us: shards(): up = lambda v: lax.ppermute(v, 'depth', [(0, 1)])]
    unnamed x6 -> x0, local copies, waits for them, and re-layouts: 10.8 us -> none
    ppermute x24, waiting for transfers between devices: 22.1 us -> 32.7 us  [slot(): parts.append(lax.ppermute(v, AXES, spots(move)))]
    ppermute x5 -> x15, waiting for transfers between devices: 5.63 us -> 13.8 us  [shards(): swap = lambda v: lax.ppermute(v, 'depth', [(0, 1), (1, 0)])]
    ppermute x24, starting transfers between devices: 36.4 us -> 34.2 us  [slot(): parts.append(lax.ppermute(v, AXES, spots(move)))]
    pallas_call x1, Pallas kernels: 8.19 us -> 6.38 us  [shards(): pl.pallas_call(functools.partial(final_kernel, slots), out_shape=(jax.Sha...]
  transfers between devices with their start and end apart: 39 -> 39, of which waited for: 30 -> 36; matrix products, arithmetic and copies ran while one was open for 0% -> 0% of each run, Pallas kernels for 0% -> 0%
where the time goes in v2:
time: 133 us
  starting transfers between devices  64 us (48%)
  waiting for transfers between devices  46.5 us (35%)
  Pallas kernels  19.7 us (15%)
  between operations  1.42 us (1%)
  other arithmetic  1.38 us (1%)
    ppermute x24, starting transfers between devices, slot(): parts.append(lax.ppermute(v, AXES, spots(move)))  34.2 us
    ppermute x24, waiting for transfers between devices, slot(): parts.append(lax.ppermute(v, AXES, spots(move)))  32.7 us
    ppermute x15, starting transfers between devices, shards(): swap = lambda v: lax.ppermute(v, 'depth', [(0, 1), (1, 0)])  29.9 us
    ppermute x15, waiting for transfers between devices, shards(): swap = lambda v: lax.ppermute(v, 'depth', [(0, 1), (1, 0)])  13.8 us
    pallas_call x6, Pallas kernels, run(): pl.pallas_call(kernel, out_shape=(vec,) * outs, in_specs=[smem] + [vmem]...  9.94 us
    pallas_call x1, Pallas kernels, shards(): pl.pallas_call(functools.partial(final_kernel, slots), out_shape=(jax.Sha...  6.38 us
    pallas_call x1, Pallas kernels, shards(): pl.pallas_call(functools.partial(load_kernel, slots), out_shape=(kept, ve...  3.39 us
  transfers between devices with their start and end apart: 39, of which 36 were waited for; matrix products, arithmetic and copies ran while one was open for 0% of the time, Pallas kernels for 0%

profile of v2, /device:TPU:1, one launch (start us, length us, event | category | flops | bytes accessed | tf_op | source)
XLA Modules:
  0.0 133.0 jit_solution(9948342481599548401)
XLA Ops:
  2.0 3.4 %load.1 = (f32[48,256,256]{2,1,0:T(8,128)S(1)}, f32[128,256]{1,0:T(8,128)S(1)}, f32[128,256]{1,0:T(8,128)S(1)}, f32[128,256]{1,0:T(8,128)S(1)}) custom-call(s32[98]{0:T(128)S(1)} %pad_add_fusion.meta_ref, f32[48,256,256]{2,1,0:T(8,128)} %bitcast.9), custom_call_target="tpu_custom_call" | custom-call | tf_op jit(solution)/shard_map/load/pallas_call | solution.py:233
  5.4 2.7 %collective-permute-start = (f32[128,256]{1,0:T(8,128)S(1)}, f32[128,256]{1,0:T(8,128)S(1)}, u32[]{:S(2)}, u32[]{:S(2)}) collective-permute-start(f32[128,256]{1,0:T(8,128)S(1)} %get-tuple-element.29), channel_id=1, source_target_pairs={{0,1},{1,0},{2,3},{3,2},{4,5},{5,4},{6,7},{7,6},{8,9},{9,8},{10,11... | collective-permute-start | bytes 393224 | tf_op jit(solution)/shard_map/ppermute | solution.py:228
  9.1 3.0 %collective-permute-start.3 = (f32[128,256]{1,0:T(8,128)S(1)}, f32[128,256]{1,0:T(8,128)S(1)}, u32[]{:S(2)}, u32[]{:S(2)}) collective-permute-start(f32[128,256]{1,0:T(8,128)S(1)} %max.72), channel_id=1, source_target_pairs={{0,24},{1,97},{2,26},{3,99},{4,28},{5,101},{6,30},{7,103},{8,16},{... | collective-permute-start | bytes 393224 | tf_op jit(solution)/shard_map/ppermute | solution.py:216
  15.9 1.9 %collective-permute-done.1 = f32[128,256]{1,0:T(8,128)S(1)} collective-permute-done((f32[128,256]{1,0:T(8,128)S(1)}, f32[128,256]{1,0:T(8,128)S(1)}, u32[]{:S(2)}, u32[]{:S(2)}) %collective-permute-start.1) | collective-permute-done | bytes 131104 | tf_op jit(solution)/shard_map/ppermute | solution.py:216
  17.9 1.6 %collective-permute-start.4 = (f32[128,256]{1,0:T(8,128)S(1)}, f32[128,256]{1,0:T(8,128)S(1)}, u32[]{:S(2)}, u32[]{:S(2)}) collective-permute-start(f32[128,256]{1,0:T(8,128)S(1)} %get-tuple-element.49.s_ref), channel_id=1, source_target_pairs={{0,1},{1,0},{2,3},{3,2},{4,5},{5,4},{6,7},{7,6},{8,9},{9,8},{10,11... | collective-permute-start | bytes 393224 | tf_op jit(solution)/shard_map/ppermute | solution.py:228
  24.3 2.5 %collective-permute-start.8 = (f32[128,256]{1,0:T(8,128)S(1)}, f32[128,256]{1,0:T(8,128)S(1)}, u32[]{:S(2)}, u32[]{:S(2)}) collective-permute-start(f32[128,256]{1,0:T(8,128)S(1)} %maximum_select_fusion.3), channel_id=1, source_target_pairs={{0,6},{1,25},{2,4},{3,27},{4,2},{5,29},{6,0},{7,31},{8,14},{9,17},... | collective-permute-start | bytes 393224 | tf_op jit(solution)/shard_map/ppermute | solution.py:216
  29.4 1.5 %collective-permute-done.7 = f32[128,256]{1,0:T(8,128)S(1)} collective-permute-done((f32[128,256]{1,0:T(8,128)S(1)}, f32[128,256]{1,0:T(8,128)S(1)}, u32[]{:S(2)}, u32[]{:S(2)}) %collective-permute-start.7) | collective-permute-done | bytes 131104 | tf_op jit(solution)/shard_map/ppermute | solution.py:216
  32.2 4.0 %collective-permute-start.9 = (f32[128,256]{1,0:T(8,128)S(1)}, f32[128,256]{1,0:T(8,128)S(1)}, u32[]{:S(2)}, u32[]{:S(2)}) collective-permute-start(f32[128,256]{1,0:T(8,128)S(1)} %rsqrt_select_fusion.s_ref), channel_id=1, source_target_pairs={{0,1},{1,0},{2,3},{3,2},{4,5},{5,4},{6,7},{7,6},{8,9},{9,8},{10,11... | collective-permute-start | bytes 393224 | tf_op jit(solution)/shard_map/ppermute | solution.py:228
  41.0 3.2 %collective-permute-start.13 = (f32[128,256]{1,0:T(8,128)S(1)}, f32[128,256]{1,0:T(8,128)S(1)}, u32[]{:S(2)}, u32[]{:S(2)}) collective-permute-start(f32[128,256]{1,0:T(8,128)S(1)} %maximum_select_fusion.2), channel_id=1, source_target_pairs={{0,96},{1,7},{2,98},{3,5},{4,100},{5,3},{6,102},{7,1},{8,104},{9,1... | collective-permute-start | bytes 393224 | tf_op jit(solution)/shard_map/ppermute | solution.py:216
  48.0 1.8 %collective-permute-done.11 = f32[128,256]{1,0:T(8,128)S(1)} collective-permute-done((f32[128,256]{1,0:T(8,128)S(1)}, f32[128,256]{1,0:T(8,128)S(1)}, u32[]{:S(2)}, u32[]{:S(2)}) %collective-permute-start.11) | collective-permute-done | bytes 131104 | tf_op jit(solution)/shard_map/ppermute | solution.py:216
  51.6 2.1 %both.1 = (f32[128,256]{1,0:T(8,128)S(1)}, f32[128,256]{1,0:T(8,128)S(1)}, f32[128,256]{1,0:T(8,128)S(1)}, f32[128,256]{1,0:T(8,128)S(1)}) custom-call(s32[98]{0:T(128)S(1)} %pad_add_fusion.meta_ref, f32[48,256,256]{2,1,0:T(8,128)S(1)} %get-tuple-element.26.tiles_ref, f32[128,256]{1,0:T(8,128)S(1)} %rsqrt_multiply_fusion.2.s_ref, ...), custom_call_target="tpu_custom_call" | custom-call | tf_op jit(solution)/shard_map/both/pallas_call | solution.py:246
  53.7 2.0 %collective-permute-start.15 = (f32[128,256]{1,0:T(8,128)S(1)}, f32[128,256]{1,0:T(8,128)S(1)}, u32[]{:S(2)}, u32[]{:S(2)}) collective-permute-start(f32[128,256]{1,0:T(8,128)S(1)} %get-tuple-element.35), channel_id=1, source_target_pairs={{0,1},{1,0},{2,3},{3,2},{4,5},{5,4},{6,7},{7,6},{8,9},{9,8},{10,11... | collective-permute-start | bytes 393224 | tf_op jit(solution)/shard_map/ppermute | solution.py:228
  57.9 2.7 %collective-permute-start.16 = (f32[128,256]{1,0:T(8,128)S(1)}, f32[128,256]{1,0:T(8,128)S(1)}, u32[]{:S(2)}, u32[]{:S(2)}) collective-permute-start(f32[128,256]{1,0:T(8,128)S(1)} %max.84), channel_id=1, source_target_pairs={{0,16},{1,65},{2,18},{3,67},{4,20},{5,69},{6,22},{7,71},{8,24},{9,... | collective-permute-start | bytes 393224 | tf_op jit(solution)/shard_map/ppermute | solution.py:216
  60.6 1.5 %collective-permute-done.18 = f32[128,256]{1,0:T(8,128)S(1)} collective-permute-done((f32[128,256]{1,0:T(8,128)S(1)}, f32[128,256]{1,0:T(8,128)S(1)}, u32[]{:S(2)}, u32[]{:S(2)}) %collective-permute-start.18) | collective-permute-done | bytes 131104 | tf_op jit(solution)/shard_map/ppermute | solution.py:216
  62.1 2.3 %collective-permute-done.16 = f32[128,256]{1,0:T(8,128)S(1)} collective-permute-done((f32[128,256]{1,0:T(8,128)S(1)}, f32[128,256]{1,0:T(8,128)S(1)}, u32[]{:S(2)}, u32[]{:S(2)}) %collective-permute-start.16) | collective-permute-done | bytes 131104 | tf_op jit(solution)/shard_map/ppermute | solution.py:216
  64.4 2.3 %collective-permute-start.19 = (f32[128,256]{1,0:T(8,128)S(1)}, f32[128,256]{1,0:T(8,128)S(1)}, u32[]{:S(2)}, u32[]{:S(2)}) collective-permute-start(f32[128,256]{1,0:T(8,128)S(1)} %multiply_select_fusion.2.s_ref), channel_id=1, source_target_pairs={{0,1},{1,0},{2,3},{3,2},{4,5},{5,4},{6,7},{7,6},{8,9},{9,8},{10,11... | collective-permute-start | bytes 393224 | tf_op jit(solution)/shard_map/ppermute | solution.py:228
  67.7 1.4 %rows.3 = (f32[128,256]{1,0:T(8,128)S(1)}, f32[128,256]{1,0:T(8,128)S(1)}) custom-call(s32[98]{0:T(128)S(1)} %pad_add_fusion.meta_ref, f32[48,256,256]{2,1,0:T(8,128)S(1)} %get-tuple-element.26.tiles_ref, f32[128,256]{1,0:T(8,128)S(1)} %multiply_select_fusion.2.s_ref, f32[128,256]{1,0:T(8,128)S(1)} %collective-permute-done.19.g_ref), custom_call_target="tpu_custom_call" | custom-call | tf_op jit(solution)/shard_map/rows/pallas_call | solution.py:246
  71.5 3.1 %collective-permute-start.23 = (f32[128,256]{1,0:T(8,128)S(1)}, f32[128,256]{1,0:T(8,128)S(1)}, u32[]{:S(2)}, u32[]{:S(2)}) collective-permute-start(f32[128,256]{1,0:T(8,128)S(1)} %maximum_select_fusion.1), channel_id=1, source_target_pairs={{0,6},{1,25},{2,4},{3,27},{4,2},{5,29},{6,0},{7,31},{8,14},{9,17},... | collective-permute-start | bytes 393224 | tf_op jit(solution)/shard_map/ppermute | solution.py:216
  77.0 1.8 %collective-permute-done.22 = f32[128,256]{1,0:T(8,128)S(1)} collective-permute-done((f32[128,256]{1,0:T(8,128)S(1)}, f32[128,256]{1,0:T(8,128)S(1)}, u32[]{:S(2)}, u32[]{:S(2)}) %collective-permute-start.22) | collective-permute-done | bytes 131104 | tf_op jit(solution)/shard_map/ppermute | solution.py:216
  80.0 4.0 %collective-permute-start.24 = (f32[128,256]{1,0:T(8,128)S(1)}, f32[128,256]{1,0:T(8,128)S(1)}, u32[]{:S(2)}, u32[]{:S(2)}) collective-permute-start(f32[128,256]{1,0:T(8,128)S(1)} %multiply_select_fusion.1.s_ref), channel_id=1, source_target_pairs={{0,1},{1,0},{2,3},{3,2},{4,5},{5,4},{6,7},{7,6},{8,9},{9,8},{10,11... | collective-permute-start | bytes 393224 | tf_op jit(solution)/shard_map/ppermute | solution.py:228
  88.8 3.2 %collective-permute-start.28 = (f32[128,256]{1,0:T(8,128)S(1)}, f32[128,256]{1,0:T(8,128)S(1)}, u32[]{:S(2)}, u32[]{:S(2)}) collective-permute-start(f32[128,256]{1,0:T(8,128)S(1)} %maximum_select_fusion), channel_id=1, source_target_pairs={{0,96},{1,7},{2,98},{3,5},{4,100},{5,3},{6,102},{7,1},{8,104},{9,1... | collective-permute-start | bytes 393224 | tf_op jit(solution)/shard_map/ppermute | solution.py:216
  95.8 1.8 %collective-permute-done.26 = f32[128,256]{1,0:T(8,128)S(1)} collective-permute-done((f32[128,256]{1,0:T(8,128)S(1)}, f32[128,256]{1,0:T(8,128)S(1)}, u32[]{:S(2)}, u32[]{:S(2)}) %collective-permute-start.26) | collective-permute-done | bytes 131104 | tf_op jit(solution)/shard_map/ppermute | solution.py:216
  99.4 2.1 %sums.1 = (f32[128,256]{1,0:T(8,128)S(1)}, f32[128,256]{1,0:T(8,128)S(1)}, f32[128,256]{1,0:T(8,128)S(1)}, f32[128,256]{1,0:T(8,128)S(1)}) custom-call(s32[98]{0:T(128)S(1)} %pad_add_fusion.meta_ref, f32[48,256,256]{2,1,0:T(8,128)S(1)} %get-tuple-element.26.tiles_ref, f32[128,256]{1,0:T(8,128)S(1)} %rsqrt_multiply_fusion.1.s_ref, ...), custom_call_target="tpu_custom_call" | custom-call | tf_op jit(solution)/shard_map/sums/pallas_call | solution.py:246
  101.4 1.9 %collective-permute-start.30 = (f32[128,256]{1,0:T(8,128)S(1)}, f32[128,256]{1,0:T(8,128)S(1)}, u32[]{:S(2)}, u32[]{:S(2)}) collective-permute-start(f32[128,256]{1,0:T(8,128)S(1)} %get-tuple-element.44), channel_id=1, source_target_pairs={{0,1},{1,0},{2,3},{3,2},{4,5},{5,4},{6,7},{7,6},{8,9},{9,8},{10,11... | collective-permute-start | bytes 393224 | tf_op jit(solution)/shard_map/ppermute | solution.py:228
  105.6 2.7 %collective-permute-start.31 = (f32[128,256]{1,0:T(8,128)S(1)}, f32[128,256]{1,0:T(8,128)S(1)}, u32[]{:S(2)}, u32[]{:S(2)}) collective-permute-start(f32[128,256]{1,0:T(8,128)S(1)} %add.51), channel_id=1, source_target_pairs={{0,16},{1,65},{2,18},{3,67},{4,20},{5,69},{6,22},{7,71},{8,24},{9,... | collective-permute-start | bytes 393224 | tf_op jit(solution)/shard_map/ppermute | solution.py:216
  108.3 1.5 %collective-permute-done.33 = f32[128,256]{1,0:T(8,128)S(1)} collective-permute-done((f32[128,256]{1,0:T(8,128)S(1)}, f32[128,256]{1,0:T(8,128)S(1)}, u32[]{:S(2)}, u32[]{:S(2)}) %collective-permute-start.33) | collective-permute-done | bytes 131104 | tf_op jit(solution)/shard_map/ppermute | solution.py:216
  109.8 2.3 %collective-permute-done.31 = f32[128,256]{1,0:T(8,128)S(1)} collective-permute-done((f32[128,256]{1,0:T(8,128)S(1)}, f32[128,256]{1,0:T(8,128)S(1)}, u32[]{:S(2)}, u32[]{:S(2)}) %collective-permute-start.31) | collective-permute-done | bytes 131104 | tf_op jit(solution)/shard_map/ppermute | solution.py:216
  112.1 2.3 %collective-permute-start.38 = (f32[128,256]{1,0:T(8,128)S(1)}, f32[128,256]{1,0:T(8,128)S(1)}, u32[]{:S(2)}, u32[]{:S(2)}) collective-permute-start(f32[128,256]{1,0:T(8,128)S(1)} %multiply_select_fusion), channel_id=1, source_target_pairs={{0,1},{1,0},{2,3},{3,2},{4,5},{5,4},{6,7},{7,6},{8,9},{9,8},{10,11... | collective-permute-start | bytes 393224 | tf_op jit(solution)/shard_map/ppermute | solution.py:228
  114.4 3.4 %collective-permute-start.36 = (f32[128,256]{1,0:T(8,128)S(1)}, f32[128,256]{1,0:T(8,128)S(1)}, u32[]{:S(2)}, u32[]{:S(2)}) collective-permute-start(f32[128,256]{1,0:T(8,128)S(1)} %multiply_select_fusion), channel_id=1, source_target_pairs={{0,6},{1,25},{2,4},{3,27},{4,2},{5,29},{6,0},{7,31},{8,14},{9,17},... | collective-permute-start | bytes 393224 | tf_op jit(solution)/shard_map/ppermute | solution.py:216
  121.6 1.5 %collective-permute-done.34 = f32[128,256]{1,0:T(8,128)S(1)} collective-permute-done((f32[128,256]{1,0:T(8,128)S(1)}, f32[128,256]{1,0:T(8,128)S(1)}, u32[]{:S(2)}, u32[]{:S(2)}) %collective-permute-start.34) | collective-permute-done | bytes 131104 | tf_op jit(solution)/shard_map/ppermute | solution.py:216
  123.2 2.4 %collective-permute-start.37 = (f32[128,256]{1,0:T(8,128)S(1)}, f32[128,256]{1,0:T(8,128)S(1)}, u32[]{:S(2)}, u32[]{:S(2)}) collective-permute-start(f32[128,256]{1,0:T(8,128)S(1)} %get-tuple-element.52), channel_id=1, source_target_pairs={{0,1},{1,0},{2,3},{3,2},{4,5},{5,4},{6,7},{7,6},{8,9},{9,8},{10,11... | collective-permute-start | bytes 393224 | tf_op jit(solution)/shard_map/ppermute | solution.py:228
  126.6 6.4 %scaled.1 = (f32[48,256,256]{2,1,0:T(8,128)}, f32[256,128]{1,0:T(8,128)}, f32[256,128]{1,0:T(8,128)}) custom-call(s32[98]{0:T(128)S(1)} %pad_add_fusion.meta_ref, f32[48,256,256]{2,1,0:T(8,128)S(1)} %get-tuple-element.26.tiles_ref, f32[128,256]{1,0:T(8,128)S(1)} %select_n.51.row_ref, f32[128,256]{1,0:T(8,128)S(1)} %get-tuple-element.51.col_ref), custom_call_target="tpu_custom_call" | custom-call | tf_op jit(solution)/shard_map/scaled/pallas_call | solution.py:290
  (71 shorter events, 51.3 us)
Async XLA Ops:
  5.4 3.7 %collective-permute-start = (f32[128,256]{1,0:T(8,128)S(1)}, f32[128,256]{1,0:T(8,128)S(1)}, u32[]{:S(2)}, u32[]{:S(2)}) collective-permute-start(f32[128,256]{1,0:T(8,128)S(1)} %get-tuple-element.29), channel_id=1, source_target_pairs={{0,1},{1,0},{2,3},{3,2},{4,5},{5,4},{6,7},{7,6},{8,9},{9,8},{10,11... | collective-permute-start | bytes 393224 | tf_op jit(solution)/shard_map/ppermute | solution.py:228
  9.1 5.6 %collective-permute-start.3 = (f32[128,256]{1,0:T(8,128)S(1)}, f32[128,256]{1,0:T(8,128)S(1)}, u32[]{:S(2)}, u32[]{:S(2)}) collective-permute-start(f32[128,256]{1,0:T(8,128)S(1)} %max.72), channel_id=1, source_target_pairs={{0,24},{1,97},{2,26},{3,99},{4,28},{5,101},{6,30},{7,103},{8,16},{... | collective-permute-start | bytes 393224 | tf_op jit(solution)/shard_map/ppermute | solution.py:216
  12.1 3.8 %collective-permute-start.2 = (f32[128,256]{1,0:T(8,128)S(1)}, f32[128,256]{1,0:T(8,128)S(1)}, u32[]{:S(2)}, u32[]{:S(2)}) collective-permute-start(f32[128,256]{1,0:T(8,128)S(1)} %max.72), channel_id=1, source_target_pairs={{0,8},{1,33},{2,10},{3,35},{4,12},{5,37},{6,14},{7,39},{8,0},{9,41... | collective-permute-start | bytes 393224 | tf_op jit(solution)/shard_map/ppermute | solution.py:216
  12.2 5.6 %collective-permute-start.1 = (f32[128,256]{1,0:T(8,128)S(1)}, f32[128,256]{1,0:T(8,128)S(1)}, u32[]{:S(2)}, u32[]{:S(2)}) collective-permute-start(f32[128,256]{1,0:T(8,128)S(1)} %max.72), channel_id=1, source_target_pairs={{0,16},{1,65},{2,18},{3,67},{4,20},{5,69},{6,22},{7,71},{8,24},{9,... | collective-permute-start | bytes 393224 | tf_op jit(solution)/shard_map/ppermute | solution.py:216
  24.3 5.1 %collective-permute-start.8 = (f32[128,256]{1,0:T(8,128)S(1)}, f32[128,256]{1,0:T(8,128)S(1)}, u32[]{:S(2)}, u32[]{:S(2)}) collective-permute-start(f32[128,256]{1,0:T(8,128)S(1)} %maximum_select_fusion.3), channel_id=1, source_target_pairs={{0,6},{1,25},{2,4},{3,27},{4,2},{5,29},{6,0},{7,31},{8,14},{9,17},... | collective-permute-start | bytes 393224 | tf_op jit(solution)/shard_map/ppermute | solution.py:216
  26.8 4.1 %collective-permute-start.7 = (f32[128,256]{1,0:T(8,128)S(1)}, f32[128,256]{1,0:T(8,128)S(1)}, u32[]{:S(2)}, u32[]{:S(2)}) collective-permute-start(f32[128,256]{1,0:T(8,128)S(1)} %maximum_select_fusion.3), channel_id=1, source_target_pairs={{0,2},{1,9},{2,0},{3,11},{4,6},{5,13},{6,4},{7,15},{8,10},{9,1},{1... | collective-permute-start | bytes 393224 | tf_op jit(solution)/shard_map/ppermute | solution.py:216
  26.8 5.3 %collective-permute-start.6 = (f32[128,256]{1,0:T(8,128)S(1)}, f32[128,256]{1,0:T(8,128)S(1)}, u32[]{:S(2)}, u32[]{:S(2)}) collective-permute-start(f32[128,256]{1,0:T(8,128)S(1)} %maximum_select_fusion.3), channel_id=1, source_target_pairs={{0,4},{1,17},{2,6},{3,19},{4,0},{5,21},{6,2},{7,23},{8,12},{9,25},... | collective-permute-start | bytes 393224 | tf_op jit(solution)/shard_map/ppermute | solution.py:216
  32.2 5.0 %collective-permute-start.9 = (f32[128,256]{1,0:T(8,128)S(1)}, f32[128,256]{1,0:T(8,128)S(1)}, u32[]{:S(2)}, u32[]{:S(2)}) collective-permute-start(f32[128,256]{1,0:T(8,128)S(1)} %rsqrt_select_fusion.s_ref), channel_id=1, source_target_pairs={{0,1},{1,0},{2,3},{3,2},{4,5},{5,4},{6,7},{7,6},{8,9},{9,8},{10,11... | collective-permute-start | bytes 393224 | tf_op jit(solution)/shard_map/ppermute | solution.py:228
  41.0 5.9 %collective-permute-start.13 = (f32[128,256]{1,0:T(8,128)S(1)}, f32[128,256]{1,0:T(8,128)S(1)}, u32[]{:S(2)}, u32[]{:S(2)}) collective-permute-start(f32[128,256]{1,0:T(8,128)S(1)} %maximum_select_fusion.2), channel_id=1, source_target_pairs={{0,96},{1,7},{2,98},{3,5},{4,100},{5,3},{6,102},{7,1},{8,104},{9,1... | collective-permute-start | bytes 393224 | tf_op jit(solution)/shard_map/ppermute | solution.py:216
  44.2 3.8 %collective-permute-start.12 = (f32[128,256]{1,0:T(8,128)S(1)}, f32[128,256]{1,0:T(8,128)S(1)}, u32[]{:S(2)}, u32[]{:S(2)}) collective-permute-start(f32[128,256]{1,0:T(8,128)S(1)} %maximum_select_fusion.2), channel_id=1, source_target_pairs={{0,32},{1,3},{2,34},{3,1},{4,36},{5,7},{6,38},{7,5},{8,40},{9,11},... | collective-permute-start | bytes 393224 | tf_op jit(solution)/shard_map/ppermute | solution.py:216
  44.2 5.6 %collective-permute-start.11 = (f32[128,256]{1,0:T(8,128)S(1)}, f32[128,256]{1,0:T(8,128)S(1)}, u32[]{:S(2)}, u32[]{:S(2)}) collective-permute-start(f32[128,256]{1,0:T(8,128)S(1)} %maximum_select_fusion.2), channel_id=1, source_target_pairs={{0,64},{1,5},{2,66},{3,7},{4,68},{5,1},{6,70},{7,3},{8,72},{9,13},... | collective-permute-start | bytes 393224 | tf_op jit(solution)/shard_map/ppermute | solution.py:216
  53.7 2.9 %collective-permute-start.15 = (f32[128,256]{1,0:T(8,128)S(1)}, f32[128,256]{1,0:T(8,128)S(1)}, u32[]{:S(2)}, u32[]{:S(2)}) collective-permute-start(f32[128,256]{1,0:T(8,128)S(1)} %get-tuple-element.35), channel_id=1, source_target_pairs={{0,1},{1,0},{2,3},{3,2},{4,5},{5,4},{6,7},{7,6},{8,9},{9,8},{10,11... | collective-permute-start | bytes 393224 | tf_op jit(solution)/shard_map/ppermute | solution.py:228
  56.7 5.4 %collective-permute-start.18 = (f32[128,256]{1,0:T(8,128)S(1)}, f32[128,256]{1,0:T(8,128)S(1)}, u32[]{:S(2)}, u32[]{:S(2)}) collective-permute-start(f32[128,256]{1,0:T(8,128)S(1)} %max.84), channel_id=1, source_target_pairs={{0,24},{1,97},{2,26},{3,99},{4,28},{5,101},{6,30},{7,103},{8,16},{... | collective-permute-start | bytes 393224 | tf_op jit(solution)/shard_map/ppermute | solution.py:216
  57.1 5.0 %collective-permute-start.17 = (f32[128,256]{1,0:T(8,128)S(1)}, f32[128,256]{1,0:T(8,128)S(1)}, u32[]{:S(2)}, u32[]{:S(2)}) collective-permute-start(f32[128,256]{1,0:T(8,128)S(1)} %max.84), channel_id=1, source_target_pairs={{0,8},{1,33},{2,10},{3,35},{4,12},{5,37},{6,14},{7,39},{8,0},{9,41... | collective-permute-start | bytes 393224 | tf_op jit(solution)/shard_map/ppermute | solution.py:216
  57.9 6.5 %collective-permute-start.16 = (f32[128,256]{1,0:T(8,128)S(1)}, f32[128,256]{1,0:T(8,128)S(1)}, u32[]{:S(2)}, u32[]{:S(2)}) collective-permute-start(f32[128,256]{1,0:T(8,128)S(1)} %max.84), channel_id=1, source_target_pairs={{0,16},{1,65},{2,18},{3,67},{4,20},{5,69},{6,22},{7,71},{8,24},{9,... | collective-permute-start | bytes 393224 | tf_op jit(solution)/shard_map/ppermute | solution.py:216
  64.4 3.3 %collective-permute-start.19 = (f32[128,256]{1,0:T(8,128)S(1)}, f32[128,256]{1,0:T(8,128)S(1)}, u32[]{:S(2)}, u32[]{:S(2)}) collective-permute-start(f32[128,256]{1,0:T(8,128)S(1)} %multiply_select_fusion.2.s_ref), channel_id=1, source_target_pairs={{0,1},{1,0},{2,3},{3,2},{4,5},{5,4},{6,7},{7,6},{8,9},{9,8},{10,11... | collective-permute-start | bytes 393224 | tf_op jit(solution)/shard_map/ppermute | solution.py:228
  71.5 5.5 %collective-permute-start.23 = (f32[128,256]{1,0:T(8,128)S(1)}, f32[128,256]{1,0:T(8,128)S(1)}, u32[]{:S(2)}, u32[]{:S(2)}) collective-permute-start(f32[128,256]{1,0:T(8,128)S(1)} %maximum_select_fusion.1), channel_id=1, source_target_pairs={{0,6},{1,25},{2,4},{3,27},{4,2},{5,29},{6,0},{7,31},{8,14},{9,17},... | collective-permute-start | bytes 393224 | tf_op jit(solution)/shard_map/ppermute | solution.py:216
  74.6 4.1 %collective-permute-start.22 = (f32[128,256]{1,0:T(8,128)S(1)}, f32[128,256]{1,0:T(8,128)S(1)}, u32[]{:S(2)}, u32[]{:S(2)}) collective-permute-start(f32[128,256]{1,0:T(8,128)S(1)} %maximum_select_fusion.1), channel_id=1, source_target_pairs={{0,2},{1,9},{2,0},{3,11},{4,6},{5,13},{6,4},{7,15},{8,10},{9,1},{1... | collective-permute-start | bytes 393224 | tf_op jit(solution)/shard_map/ppermute | solution.py:216
  74.6 5.3 %collective-permute-start.21 = (f32[128,256]{1,0:T(8,128)S(1)}, f32[128,256]{1,0:T(8,128)S(1)}, u32[]{:S(2)}, u32[]{:S(2)}) collective-permute-start(f32[128,256]{1,0:T(8,128)S(1)} %maximum_select_fusion.1), channel_id=1, source_target_pairs={{0,4},{1,17},{2,6},{3,19},{4,0},{5,21},{6,2},{7,23},{8,12},{9,25},... | collective-permute-start | bytes 393224 | tf_op jit(solution)/shard_map/ppermute | solution.py:216
  80.0 5.0 %collective-permute-start.24 = (f32[128,256]{1,0:T(8,128)S(1)}, f32[128,256]{1,0:T(8,128)S(1)}, u32[]{:S(2)}, u32[]{:S(2)}) collective-permute-start(f32[128,256]{1,0:T(8,128)S(1)} %multiply_select_fusion.1.s_ref), channel_id=1, source_target_pairs={{0,1},{1,0},{2,3},{3,2},{4,5},{5,4},{6,7},{7,6},{8,9},{9,8},{10,11... | collective-permute-start | bytes 393224 | tf_op jit(solution)/shard_map/ppermute | solution.py:228
  88.8 5.9 %collective-permute-start.28 = (f32[128,256]{1,0:T(8,128)S(1)}, f32[128,256]{1,0:T(8,128)S(1)}, u32[]{:S(2)}, u32[]{:S(2)}) collective-permute-start(f32[128,256]{1,0:T(8,128)S(1)} %maximum_select_fusion), channel_id=1, source_target_pairs={{0,96},{1,7},{2,98},{3,5},{4,100},{5,3},{6,102},{7,1},{8,104},{9,1... | collective-permute-start | bytes 393224 | tf_op jit(solution)/shard_map/ppermute | solution.py:216
  92.0 3.8 %collective-permute-start.27 = (f32[128,256]{1,0:T(8,128)S(1)}, f32[128,256]{1,0:T(8,128)S(1)}, u32[]{:S(2)}, u32[]{:S(2)}) collective-permute-start(f32[128,256]{1,0:T(8,128)S(1)} %maximum_select_fusion), channel_id=1, source_target_pairs={{0,32},{1,3},{2,34},{3,1},{4,36},{5,7},{6,38},{7,5},{8,40},{9,11},... | collective-permute-start | bytes 393224 | tf_op jit(solution)/shard_map/ppermute | solution.py:216
  92.0 5.6 %collective-permute-start.26 = (f32[128,256]{1,0:T(8,128)S(1)}, f32[128,256]{1,0:T(8,128)S(1)}, u32[]{:S(2)}, u32[]{:S(2)}) collective-permute-start(f32[128,256]{1,0:T(8,128)S(1)} %maximum_select_fusion), channel_id=1, source_target_pairs={{0,64},{1,5},{2,66},{3,7},{4,68},{5,1},{6,70},{7,3},{8,72},{9,13},... | collective-permute-start | bytes 393224 | tf_op jit(solution)/shard_map/ppermute | solution.py:216
  101.4 2.9 %collective-permute-start.30 = (f32[128,256]{1,0:T(8,128)S(1)}, f32[128,256]{1,0:T(8,128)S(1)}, u32[]{:S(2)}, u32[]{:S(2)}) collective-permute-start(f32[128,256]{1,0:T(8,128)S(1)} %get-tuple-element.44), channel_id=1, source_target_pairs={{0,1},{1,0},{2,3},{3,2},{4,5},{5,4},{6,7},{7,6},{8,9},{9,8},{10,11... | collective-permute-start | bytes 393224 | tf_op jit(solution)/shard_map/ppermute | solution.py:228
  104.4 5.4 %collective-permute-start.33 = (f32[128,256]{1,0:T(8,128)S(1)}, f32[128,256]{1,0:T(8,128)S(1)}, u32[]{:S(2)}, u32[]{:S(2)}) collective-permute-start(f32[128,256]{1,0:T(8,128)S(1)} %add.51), channel_id=1, source_target_pairs={{0,24},{1,97},{2,26},{3,99},{4,28},{5,101},{6,30},{7,103},{8,16},{... | collective-permute-start | bytes 393224 | tf_op jit(solution)/shard_map/ppermute | solution.py:216
  104.8 5.0 %collective-permute-start.32 = (f32[128,256]{1,0:T(8,128)S(1)}, f32[128,256]{1,0:T(8,128)S(1)}, u32[]{:S(2)}, u32[]{:S(2)}) collective-permute-start(f32[128,256]{1,0:T(8,128)S(1)} %add.51), channel_id=1, source_target_pairs={{0,8},{1,33},{2,10},{3,35},{4,12},{5,37},{6,14},{7,39},{8,0},{9,41... | collective-permute-start | bytes 393224 | tf_op jit(solution)/shard_map/ppermute | solution.py:216
  105.6 6.5 %collective-permute-start.31 = (f32[128,256]{1,0:T(8,128)S(1)}, f32[128,256]{1,0:T(8,128)S(1)}, u32[]{:S(2)}, u32[]{:S(2)}) collective-permute-start(f32[128,256]{1,0:T(8,128)S(1)} %add.51), channel_id=1, source_target_pairs={{0,16},{1,65},{2,18},{3,67},{4,20},{5,69},{6,22},{7,71},{8,24},{9,... | collective-permute-start | bytes 393224 | tf_op jit(solution)/shard_map/ppermute | solution.py:216
  112.1 7.0 %collective-permute-start.38 = (f32[128,256]{1,0:T(8,128)S(1)}, f32[128,256]{1,0:T(8,128)S(1)}, u32[]{:S(2)}, u32[]{:S(2)}) collective-permute-start(f32[128,256]{1,0:T(8,128)S(1)} %multiply_select_fusion), channel_id=1, source_target_pairs={{0,1},{1,0},{2,3},{3,2},{4,5},{5,4},{6,7},{7,6},{8,9},{9,8},{10,11... | collective-permute-start | bytes 393224 | tf_op jit(solution)/shard_map/ppermute | solution.py:228
  114.4 6.0 %collective-permute-start.36 = (f32[128,256]{1,0:T(8,128)S(1)}, f32[128,256]{1,0:T(8,128)S(1)}, u32[]{:S(2)}, u32[]{:S(2)}) collective-permute-start(f32[128,256]{1,0:T(8,128)S(1)} %multiply_select_fusion), channel_id=1, source_target_pairs={{0,6},{1,25},{2,4},{3,27},{4,2},{5,29},{6,0},{7,31},{8,14},{9,17},... | collective-permute-start | bytes 393224 | tf_op jit(solution)/shard_map/ppermute | solution.py:216
  117.8 3.8 %collective-permute-start.35 = (f32[128,256]{1,0:T(8,128)S(1)}, f32[128,256]{1,0:T(8,128)S(1)}, u32[]{:S(2)}, u32[]{:S(2)}) collective-permute-start(f32[128,256]{1,0:T(8,128)S(1)} %multiply_select_fusion), channel_id=1, source_target_pairs={{0,2},{1,9},{2,0},{3,11},{4,6},{5,13},{6,4},{7,15},{8,10},{9,1},{1... | collective-permute-start | bytes 393224 | tf_op jit(solution)/shard_map/ppermute | solution.py:216
  117.8 5.3 %collective-permute-start.34 = (f32[128,256]{1,0:T(8,128)S(1)}, f32[128,256]{1,0:T(8,128)S(1)}, u32[]{:S(2)}, u32[]{:S(2)}) collective-permute-start(f32[128,256]{1,0:T(8,128)S(1)} %multiply_select_fusion), channel_id=1, source_target_pairs={{0,4},{1,17},{2,6},{3,19},{4,0},{5,21},{6,2},{7,23},{8,12},{9,25},... | collective-permute-start | bytes 393224 | tf_op jit(solution)/shard_map/ppermute | solution.py:216
  123.2 3.4 %collective-permute-start.37 = (f32[128,256]{1,0:T(8,128)S(1)}, f32[128,256]{1,0:T(8,128)S(1)}, u32[]{:S(2)}, u32[]{:S(2)}) collective-permute-start(f32[128,256]{1,0:T(8,128)S(1)} %get-tuple-element.52), channel_id=1, source_target_pairs={{0,1},{1,0},{2,3},{3,2},{4,5},{5,4},{6,7},{7,6},{8,9},{9,8},{10,11... | collective-permute-start | bytes 393224 | tf_op jit(solution)/shard_map/ppermute | solution.py:228
  (7 other events, 15.2 us)

commit v3 on v2

v3 whole, which is shorter than its diff:
```python
import functools
import math

import jax
import jax.numpy as jnp
from jax import lax
from jax.experimental import pallas as pl
from jax.experimental.pallas import tpu as pltpu
from jax.sharding import PartitionSpec as P

BLOCKS = 128
EPS = 1e-06
AXES = ("row", "col", "depth")
LOAD_GROUP = 8
SWEEP_GROUP = 12
FINAL_GROUP = 4
MIB = 1024 * 1024


def scale_row(meta_ref, slots, t):
    return meta_ref[t], meta_ref[slots + t]


def fold(summed):
    return (lambda a, b: a + b) if summed else jnp.maximum


def tile_partials(values, row_vec, col_vec, want_row, want_col, summed):
    join = fold(summed)
    reduce = jnp.sum if summed else jnp.max
    row_halves = []
    col_acc = None
    for h in range(2):
        rows = slice(h * 128, (h + 1) * 128)
        left = jnp.abs(values[rows, 0:128])
        right = jnp.abs(values[rows, 128:256])
        if want_row:
            if col_vec is None:
                part = join(left, right)
            else:
                part = join(left * col_vec[:, 0:128], right * col_vec[:, 128:256])
            row_halves.append(reduce(part.T, axis=0, keepdims=True))
        if want_col:
            if row_vec is not None:
                factor = jnp.broadcast_to(row_vec[:, rows], (128, 128)).T
                left = left * factor
                right = right * factor
            both = [reduce(x.reshape(16, 8, 128), axis=0) for x in (left, right)]
            col_acc = both if col_acc is None else [join(a, b) for a, b in zip(col_acc, both)]
    row_out = jnp.concatenate(row_halves, axis=1) if want_row else None
    col_out = None
    if want_col:
        col_out = jnp.concatenate([reduce(a, axis=0, keepdims=True) for a in col_acc], axis=1)
    return row_out, col_out


def clear(*accs):
    for acc in accs:
        if acc is not None:
            acc[...] = jnp.zeros_like(acc)


def sweep(slots, group, meta_ref, tiles_ref, offset, row_ref, col_ref, row_acc, col_acc, summed, before=None):
    want_row, want_col = row_acc is not None, col_acc is not None
    join = fold(summed)
    held = tiles_ref.shape[0]
    group = math.gcd(held, group)
    count = jnp.clip(meta_ref[2 * slots] - offset, 0, held)

    def body(g, carry):
        found = []
        if before is not None:
            for k in range(group):
                before(g * group + k)
        for k in range(group):
            t = g * group + k
            row, col = meta_ref[offset + t], meta_ref[slots + offset + t]
            row_vec = None if row_ref is None else row_ref[pl.ds(row, 1), :]
            col_vec = None if col_ref is None else col_ref[pl.ds(col, 1), :]
            values = tiles_ref.at[t]
            row_out, col_out = tile_partials(values, row_vec, col_vec, want_row, want_col, summed)
            live = t < count
            if want_row:
                row_out = jnp.where(live, row_out, 0.0)
            if want_col:
                col_out = jnp.where(live, col_out, 0.0)
            found.append((row, col, row_out, col_out))
        for row, col, row_out, col_out in found:
            if want_row:
                row_acc[pl.ds(row, 1), :] = join(row_acc[pl.ds(row, 1), :], row_out)
            if want_col:
                col_acc[pl.ds(col, 1), :] = join(col_acc[pl.ds(col, 1), :], col_out)
        return carry

    lax.fori_loop(0, (count + group - 1) // group, body, 0)


def split(core, row_acc, col_acc, mine_ref, other_ref):
    first = core == 0
    mine_ref[...] = jnp.where(first, row_acc[...], col_acc[...])
    other_ref[...] = jnp.where(first, col_acc[...], row_acc[...])


def load_kernel(
    slots, half, meta_ref, hbm_ref, low_ref, high_ref, mine_ref, other_ref, first_ref, row_acc, col_acc, sem
):
    count = meta_ref[2 * slots]
    pieces = ((low_ref, 0), (high_ref, half))

    def copy(ref, offset, t):
        return pltpu.make_async_copy(hbm_ref.at[offset + t], ref.at[t], sem.at[offset + t])

    for ref, offset in pieces:

        def start(t, carry, ref=ref, offset=offset):
            copy(ref, offset, t).start()
            return carry

        lax.fori_loop(0, jnp.clip(count - offset, 0, half), start, 0)
    first_ref[...] = jnp.where(meta_ref[2 * slots + 1] == 0, jnp.ones_like(first_ref), 0.0)
    clear(row_acc, col_acc)
    for ref, offset in pieces:

        def before(t, ref=ref, offset=offset):
            @pl.when(t + offset < count)
            def _():
                copy(ref, offset, t).wait()

        sweep(slots, LOAD_GROUP, meta_ref, ref, offset, None, None, row_acc, col_acc, False, before)
    split(meta_ref[2 * slots + 1], row_acc, col_acc, mine_ref, other_ref)


def row_kernel(slots, half, meta_ref, low_ref, high_ref, s_ref, g_ref, part_ref, col_ref):
    first = meta_ref[2 * slots + 1] == 0
    col_ref[...] = jnp.where(first, g_ref[...], s_ref[...])
    clear(part_ref)
    for ref, offset in ((low_ref, 0), (high_ref, half)):
        sweep(slots, SWEEP_GROUP, meta_ref, ref, offset, None, col_ref, part_ref, None, False)


def col_kernel(slots, half, meta_ref, low_ref, high_ref, s_ref, g_ref, part_ref, row_ref):
    first = meta_ref[2 * slots + 1] == 0
    row_ref[...] = jnp.where(first, s_ref[...], g_ref[...])
    clear(part_ref)
    for ref, offset in ((low_ref, 0), (high_ref, half)):
        sweep(slots, SWEEP_GROUP, meta_ref, ref, offset, row_ref, None, None, part_ref, False)


def chip_kernel(
    slots, half, kinds, summed, meta_ref, twin_ref, low_ref, high_ref, twin_low_ref, twin_high_ref, s_ref, part_ref
):
    core = meta_ref[2 * slots + 1]
    pieces = (
        (meta_ref, low_ref, 0),
        (meta_ref, high_ref, half),
        (twin_ref, twin_low_ref, 0),
        (twin_ref, twin_high_ref, half),
    )
    for place, kind in enumerate(kinds):

        @pl.when(core == place)
        def _():
            if kind is None:
                part_ref[...] = s_ref[...]
                return
            clear(part_ref)
            for meta, ref, offset in pieces:
                if kind == "rows":
                    sweep(slots, SWEEP_GROUP, meta, ref, offset, None, s_ref, part_ref, None, summed)
                else:
                    sweep(slots, SWEEP_GROUP, meta, ref, offset, s_ref, None, None, part_ref, summed)


def final_kernel(slots, half, meta_ref, low_ref, high_ref, row_ref, col_ref, out_ref, row_out, col_out, done, sem):
    count = meta_ref[2 * slots]
    group = math.gcd(half, FINAL_GROUP)

    def copy(t):
        return pltpu.make_async_copy(done.at[t], out_ref.at[t], sem.at[t])

    for ref, offset in ((low_ref, 0), (high_ref, half)):

        def fill(g, carry, ref=ref, offset=offset):
            for k in range(group):
                t = g * group + k
                slot = offset + t
                live = slot < count
                row_vec = row_ref[pl.ds(meta_ref[slot], 1), :]
                col_vec = col_ref[pl.ds(meta_ref[slots + slot], 1), :]
                for h in range(2):
                    rows = slice(h * 128, (h + 1) * 128)
                    factor = jnp.broadcast_to(row_vec[:, rows], (128, 128)).T
                    for w in range(2):
                        cols = slice(w * 128, (w + 1) * 128)
                        scaled = ref[t, rows, cols] * factor * col_vec[:, cols]
                        done[slot, rows, cols] = jnp.where(live, scaled, 0.0)
            for k in range(group):
                copy(offset + g * group + k).start()
            return carry

        full = (jnp.clip(count - offset, 0, half) + group - 1) // group
        lax.fori_loop(0, full, fill, 0)

        def zero(slot, carry):
            done[slot] = jnp.zeros(done.shape[1:], jnp.float32)
            copy(slot).start()
            return carry

        lax.fori_loop(offset + full * group, offset + half, zero, 0)
    for vec_ref, flat in ((row_ref, row_out), (col_ref, col_out)):
        for w in range(2):
            flat[pl.ds(w, BLOCKS, 2), :] = vec_ref[:, w * 128 : (w + 1) * 128]

    def finish(t, carry):
        copy(t).wait()
        return carry

    lax.fori_loop(0, slots, finish, 0)


def shards(sizes, tiles, tile_rows, tile_cols, tile_count):
    zs, xs, ys = sizes
    values = tiles[0, 0]
    slots, size = values.shape[0], values.shape[1]
    core = lax.axis_index("depth")
    meta = jnp.concatenate(
        [tile_rows[0, 0], tile_cols[0, 0], tile_count[0, 0], core[None].astype(jnp.int32)]
    )

    smem = pl.BlockSpec(memory_space=pltpu.SMEM)
    vmem = pl.BlockSpec(memory_space=pltpu.VMEM)
    params = pltpu.CompilerParams(vmem_limit_bytes=8 * MIB)
    vec = jax.ShapeDtypeStruct((BLOCKS, size), jnp.float32)
    acc = pltpu.VMEM((BLOCKS, size), jnp.float32)
    half = slots // 2
    kept = pltpu.VMEM((half, size, size), jnp.float32)

    def spots(move):
        pairs = []
        for z in range(zs):
            for x in range(xs):
                for y in range(ys):
                    for d in range(2):
                        pairs.append((index(z, x, y, d), index(*move(z, x, y, d))))
        return pairs

    def index(z, x, y, d):
        return ((z * xs + x) * ys + y) * 2 + d

    steps = {
        "x": lambda z, x, y, d, s: (z, x ^ s, y, d),
        "y": lambda z, x, y, d, s: (z, x, y ^ s, d),
        "z": lambda z, x, y, d, s: (z ^ s, x, y, d),
    }

    def slot(v, first_axis, second_axis):
        parts = [v]
        for s in (2, 1, 3):
            def move(z, x, y, d, s=s):
                return steps[first_axis if d == 0 else second_axis](z, x, y, d, s)
            parts.append(lax.ppermute(v, AXES, spots(move)))
        return parts

    def top(parts):
        return jnp.maximum(jnp.maximum(parts[0], parts[1]), jnp.maximum(parts[2], parts[3]))

    def total(parts):
        return (parts[0] + parts[1]) + (parts[2] + parts[3])

    def next_factor(old, partial):
        return old * lax.rsqrt(old * partial + EPS)

    swap = lambda v: lax.ppermute(v, "depth", [(0, 1), (1, 0)])

    def pick(a, b):
        return jnp.where(is_first > 0.5, a, b)

    low, high, mine, other, is_first = pl.pallas_call(
        functools.partial(load_kernel, slots, half),
        out_shape=(kept, kept, vec, vec, vec),
        in_specs=[smem, pl.BlockSpec(memory_space=pltpu.HBM)],
        out_specs=(vmem,) * 5,
        scratch_shapes=[acc, acc, pltpu.SemaphoreType.DMA((slots,))],
        compiler_params=params,
        name="load",
    )(meta, pltpu.with_memory_space_constraint(values, pltpu.HBM))

    def stay(v):
        return pltpu.with_memory_space_constraint(v, pltpu.VMEM)

    def share(v, after):
        v, after = lax.optimization_barrier((v, after))
        return swap(v), after

    def own(kernel, name):
        def run(*args):
            return pl.pallas_call(
                functools.partial(kernel, slots, half),
                out_shape=(vec, vec),
                in_specs=[smem] + [vmem] * 4,
                out_specs=(vmem, vmem),
                compiler_params=params,
                name=name,
            )(meta, stay(low), stay(high), *args)
        return run

    def chip(kinds, summed, name, s):
        return pl.pallas_call(
            functools.partial(chip_kernel, slots, half, kinds, summed),
            out_shape=vec,
            in_specs=[smem, smem] + [vmem] * 5,
            out_specs=vmem,
            compiler_params=params,
            name=name,
        )(meta, twin, stay(low), stay(high), stay(twin_low), stay(twin_high), s)

    def late_swap(v, parts):
        return swap(lax.optimization_barrier((v, parts[1]))[0])

    twin = swap(meta)
    m = jnp.maximum(mine, swap(other))
    twin_low, m = share(low, m)
    u = top(slot(m, "x", "z"))
    s = pick(u, lax.rsqrt(u + EPS))
    twin_low, s = lax.optimization_barrier((twin_low, s))
    part, col_1 = own(row_kernel, "rows")(s, swap(s))
    m = pick(s, jnp.maximum(part, swap(part)))
    twin_high, m = share(high, m)
    u = top(slot(m, "y", "x"))
    s = pick(lax.rsqrt(u + EPS), u)
    twin_high, s = lax.optimization_barrier((twin_high, s))
    part, row_1 = own(col_kernel, "cols")(s, swap(s))
    m = pick(jnp.maximum(part, swap(part)), s)
    u = top(slot(m, "z", "y"))
    now_2 = next_factor(pick(col_1, row_1), u)

    parts = slot(chip(("rows", "cols"), False, "chip_both", now_2), "x", "z")
    old_2 = late_swap(now_2, parts)
    u = top(parts)
    s = pick(u, next_factor(old_2, u))
    col_3 = swap(s)
    u = top(slot(chip((None, "rows"), False, "chip_rows", s), "y", "x"))
    s = pick(next_factor(old_2, u), u)
    row_3 = swap(s)
    u = top(slot(chip(("cols", None), False, "chip_cols", s), "z", "y"))
    now_4 = next_factor(pick(col_3, row_3), u)
    parts = slot(chip(("rows", "cols"), True, "chip_sums", now_4), "x", "z")
    old_4 = late_swap(now_4, parts)
    u = total(parts)
    s = pick(u, next_factor(old_4, u))
    col_last = pick(swap(s), s)
    u = total(slot(s, "y", "x"))
    s = next_factor(old_4, u)
    row_last = pick(s, swap(s))

    flat = jax.ShapeDtypeStruct((2 * BLOCKS, size // 2), jnp.float32)
    scaled, row_out, col_out = pl.pallas_call(
        functools.partial(final_kernel, slots, half),
        out_shape=(jax.ShapeDtypeStruct((slots, size, size), jnp.float32), flat, flat),
        in_specs=[smem] + [vmem] * 4,
        out_specs=(pl.BlockSpec(memory_space=pltpu.HBM), vmem, vmem),
        scratch_shapes=[pltpu.VMEM((slots, size, size), jnp.float32), pltpu.SemaphoreType.DMA((slots,))],
        compiler_params=pltpu.CompilerParams(vmem_limit_bytes=16 * MIB),
        name="scaled",
    )(meta, stay(low), stay(high), row_last, col_last)
    return row_out.reshape(-1), col_out.reshape(-1), scaled[None, None]


def solution(mesh):
    zs, cs, ds = (mesh.shape[a] for a in AXES)
    xs = 4
    sizes = (zs, xs, cs // xs)
    in_specs = (
        P("row", "col", "depth", None, None),
        P("row", "col", "depth"),
        P("row", "col", "depth"),
        P("row", "col", "depth"),
    )
    out_specs = (P("row"), P("col"), P("row", "col", "depth", None, None))
    return jax.shard_map(
        functools.partial(shards, sizes), mesh=mesh, in_specs=in_specs, out_specs=out_specs, check_vma=False
    )
```

time: 133 us -> 118 us (0.89)
  waiting for transfers between devices: 46.5 us -> 29.7 us
  Pallas kernels: 19.7 us -> 21.9 us
    ppermute x24, waiting for transfers between devices: 32.7 us -> 21.6 us  [slot(): parts.append(lax.ppermute(v, AXES, spots(move)))]
    ppermute x15 -> x14, starting transfers between devices: 29.9 us -> 23 us  [shards(): swap = lambda v: lax.ppermute(v, 'depth', [(0, 1), (1, 0)])]
    ppermute x24, starting transfers between devices: 34.2 us -> 40.7 us  [slot(): parts.append(lax.ppermute(v, AXES, spots(move)))]
    ppermute x15 -> x14, waiting for transfers between devices: 13.8 us -> 8.12 us  [shards(): swap = lambda v: lax.ppermute(v, 'depth', [(0, 1), (1, 0)])]
    pallas_call x8, Pallas kernels: 19.7 us -> 21.9 us  [the longest x4 8.78 us: chip(): pl.pallas_call(functools.partial(chip_kernel, slots, half, kinds, summed)...]
  transfers between devices with their start and end apart: 39 -> 38, of which waited for: 36 -> 27; matrix products, arithmetic and copies ran while one was open for 0% -> 0% of each run, Pallas kernels for 0% -> 0%
where the time goes in v3:
time: 118 us
  starting transfers between devices  63.7 us (54%)
  waiting for transfers between devices  29.7 us (25%)
  Pallas kernels  21.9 us (19%)
  between operations  1.61 us (1%)
  other arithmetic  1.31 us (1%)
    ppermute x24, starting transfers between devices, slot(): parts.append(lax.ppermute(v, AXES, spots(move)))  40.7 us
    ppermute x14, starting transfers between devices, shards(): swap = lambda v: lax.ppermute(v, 'depth', [(0, 1), (1, 0)])  23 us
    ppermute x24, waiting for transfers between devices, slot(): parts.append(lax.ppermute(v, AXES, spots(move)))  21.6 us
    pallas_call x4, Pallas kernels, chip(): pl.pallas_call(functools.partial(chip_kernel, slots, half, kinds, summed)...  8.78 us
    ppermute x14, waiting for transfers between devices, shards(): swap = lambda v: lax.ppermute(v, 'depth', [(0, 1), (1, 0)])  8.12 us
    pallas_call x1, Pallas kernels, shards(): pl.pallas_call(functools.partial(final_kernel, slots, half), out_shape=(j...  6.4 us
    pallas_call x1, Pallas kernels, shards(): pl.pallas_call(functools.partial(load_kernel, slots, half), out_shape=(ke...  3.56 us
    pallas_call x2, Pallas kernels, run(): pl.pallas_call(functools.partial(kernel, slots, half), out_shape=(vec, ve...  3.12 us
  transfers between devices with their start and end apart: 38, of which 27 were waited for; matrix products, arithmetic and copies ran while one was open for 0% of the time, Pallas kernels for 0%

profile of v3, /device:TPU:1, one launch (start us, length us, event | category | flops | bytes accessed | tf_op | source)
XLA Modules:
  0.0 118.2 jit_solution(9661405068809118051)
XLA Ops:
  2.0 3.6 %load.1 = (f32[24,256,256]{2,1,0:T(8,128)S(1)}, f32[24,256,256]{2,1,0:T(8,128)S(1)}, f32[128,256]{1,0:T(8,128)S(1)}, f32[128,256]{1,0:T(8,128)S(1)}, f32[128,256]{1,0:T(8,128)S(1)}) custom-call(s32[98]{0:T(128)S(1)} %pad_add_fusion.meta_ref, f32[48,256,256]{2,1,0:T(8,128)} %bitcast.9), custom_call_target="tpu_custom_call" | custom-call | tf_op jit(solution)/shard_map/load/pallas_call | solution.py:278
  5.6 1.9 %collective-permute-start.1 = (f32[128,256]{1,0:T(8,128)S(1)}, f32[128,256]{1,0:T(8,128)S(1)}, u32[]{:S(2)}, u32[]{:S(2)}) collective-permute-start(f32[128,256]{1,0:T(8,128)S(1)} %get-tuple-element.29), channel_id=1, source_target_pairs={{0,1},{1,0},{2,3},{3,2},{4,5},{5,4},{6,7},{7,6},{8,9},{9,8},{10,11... | collective-permute-start | bytes 393224 | tf_op jit(solution)/shard_map/ppermute | solution.py:273
  9.0 3.4 %collective-permute-start.5 = (f32[128,256]{1,0:T(8,128)S(1)}, f32[128,256]{1,0:T(8,128)S(1)}, u32[]{:S(2)}, u32[]{:S(2)}) collective-permute-start(f32[128,256]{1,0:T(8,128)S(1)} %max.63), channel_id=1, source_target_pairs={{0,24},{1,97},{2,26},{3,99},{4,28},{5,101},{6,30},{7,103},{8,16},{... | collective-permute-start | bytes 393224 | tf_op jit(solution)/shard_map/ppermute | solution.py:261
  14.7 1.8 %collective-permute-done.4 = f32[128,256]{1,0:T(8,128)S(1)} collective-permute-done((f32[128,256]{1,0:T(8,128)S(1)}, f32[128,256]{1,0:T(8,128)S(1)}, u32[]{:S(2)}, u32[]{:S(2)}) %collective-permute-start.4) | collective-permute-done | bytes 131104 | tf_op jit(solution)/shard_map/ppermute | solution.py:261
  16.5 1.8 %collective-permute-done.3 = f32[128,256]{1,0:T(8,128)S(1)} collective-permute-done((f32[128,256]{1,0:T(8,128)S(1)}, f32[128,256]{1,0:T(8,128)S(1)}, u32[]{:S(2)}, u32[]{:S(2)}) %collective-permute-start.3) | collective-permute-done | bytes 131104 | tf_op jit(solution)/shard_map/ppermute | solution.py:261
  18.8 1.9 %collective-permute-start.6 = (f32[128,256]{1,0:T(8,128)S(1)}, f32[128,256]{1,0:T(8,128)S(1)}, u32[]{:S(2)}, u32[]{:S(2)}) collective-permute-start(f32[128,256]{1,0:T(8,128)S(1)} %get-tuple-element.33.s_ref), channel_id=1, source_target_pairs={{0,1},{1,0},{2,3},{3,2},{4,5},{5,4},{6,7},{7,6},{8,9},{9,8},{10,11... | collective-permute-start | bytes 393224 | tf_op jit(solution)/shard_map/ppermute | solution.py:273
  21.6 1.6 %rows.1 = (f32[128,256]{1,0:T(8,128)S(1)}, f32[128,256]{1,0:T(8,128)S(1)}) custom-call(s32[98]{0:T(128)S(1)} %pad_add_fusion.meta_ref, f32[24,256,256]{2,1,0:T(8,128)S(1)} %get-tuple-element.30.low_ref, f32[24,256,256]{2,1,0:T(8,128)S(1)} %get-tuple-element.35.high_ref, f32[128,256]{1,0:T(8,128)S(1)} %get-tuple-element.33.s_ref, ...), custom_call_target="tpu_custom_call" | custom-call | tf_op jit(solution)/shard_map/rows/pallas_call | solution.py:297
  25.1 4.1 %collective-permute-start.11 = (f32[128,256]{1,0:T(8,128)S(1)}, f32[128,256]{1,0:T(8,128)S(1)}, u32[]{:S(2)}, u32[]{:S(2)}) collective-permute-start(f32[128,256]{1,0:T(8,128)S(1)} %maximum_select_fusion.1), channel_id=1, source_target_pairs={{0,6},{1,25},{2,4},{3,27},{4,2},{5,29},{6,0},{7,31},{8,14},{9,17},... | collective-permute-start | bytes 393224 | tf_op jit(solution)/shard_map/ppermute | solution.py:261
  33.0 1.8 %collective-permute-done.9 = f32[128,256]{1,0:T(8,128)S(1)} collective-permute-done((f32[128,256]{1,0:T(8,128)S(1)}, f32[128,256]{1,0:T(8,128)S(1)}, u32[]{:S(2)}, u32[]{:S(2)}) %collective-permute-start.9) | collective-permute-done | bytes 131104 | tf_op jit(solution)/shard_map/ppermute | solution.py:261
  37.1 1.6 %cols.1 = (f32[128,256]{1,0:T(8,128)S(1)}, f32[128,256]{1,0:T(8,128)S(1)}) custom-call(s32[98]{0:T(128)S(1)} %pad_add_fusion.meta_ref, f32[24,256,256]{2,1,0:T(8,128)S(1)} %get-tuple-element.30.low_ref, f32[24,256,256]{2,1,0:T(8,128)S(1)} %get-tuple-element.35.high_ref, f32[128,256]{1,0:T(8,128)S(1)} %rsqrt_select_fusion.s_ref, ...), custom_call_target="tpu_custom_call" | custom-call | tf_op jit(solution)/shard_map/cols/pallas_call | solution.py:297
  40.8 3.2 %collective-permute-start.15 = (f32[128,256]{1,0:T(8,128)S(1)}, f32[128,256]{1,0:T(8,128)S(1)}, u32[]{:S(2)}, u32[]{:S(2)}) collective-permute-start(f32[128,256]{1,0:T(8,128)S(1)} %maximum_select_fusion), channel_id=1, source_target_pairs={{0,32},{1,3},{2,34},{3,1},{4,36},{5,7},{6,38},{7,5},{8,40},{9,11},... | collective-permute-start | bytes 393224 | tf_op jit(solution)/shard_map/ppermute | solution.py:261
  44.5 1.8 %collective-permute-start = (s32[98]{0:T(128)S(1)}, s32[98]{0:T(128)S(1)}, u32[]{:S(2)}, u32[]{:S(2)}) collective-permute-start(s32[98]{0:T(128)S(1)} %pad_add_fusion.meta_ref), channel_id=1, source_target_pairs={{0,1},{1,0},{2,3},{3,2},{4,5},{5,4},{6,7},{7,6},{8,9},{9,8},{10,11... | collective-permute-start | bytes 1184 | tf_op jit(solution)/shard_map/ppermute | solution.py:273
  46.6 3.0 %collective-permute-done.14 = f32[128,256]{1,0:T(8,128)S(1)} collective-permute-done((f32[128,256]{1,0:T(8,128)S(1)}, f32[128,256]{1,0:T(8,128)S(1)}, u32[]{:S(2)}, u32[]{:S(2)}) %collective-permute-start.14) | collective-permute-done | bytes 131104 | tf_op jit(solution)/shard_map/ppermute | solution.py:261
  49.7 2.8 %chip_both.1 = f32[128,256]{1,0:T(8,128)S(1)} custom-call(s32[98]{0:T(128)S(1)} %pad_add_fusion.meta_ref, s32[98]{0:T(128)S(1)} %collective-permute-done.twin_ref, f32[24,256,256]{2,1,0:T(8,128)S(1)} %get-tuple-element.30.low_ref, f32[24,256,256]{2,1,0:T(8,128)S(1)} %get-tuple-element.35.high_ref, f32[24,256,256]{2,1,0:T(8,128)S(1)} %collective-permute-done.2.twin_low_ref, ...), custom_call_target="tpu_custom_call" | custom-call | tf_op jit(solution)/shard_map/chip_both/pallas_call | solution.py:308
  52.5 3.3 %collective-permute-start.17 = (f32[128,256]{1,0:T(8,128)S(1)}, f32[128,256]{1,0:T(8,128)S(1)}, u32[]{:S(2)}, u32[]{:S(2)}) collective-permute-start(f32[128,256]{1,0:T(8,128)S(1)} %chip_both.1), channel_id=1, source_target_pairs={{0,16},{1,65},{2,18},{3,67},{4,20},{5,69},{6,22},{7,71},{8,24},{9,... | collective-permute-start | bytes 393224 | tf_op jit(solution)/shard_map/ppermute | solution.py:261
  55.7 2.0 %collective-permute-start.19 = (f32[128,256]{1,0:T(8,128)S(1)}, f32[128,256]{1,0:T(8,128)S(1)}, u32[]{:S(2)}, u32[]{:S(2)}) collective-permute-start(f32[128,256]{1,0:T(8,128)S(1)} %chip_both.1), channel_id=1, source_target_pairs={{0,24},{1,97},{2,26},{3,99},{4,28},{5,101},{6,30},{7,103},{8,16},{... | collective-permute-start | bytes 393224 | tf_op jit(solution)/shard_map/ppermute | solution.py:261
  58.1 3.2 %collective-permute-start.20 = (f32[128,256]{1,0:T(8,128)S(1)}, f32[128,256]{1,0:T(8,128)S(1)}, u32[]{:S(2)}, u32[]{:S(2)}) collective-permute-start(f32[128,256]{1,0:T(8,128)S(1)} %rsqrt_multiply_fusion.2.s_ref), channel_id=1, source_target_pairs={{0,1},{1,0},{2,3},{3,2},{4,5},{5,4},{6,7},{7,6},{8,9},{9,8},{10,11... | collective-permute-start | bytes 393224 | tf_op jit(solution)/shard_map/ppermute | solution.py:273
  62.4 2.6 %chip_rows.1 = f32[128,256]{1,0:T(8,128)S(1)} custom-call(s32[98]{0:T(128)S(1)} %pad_add_fusion.meta_ref, s32[98]{0:T(128)S(1)} %collective-permute-done.twin_ref, f32[24,256,256]{2,1,0:T(8,128)S(1)} %get-tuple-element.30.low_ref, f32[24,256,256]{2,1,0:T(8,128)S(1)} %get-tuple-element.35.high_ref, f32[24,256,256]{2,1,0:T(8,128)S(1)} %collective-permute-done.2.twin_low_ref, ...), custom_call_target="tpu_custom_call" | custom-call | tf_op jit(solution)/shard_map/chip_rows/pallas_call | solution.py:308
  65.0 4.1 %collective-permute-start.24 = (f32[128,256]{1,0:T(8,128)S(1)}, f32[128,256]{1,0:T(8,128)S(1)}, u32[]{:S(2)}, u32[]{:S(2)}) collective-permute-start(f32[128,256]{1,0:T(8,128)S(1)} %chip_rows.1), channel_id=1, source_target_pairs={{0,6},{1,25},{2,4},{3,27},{4,2},{5,29},{6,0},{7,31},{8,14},{9,17},... | collective-permute-start | bytes 393224 | tf_op jit(solution)/shard_map/ppermute | solution.py:261
  71.5 1.8 %collective-permute-done.23 = f32[128,256]{1,0:T(8,128)S(1)} collective-permute-done((f32[128,256]{1,0:T(8,128)S(1)}, f32[128,256]{1,0:T(8,128)S(1)}, u32[]{:S(2)}, u32[]{:S(2)}) %collective-permute-start.23) | collective-permute-done | bytes 131104 | tf_op jit(solution)/shard_map/ppermute | solution.py:261
  75.1 2.2 %collective-permute-start.28 = (f32[128,256]{1,0:T(8,128)S(1)}, f32[128,256]{1,0:T(8,128)S(1)}, u32[]{:S(2)}, u32[]{:S(2)}) collective-permute-start(f32[128,256]{1,0:T(8,128)S(1)} %chip_cols.1), channel_id=1, source_target_pairs={{0,96},{1,7},{2,98},{3,5},{4,100},{5,3},{6,102},{7,1},{8,104},{9,1... | collective-permute-start | bytes 393224 | tf_op jit(solution)/shard_map/ppermute | solution.py:261
  77.3 1.9 %collective-permute-start.27 = (f32[128,256]{1,0:T(8,128)S(1)}, f32[128,256]{1,0:T(8,128)S(1)}, u32[]{:S(2)}, u32[]{:S(2)}) collective-permute-start(f32[128,256]{1,0:T(8,128)S(1)} %chip_cols.1), channel_id=1, source_target_pairs={{0,32},{1,3},{2,34},{3,1},{4,36},{5,7},{6,38},{7,5},{8,40},{9,11},... | collective-permute-start | bytes 393224 | tf_op jit(solution)/shard_map/ppermute | solution.py:261
  79.7 3.4 %collective-permute-start.25 = (f32[128,256]{1,0:T(8,128)S(1)}, f32[128,256]{1,0:T(8,128)S(1)}, u32[]{:S(2)}, u32[]{:S(2)}) collective-permute-start(f32[128,256]{1,0:T(8,128)S(1)} %multiply_select_fusion.1.s_ref), channel_id=1, source_target_pairs={{0,1},{1,0},{2,3},{3,2},{4,5},{5,4},{6,7},{7,6},{8,9},{9,8},{10,11... | collective-permute-start | bytes 393224 | tf_op jit(solution)/shard_map/ppermute | solution.py:273
  84.5 2.8 %chip_sums.1 = f32[128,256]{1,0:T(8,128)S(1)} custom-call(s32[98]{0:T(128)S(1)} %pad_add_fusion.meta_ref, s32[98]{0:T(128)S(1)} %collective-permute-done.twin_ref, f32[24,256,256]{2,1,0:T(8,128)S(1)} %get-tuple-element.30.low_ref, f32[24,256,256]{2,1,0:T(8,128)S(1)} %get-tuple-element.35.high_ref, f32[24,256,256]{2,1,0:T(8,128)S(1)} %collective-permute-done.2.twin_low_ref, ...), custom_call_target="tpu_custom_call" | custom-call | tf_op jit(solution)/shard_map/chip_sums/pallas_call | solution.py:308
  87.4 1.6 %collective-permute-start.29 = (f32[128,256]{1,0:T(8,128)S(1)}, f32[128,256]{1,0:T(8,128)S(1)}, u32[]{:S(2)}, u32[]{:S(2)}) collective-permute-start(f32[128,256]{1,0:T(8,128)S(1)} %chip_sums.1), channel_id=1, source_target_pairs={{0,16},{1,65},{2,18},{3,67},{4,20},{5,69},{6,22},{7,71},{8,24},{9,... | collective-permute-start | bytes 393224 | tf_op jit(solution)/shard_map/ppermute | solution.py:261
  89.0 4.7 %collective-permute-start.32 = (f32[128,256]{1,0:T(8,128)S(1)}, f32[128,256]{1,0:T(8,128)S(1)}, u32[]{:S(2)}, u32[]{:S(2)}) collective-permute-start(f32[128,256]{1,0:T(8,128)S(1)} %chip_sums.1), channel_id=1, source_target_pairs={{0,24},{1,97},{2,26},{3,99},{4,28},{5,101},{6,30},{7,103},{8,16},{... | collective-permute-start | bytes 393224 | tf_op jit(solution)/shard_map/ppermute | solution.py:261
  93.7 4.3 %collective-permute-start.30 = (f32[128,256]{1,0:T(8,128)S(1)}, f32[128,256]{1,0:T(8,128)S(1)}, u32[]{:S(2)}, u32[]{:S(2)}) collective-permute-start(f32[128,256]{1,0:T(8,128)S(1)} %rsqrt_multiply_fusion.1.s_ref), channel_id=1, source_target_pairs={{0,1},{1,0},{2,3},{3,2},{4,5},{5,4},{6,7},{7,6},{8,9},{9,8},{10,11... | collective-permute-start | bytes 393224 | tf_op jit(solution)/shard_map/ppermute | solution.py:273
  99.0 2.3 %collective-permute-start.37 = (f32[128,256]{1,0:T(8,128)S(1)}, f32[128,256]{1,0:T(8,128)S(1)}, u32[]{:S(2)}, u32[]{:S(2)}) collective-permute-start(f32[128,256]{1,0:T(8,128)S(1)} %multiply_select_fusion), channel_id=1, source_target_pairs={{0,1},{1,0},{2,3},{3,2},{4,5},{5,4},{6,7},{7,6},{8,9},{9,8},{10,11... | collective-permute-start | bytes 393224 | tf_op jit(solution)/shard_map/ppermute | solution.py:273
  101.4 1.7 %collective-permute-start.35 = (f32[128,256]{1,0:T(8,128)S(1)}, f32[128,256]{1,0:T(8,128)S(1)}, u32[]{:S(2)}, u32[]{:S(2)}) collective-permute-start(f32[128,256]{1,0:T(8,128)S(1)} %multiply_select_fusion), channel_id=1, source_target_pairs={{0,6},{1,25},{2,4},{3,27},{4,2},{5,29},{6,0},{7,31},{8,14},{9,17},... | collective-permute-start | bytes 393224 | tf_op jit(solution)/shard_map/ppermute | solution.py:261
  103.1 2.1 %collective-permute-start.33 = (f32[128,256]{1,0:T(8,128)S(1)}, f32[128,256]{1,0:T(8,128)S(1)}, u32[]{:S(2)}, u32[]{:S(2)}) collective-permute-start(f32[128,256]{1,0:T(8,128)S(1)} %multiply_select_fusion), channel_id=1, source_target_pairs={{0,4},{1,17},{2,6},{3,19},{4,0},{5,21},{6,2},{7,23},{8,12},{9,25},... | collective-permute-start | bytes 393224 | tf_op jit(solution)/shard_map/ppermute | solution.py:261
  107.2 2.1 %collective-permute-done.33 = f32[128,256]{1,0:T(8,128)S(1)} collective-permute-done((f32[128,256]{1,0:T(8,128)S(1)}, f32[128,256]{1,0:T(8,128)S(1)}, u32[]{:S(2)}, u32[]{:S(2)}) %collective-permute-start.33) | collective-permute-done | bytes 131104 | tf_op jit(solution)/shard_map/ppermute | solution.py:261
  111.7 6.4 %scaled.1 = (f32[48,256,256]{2,1,0:T(8,128)}, f32[256,128]{1,0:T(8,128)}, f32[256,128]{1,0:T(8,128)}) custom-call(s32[98]{0:T(128)S(1)} %pad_add_fusion.meta_ref, f32[24,256,256]{2,1,0:T(8,128)S(1)} %get-tuple-element.30.low_ref, f32[24,256,256]{2,1,0:T(8,128)S(1)} %get-tuple-element.35.high_ref, f32[128,256]{1,0:T(8,128)S(1)} %select_n.43.row_ref, ...), custom_call_target="tpu_custom_call" | custom-call | tf_op jit(solution)/shard_map/scaled/pallas_call | solution.py:357
  (65 shorter events, 30.1 us)
Async XLA Ops:
  8.5 10.2 %collective-permute-start.2 = (f32[24,256,256]{2,1,0:T(8,128)S(1)}, f32[24,256,256]{2,1,0:T(8,128)S(1)}, u32[]{:S(2)}, u32[]{:S(2)}) collective-permute-start(f32[24,256,256]{2,1,0:T(8,128)S(1)} %get-tuple-element.30.low_ref), channel_id=1, source_target_pairs={{0,1},{1,0},{2,3},{3,2},{4,5},{5,4},{6,7},{7,6},{8,9},{9,8},{10,11... | collective-permute-start | bytes 18874376 | tf_op jit(solution)/shard_map/ppermute | solution.py:273
  9.0 5.8 %collective-permute-start.5 = (f32[128,256]{1,0:T(8,128)S(1)}, f32[128,256]{1,0:T(8,128)S(1)}, u32[]{:S(2)}, u32[]{:S(2)}) collective-permute-start(f32[128,256]{1,0:T(8,128)S(1)} %max.63), channel_id=1, source_target_pairs={{0,24},{1,97},{2,26},{3,99},{4,28},{5,101},{6,30},{7,103},{8,16},{... | collective-permute-start | bytes 393224 | tf_op jit(solution)/shard_map/ppermute | solution.py:261
  12.4 4.1 %collective-permute-start.4 = (f32[128,256]{1,0:T(8,128)S(1)}, f32[128,256]{1,0:T(8,128)S(1)}, u32[]{:S(2)}, u32[]{:S(2)}) collective-permute-start(f32[128,256]{1,0:T(8,128)S(1)} %max.63), channel_id=1, source_target_pairs={{0,8},{1,33},{2,10},{3,35},{4,12},{5,37},{6,14},{7,39},{8,0},{9,41... | collective-permute-start | bytes 393224 | tf_op jit(solution)/shard_map/ppermute | solution.py:261
  13.0 5.3 %collective-permute-start.3 = (f32[128,256]{1,0:T(8,128)S(1)}, f32[128,256]{1,0:T(8,128)S(1)}, u32[]{:S(2)}, u32[]{:S(2)}) collective-permute-start(f32[128,256]{1,0:T(8,128)S(1)} %max.63), channel_id=1, source_target_pairs={{0,16},{1,65},{2,18},{3,67},{4,20},{5,69},{6,22},{7,71},{8,24},{9,... | collective-permute-start | bytes 393224 | tf_op jit(solution)/shard_map/ppermute | solution.py:261
  24.7 10.2 %collective-permute-start.8 = (f32[24,256,256]{2,1,0:T(8,128)S(1)}, f32[24,256,256]{2,1,0:T(8,128)S(1)}, u32[]{:S(2)}, u32[]{:S(2)}) collective-permute-start(f32[24,256,256]{2,1,0:T(8,128)S(1)} %get-tuple-element.35.high_ref), channel_id=1, source_target_pairs={{0,1},{1,0},{2,3},{3,2},{4,5},{5,4},{6,7},{7,6},{8,9},{9,8},{10,11... | collective-permute-start | bytes 18874376 | tf_op jit(solution)/shard_map/ppermute | solution.py:273
  25.1 6.4 %collective-permute-start.11 = (f32[128,256]{1,0:T(8,128)S(1)}, f32[128,256]{1,0:T(8,128)S(1)}, u32[]{:S(2)}, u32[]{:S(2)}) collective-permute-start(f32[128,256]{1,0:T(8,128)S(1)} %maximum_select_fusion.1), channel_id=1, source_target_pairs={{0,6},{1,25},{2,4},{3,27},{4,2},{5,29},{6,0},{7,31},{8,14},{9,17},... | collective-permute-start | bytes 393224 | tf_op jit(solution)/shard_map/ppermute | solution.py:261
  29.2 3.8 %collective-permute-start.10 = (f32[128,256]{1,0:T(8,128)S(1)}, f32[128,256]{1,0:T(8,128)S(1)}, u32[]{:S(2)}, u32[]{:S(2)}) collective-permute-start(f32[128,256]{1,0:T(8,128)S(1)} %maximum_select_fusion.1), channel_id=1, source_target_pairs={{0,2},{1,9},{2,0},{3,11},{4,6},{5,13},{6,4},{7,15},{8,10},{9,1},{1... | collective-permute-start | bytes 393224 | tf_op jit(solution)/shard_map/ppermute | solution.py:261
  29.2 5.6 %collective-permute-start.9 = (f32[128,256]{1,0:T(8,128)S(1)}, f32[128,256]{1,0:T(8,128)S(1)}, u32[]{:S(2)}, u32[]{:S(2)}) collective-permute-start(f32[128,256]{1,0:T(8,128)S(1)} %maximum_select_fusion.1), channel_id=1, source_target_pairs={{0,4},{1,17},{2,6},{3,19},{4,0},{5,21},{6,2},{7,23},{8,12},{9,25},... | collective-permute-start | bytes 393224 | tf_op jit(solution)/shard_map/ppermute | solution.py:261
  40.1 6.2 %collective-permute-start.16 = (f32[128,256]{1,0:T(8,128)S(1)}, f32[128,256]{1,0:T(8,128)S(1)}, u32[]{:S(2)}, u32[]{:S(2)}) collective-permute-start(f32[128,256]{1,0:T(8,128)S(1)} %maximum_select_fusion), channel_id=1, source_target_pairs={{0,96},{1,7},{2,98},{3,5},{4,100},{5,3},{6,102},{7,1},{8,104},{9,1... | collective-permute-start | bytes 393224 | tf_op jit(solution)/shard_map/ppermute | solution.py:261
  40.8 5.8 %collective-permute-start.15 = (f32[128,256]{1,0:T(8,128)S(1)}, f32[128,256]{1,0:T(8,128)S(1)}, u32[]{:S(2)}, u32[]{:S(2)}) collective-permute-start(f32[128,256]{1,0:T(8,128)S(1)} %maximum_select_fusion), channel_id=1, source_target_pairs={{0,32},{1,3},{2,34},{3,1},{4,36},{5,7},{6,38},{7,5},{8,40},{9,11},... | collective-permute-start | bytes 393224 | tf_op jit(solution)/shard_map/ppermute | solution.py:261
  44.0 5.6 %collective-permute-start.14 = (f32[128,256]{1,0:T(8,128)S(1)}, f32[128,256]{1,0:T(8,128)S(1)}, u32[]{:S(2)}, u32[]{:S(2)}) collective-permute-start(f32[128,256]{1,0:T(8,128)S(1)} %maximum_select_fusion), channel_id=1, source_target_pairs={{0,64},{1,5},{2,66},{3,7},{4,68},{5,1},{6,70},{7,3},{8,72},{9,13},... | collective-permute-start | bytes 393224 | tf_op jit(solution)/shard_map/ppermute | solution.py:261
  44.5 5.2 %collective-permute-start = (s32[98]{0:T(128)S(1)}, s32[98]{0:T(128)S(1)}, u32[]{:S(2)}, u32[]{:S(2)}) collective-permute-start(s32[98]{0:T(128)S(1)} %pad_add_fusion.meta_ref), channel_id=1, source_target_pairs={{0,1},{1,0},{2,3},{3,2},{4,5},{5,4},{6,7},{7,6},{8,9},{9,8},{10,11... | collective-permute-start | bytes 1184 | tf_op jit(solution)/shard_map/ppermute | solution.py:273
  52.5 5.6 %collective-permute-start.17 = (f32[128,256]{1,0:T(8,128)S(1)}, f32[128,256]{1,0:T(8,128)S(1)}, u32[]{:S(2)}, u32[]{:S(2)}) collective-permute-start(f32[128,256]{1,0:T(8,128)S(1)} %chip_both.1), channel_id=1, source_target_pairs={{0,16},{1,65},{2,18},{3,67},{4,20},{5,69},{6,22},{7,71},{8,24},{9,... | collective-permute-start | bytes 393224 | tf_op jit(solution)/shard_map/ppermute | solution.py:261
  55.7 5.6 %collective-permute-start.19 = (f32[128,256]{1,0:T(8,128)S(1)}, f32[128,256]{1,0:T(8,128)S(1)}, u32[]{:S(2)}, u32[]{:S(2)}) collective-permute-start(f32[128,256]{1,0:T(8,128)S(1)} %chip_both.1), channel_id=1, source_target_pairs={{0,24},{1,97},{2,26},{3,99},{4,28},{5,101},{6,30},{7,103},{8,16},{... | collective-permute-start | bytes 393224 | tf_op jit(solution)/shard_map/ppermute | solution.py:261
  57.8 3.8 %collective-permute-start.18 = (f32[128,256]{1,0:T(8,128)S(1)}, f32[128,256]{1,0:T(8,128)S(1)}, u32[]{:S(2)}, u32[]{:S(2)}) collective-permute-start(f32[128,256]{1,0:T(8,128)S(1)} %chip_both.1), channel_id=1, source_target_pairs={{0,8},{1,33},{2,10},{3,35},{4,12},{5,37},{6,14},{7,39},{8,0},{9,41... | collective-permute-start | bytes 393224 | tf_op jit(solution)/shard_map/ppermute | solution.py:261
  58.1 4.2 %collective-permute-start.20 = (f32[128,256]{1,0:T(8,128)S(1)}, f32[128,256]{1,0:T(8,128)S(1)}, u32[]{:S(2)}, u32[]{:S(2)}) collective-permute-start(f32[128,256]{1,0:T(8,128)S(1)} %rsqrt_multiply_fusion.2.s_ref), channel_id=1, source_target_pairs={{0,1},{1,0},{2,3},{3,2},{4,5},{5,4},{6,7},{7,6},{8,9},{9,8},{10,11... | collective-permute-start | bytes 393224 | tf_op jit(solution)/shard_map/ppermute | solution.py:273
  65.0 6.5 %collective-permute-start.24 = (f32[128,256]{1,0:T(8,128)S(1)}, f32[128,256]{1,0:T(8,128)S(1)}, u32[]{:S(2)}, u32[]{:S(2)}) collective-permute-start(f32[128,256]{1,0:T(8,128)S(1)} %chip_rows.1), channel_id=1, source_target_pairs={{0,6},{1,25},{2,4},{3,27},{4,2},{5,29},{6,0},{7,31},{8,14},{9,17},... | collective-permute-start | bytes 393224 | tf_op jit(solution)/shard_map/ppermute | solution.py:261
  69.1 4.1 %collective-permute-start.23 = (f32[128,256]{1,0:T(8,128)S(1)}, f32[128,256]{1,0:T(8,128)S(1)}, u32[]{:S(2)}, u32[]{:S(2)}) collective-permute-start(f32[128,256]{1,0:T(8,128)S(1)} %chip_rows.1), channel_id=1, source_target_pairs={{0,2},{1,9},{2,0},{3,11},{4,6},{5,13},{6,4},{7,15},{8,10},{9,1},{1... | collective-permute-start | bytes 393224 | tf_op jit(solution)/shard_map/ppermute | solution.py:261
  69.1 5.3 %collective-permute-start.22 = (f32[128,256]{1,0:T(8,128)S(1)}, f32[128,256]{1,0:T(8,128)S(1)}, u32[]{:S(2)}, u32[]{:S(2)}) collective-permute-start(f32[128,256]{1,0:T(8,128)S(1)} %chip_rows.1), channel_id=1, source_target_pairs={{0,4},{1,17},{2,6},{3,19},{4,0},{5,21},{6,2},{7,23},{8,12},{9,25},... | collective-permute-start | bytes 393224 | tf_op jit(solution)/shard_map/ppermute | solution.py:261
  70.4 12.7 %collective-permute-start.21 = (f32[128,256]{1,0:T(8,128)S(1)}, f32[128,256]{1,0:T(8,128)S(1)}, u32[]{:S(2)}, u32[]{:S(2)}) collective-permute-start(f32[128,256]{1,0:T(8,128)S(1)} %multiply_select_fusion.2.s_ref), channel_id=1, source_target_pairs={{0,1},{1,0},{2,3},{3,2},{4,5},{5,4},{6,7},{7,6},{8,9},{9,8},{10,11... | collective-permute-start | bytes 393224 | tf_op jit(solution)/shard_map/ppermute | solution.py:273
  75.1 8.0 %collective-permute-start.28 = (f32[128,256]{1,0:T(8,128)S(1)}, f32[128,256]{1,0:T(8,128)S(1)}, u32[]{:S(2)}, u32[]{:S(2)}) collective-permute-start(f32[128,256]{1,0:T(8,128)S(1)} %chip_cols.1), channel_id=1, source_target_pairs={{0,96},{1,7},{2,98},{3,5},{4,100},{5,3},{6,102},{7,1},{8,104},{9,1... | collective-permute-start | bytes 393224 | tf_op jit(solution)/shard_map/ppermute | solution.py:261
  77.3 5.8 %collective-permute-start.27 = (f32[128,256]{1,0:T(8,128)S(1)}, f32[128,256]{1,0:T(8,128)S(1)}, u32[]{:S(2)}, u32[]{:S(2)}) collective-permute-start(f32[128,256]{1,0:T(8,128)S(1)} %chip_cols.1), channel_id=1, source_target_pairs={{0,32},{1,3},{2,34},{3,1},{4,36},{5,7},{6,38},{7,5},{8,40},{9,11},... | collective-permute-start | bytes 393224 | tf_op jit(solution)/shard_map/ppermute | solution.py:261
  79.2 5.3 %collective-permute-start.26 = (f32[128,256]{1,0:T(8,128)S(1)}, f32[128,256]{1,0:T(8,128)S(1)}, u32[]{:S(2)}, u32[]{:S(2)}) collective-permute-start(f32[128,256]{1,0:T(8,128)S(1)} %chip_cols.1), channel_id=1, source_target_pairs={{0,64},{1,5},{2,66},{3,7},{4,68},{5,1},{6,70},{7,3},{8,72},{9,13},... | collective-permute-start | bytes 393224 | tf_op jit(solution)/shard_map/ppermute | solution.py:261
  79.7 4.8 %collective-permute-start.25 = (f32[128,256]{1,0:T(8,128)S(1)}, f32[128,256]{1,0:T(8,128)S(1)}, u32[]{:S(2)}, u32[]{:S(2)}) collective-permute-start(f32[128,256]{1,0:T(8,128)S(1)} %multiply_select_fusion.1.s_ref), channel_id=1, source_target_pairs={{0,1},{1,0},{2,3},{3,2},{4,5},{5,4},{6,7},{7,6},{8,9},{9,8},{10,11... | collective-permute-start | bytes 393224 | tf_op jit(solution)/shard_map/ppermute | solution.py:273
  87.4 6.3 %collective-permute-start.29 = (f32[128,256]{1,0:T(8,128)S(1)}, f32[128,256]{1,0:T(8,128)S(1)}, u32[]{:S(2)}, u32[]{:S(2)}) collective-permute-start(f32[128,256]{1,0:T(8,128)S(1)} %chip_sums.1), channel_id=1, source_target_pairs={{0,16},{1,65},{2,18},{3,67},{4,20},{5,69},{6,22},{7,71},{8,24},{9,... | collective-permute-start | bytes 393224 | tf_op jit(solution)/shard_map/ppermute | solution.py:261
  89.0 9.0 %collective-permute-start.32 = (f32[128,256]{1,0:T(8,128)S(1)}, f32[128,256]{1,0:T(8,128)S(1)}, u32[]{:S(2)}, u32[]{:S(2)}) collective-permute-start(f32[128,256]{1,0:T(8,128)S(1)} %chip_sums.1), channel_id=1, source_target_pairs={{0,24},{1,97},{2,26},{3,99},{4,28},{5,101},{6,30},{7,103},{8,16},{... | collective-permute-start | bytes 393224 | tf_op jit(solution)/shard_map/ppermute | solution.py:261
  93.7 4.3 %collective-permute-start.31 = (f32[128,256]{1,0:T(8,128)S(1)}, f32[128,256]{1,0:T(8,128)S(1)}, u32[]{:S(2)}, u32[]{:S(2)}) collective-permute-start(f32[128,256]{1,0:T(8,128)S(1)} %chip_sums.1), channel_id=1, source_target_pairs={{0,8},{1,33},{2,10},{3,35},{4,12},{5,37},{6,14},{7,39},{8,0},{9,41... | collective-permute-start | bytes 393224 | tf_op jit(solution)/shard_map/ppermute | solution.py:261
  93.7 5.2 %collective-permute-start.30 = (f32[128,256]{1,0:T(8,128)S(1)}, f32[128,256]{1,0:T(8,128)S(1)}, u32[]{:S(2)}, u32[]{:S(2)}) collective-permute-start(f32[128,256]{1,0:T(8,128)S(1)} %rsqrt_multiply_fusion.1.s_ref), channel_id=1, source_target_pairs={{0,1},{1,0},{2,3},{3,2},{4,5},{5,4},{6,7},{7,6},{8,9},{9,8},{10,11... | collective-permute-start | bytes 393224 | tf_op jit(solution)/shard_map/ppermute | solution.py:273
  99.0 6.2 %collective-permute-start.37 = (f32[128,256]{1,0:T(8,128)S(1)}, f32[128,256]{1,0:T(8,128)S(1)}, u32[]{:S(2)}, u32[]{:S(2)}) collective-permute-start(f32[128,256]{1,0:T(8,128)S(1)} %multiply_select_fusion), channel_id=1, source_target_pairs={{0,1},{1,0},{2,3},{3,2},{4,5},{5,4},{6,7},{7,6},{8,9},{9,8},{10,11... | collective-permute-start | bytes 393224 | tf_op jit(solution)/shard_map/ppermute | solution.py:273
  101.4 5.3 %collective-permute-start.35 = (f32[128,256]{1,0:T(8,128)S(1)}, f32[128,256]{1,0:T(8,128)S(1)}, u32[]{:S(2)}, u32[]{:S(2)}) collective-permute-start(f32[128,256]{1,0:T(8,128)S(1)} %multiply_select_fusion), channel_id=1, source_target_pairs={{0,6},{1,25},{2,4},{3,27},{4,2},{5,29},{6,0},{7,31},{8,14},{9,17},... | collective-permute-start | bytes 393224 | tf_op jit(solution)/shard_map/ppermute | solution.py:261
  103.1 4.1 %collective-permute-start.34 = (f32[128,256]{1,0:T(8,128)S(1)}, f32[128,256]{1,0:T(8,128)S(1)}, u32[]{:S(2)}, u32[]{:S(2)}) collective-permute-start(f32[128,256]{1,0:T(8,128)S(1)} %multiply_select_fusion), channel_id=1, source_target_pairs={{0,2},{1,9},{2,0},{3,11},{4,6},{5,13},{6,4},{7,15},{8,10},{9,1},{1... | collective-permute-start | bytes 393224 | tf_op jit(solution)/shard_map/ppermute | solution.py:261
  103.1 6.2 %collective-permute-start.33 = (f32[128,256]{1,0:T(8,128)S(1)}, f32[128,256]{1,0:T(8,128)S(1)}, u32[]{:S(2)}, u32[]{:S(2)}) collective-permute-start(f32[128,256]{1,0:T(8,128)S(1)} %multiply_select_fusion), channel_id=1, source_target_pairs={{0,4},{1,17},{2,6},{3,19},{4,0},{5,21},{6,2},{7,23},{8,12},{9,25},... | collective-permute-start | bytes 393224 | tf_op jit(solution)/shard_map/ppermute | solution.py:261
  (6 other events, 13.1 us)

commit v4 on v3

--- a/solution.py
+++ b/solution.py
@@ -12,8 +12,11 @@
 EPS = 1e-06
 AXES = ("row", "col", "depth")
 LOAD_GROUP = 8
-SWEEP_GROUP = 12
-FINAL_GROUP = 4
+SWEEP_GROUP = 16
+CHIP_GROUP = 8
+COPY_GROUP = 4
+PIECES = 3
+ORDER = (1, 3, 2)
 MIB = 1024 * 1024
 
 
@@ -60,7 +63,7 @@
             acc[...] = jnp.zeros_like(acc)
 
 
-def sweep(slots, group, meta_ref, tiles_ref, offset, row_ref, col_ref, row_acc, col_acc, summed, before=None):
+def sweep(slots, group, meta_ref, tiles_ref, offset, row_ref, col_ref, row_acc, col_acc, summed, before=None, step=1):
     want_row, want_col = row_acc is not None, col_acc is not None
     join = fold(summed)
     held = tiles_ref.shape[0]
@@ -70,7 +73,7 @@
     def body(g, carry):
         found = []
         if before is not None:
-            for k in range(group):
+            for k in range(0, group, step):
                 before(g * group + k)
         for k in range(group):
             t = g * group + k
@@ -101,61 +104,58 @@
     other_ref[...] = jnp.where(first, col_acc[...], row_acc[...])
 
 
-def load_kernel(
-    slots, half, meta_ref, hbm_ref, low_ref, high_ref, mine_ref, other_ref, first_ref, row_acc, col_acc, sem
-):
+def load_kernel(slots, size, meta_ref, hbm_ref, *refs):
+    held, (mine_ref, other_ref, first_ref, row_acc, col_acc, sem) = refs[:PIECES], refs[PIECES:]
     count = meta_ref[2 * slots]
-    pieces = ((low_ref, 0), (high_ref, half))
-
-    def copy(ref, offset, t):
-        return pltpu.make_async_copy(hbm_ref.at[offset + t], ref.at[t], sem.at[offset + t])
-
-    for ref, offset in pieces:
-
-        def start(t, carry, ref=ref, offset=offset):
-            copy(ref, offset, t).start()
+    step = math.gcd(size, COPY_GROUP)
+    group = math.gcd(size, LOAD_GROUP)
+
+    def copy(ref, offset, g):
+        return pltpu.make_async_copy(
+            hbm_ref.at[pl.ds(offset + g * step, step)], ref.at[pl.ds(g * step, step)], sem.at[offset // step + g]
+        )
+
+    for place, ref in enumerate(held):
+
+        def start(g, carry, ref=ref, offset=place * size):
+            copy(ref, offset, g).start()
             return carry
 
-        lax.fori_loop(0, jnp.clip(count - offset, 0, half), start, 0)
+        lax.fori_loop(0, (jnp.clip(count - place * size, 0, size) + step - 1) // step, start, 0)
     first_ref[...] = jnp.where(meta_ref[2 * slots + 1] == 0, jnp.ones_like(first_ref), 0.0)
     clear(row_acc, col_acc)
-    for ref, offset in pieces:
-
-        def before(t, ref=ref, offset=offset):
-            @pl.when(t + offset < count)
+    for place, ref in enumerate(held):
+
+        def before(t, ref=ref, offset=place * size):
+            @pl.when(offset + t < count)
             def _():
-                copy(ref, offset, t).wait()
-
-        sweep(slots, LOAD_GROUP, meta_ref, ref, offset, None, None, row_acc, col_acc, False, before)
+                copy(ref, offset, t // step).wait()
+
+        sweep(slots, group, meta_ref, ref, place * size, None, None, row_acc, col_acc, False, before, step)
     split(meta_ref[2 * slots + 1], row_acc, col_acc, mine_ref, other_ref)
 
 
-def row_kernel(slots, half, meta_ref, low_ref, high_ref, s_ref, g_ref, part_ref, col_ref):
+def row_kernel(slots, size, meta_ref, *refs):
+    held, (s_ref, g_ref, part_ref, col_ref) = refs[:PIECES], refs[PIECES:]
     first = meta_ref[2 * slots + 1] == 0
     col_ref[...] = jnp.where(first, g_ref[...], s_ref[...])
     clear(part_ref)
-    for ref, offset in ((low_ref, 0), (high_ref, half)):
-        sweep(slots, SWEEP_GROUP, meta_ref, ref, offset, None, col_ref, part_ref, None, False)
-
-
-def col_kernel(slots, half, meta_ref, low_ref, high_ref, s_ref, g_ref, part_ref, row_ref):
+    for place, ref in enumerate(held):
+        sweep(slots, SWEEP_GROUP, meta_ref, ref, place * size, None, col_ref, part_ref, None, False)
+
+
+def col_kernel(slots, size, meta_ref, *refs):
+    held, (s_ref, g_ref, part_ref, row_ref) = refs[:PIECES], refs[PIECES:]
     first = meta_ref[2 * slots + 1] == 0
     row_ref[...] = jnp.where(first, s_ref[...], g_ref[...])
     clear(part_ref)
-    for ref, offset in ((low_ref, 0), (high_ref, half)):
-        sweep(slots, SWEEP_GROUP, meta_ref, ref, offset, row_ref, None, None, part_ref, False)
-
-
-def chip_kernel(
-    slots, half, kinds, summed, meta_ref, twin_ref, low_ref, high_ref, twin_low_ref, twin_high_ref, s_ref, part_ref
-):
+    for place, ref in enumerate(held):
+        sweep(slots, SWEEP_GROUP, meta_ref, ref, place * size, row_ref, None, None, part_ref, False)
+
+
+def chip_kernel(slots, size, kinds, summed, meta_ref, twin_ref, *refs):
+    held, twins, (s_ref, part_ref) = refs[:PIECES], refs[PIECES : 2 * PIECES], refs[2 * PIECES :]
     core = meta_ref[2 * slots + 1]
-    pieces = (
-        (meta_ref, low_ref, 0),
-        (meta_ref, high_ref, half),
-        (twin_ref, twin_low_ref, 0),
-        (twin_ref, twin_high_ref, half),
-    )
     for place, kind in enumerate(kinds):
 
         @pl.when(core == place)
@@ -164,21 +164,25 @@
                 part_ref[...] = s_ref[...]
                 return
             clear(part_ref)
-            for meta, ref, offset in pieces:
-                if kind == "rows":
-                    sweep(slots, SWEEP_GROUP, meta, ref, offset, None, s_ref, part_ref, None, summed)
-                else:
-                    sweep(slots, SWEEP_GROUP, meta, ref, offset, s_ref, None, None, part_ref, summed)
-
-
-def final_kernel(slots, half, meta_ref, low_ref, high_ref, row_ref, col_ref, out_ref, row_out, col_out, done, sem):
+            for meta, pieces in ((meta_ref, held), (twin_ref, twins)):
+                for spot, ref in enumerate(pieces):
+                    if kind == "rows":
+                        sweep(slots, CHIP_GROUP, meta, ref, spot * size, None, s_ref, part_ref, None, summed)
+                    else:
+                        sweep(slots, CHIP_GROUP, meta, ref, spot * size, s_ref, None, None, part_ref, summed)
+
+
+def final_kernel(slots, size, meta_ref, *refs):
+    held, (row_ref, col_ref, out_ref, row_out, col_out, done, sem) = refs[:PIECES], refs[PIECES:]
     count = meta_ref[2 * slots]
-    group = math.gcd(half, FINAL_GROUP)
-
-    def copy(t):
-        return pltpu.make_async_copy(done.at[t], out_ref.at[t], sem.at[t])
-
-    for ref, offset in ((low_ref, 0), (high_ref, half)):
+    group = math.gcd(size, COPY_GROUP)
+
+    def copy(g):
+        span = pl.ds(g * group, group)
+        return pltpu.make_async_copy(done.at[span], out_ref.at[span], sem.at[g])
+
+    for place, ref in enumerate(held):
+        offset = place * size
 
         def fill(g, carry, ref=ref, offset=offset):
             for k in range(group):
@@ -194,28 +198,27 @@
                         cols = slice(w * 128, (w + 1) * 128)
                         scaled = ref[t, rows, cols] * factor * col_vec[:, cols]
                         done[slot, rows, cols] = jnp.where(live, scaled, 0.0)
-            for k in range(group):
-                copy(offset + g * group + k).start()
+            copy(offset // group + g).start()
             return carry
 
-        full = (jnp.clip(count - offset, 0, half) + group - 1) // group
+        full = (jnp.clip(count - offset, 0, size) + group - 1) // group
         lax.fori_loop(0, full, fill, 0)
 
-        def zero(slot, carry):
-            done[slot] = jnp.zeros(done.shape[1:], jnp.float32)
-            copy(slot).start()
+        def zero(g, carry, offset=offset):
+            done[pl.ds(offset + g * group, group)] = jnp.zeros((group,) + done.shape[1:], jnp.float32)
+            copy(offset // group + g).start()
             return carry
 
-        lax.fori_loop(offset + full * group, offset + half, zero, 0)
+        lax.fori_loop(full, size // group, zero, 0)
     for vec_ref, flat in ((row_ref, row_out), (col_ref, col_out)):
         for w in range(2):
             flat[pl.ds(w, BLOCKS, 2), :] = vec_ref[:, w * 128 : (w + 1) * 128]
 
-    def finish(t, carry):
-        copy(t).wait()
+    def finish(g, carry):
+        copy(g).wait()
         return carry
 
-    lax.fori_loop(0, slots, finish, 0)
+    lax.fori_loop(0, slots // group, finish, 0)
 
 
 def shards(sizes, tiles, tile_rows, tile_cols, tile_count):
@@ -232,8 +235,8 @@
     params = pltpu.CompilerParams(vmem_limit_bytes=8 * MIB)
     vec = jax.ShapeDtypeStruct((BLOCKS, size), jnp.float32)
     acc = pltpu.VMEM((BLOCKS, size), jnp.float32)
-    half = slots // 2
-    kept = pltpu.VMEM((half, size, size), jnp.float32)
+    part_slots = slots // PIECES
+    kept = pltpu.VMEM((part_slots, size, size), jnp.float32)
 
     def spots(move):
         pairs = []
@@ -255,7 +258,7 @@
 
     def slot(v, first_axis, second_axis):
         parts = [v]
-        for s in (2, 1, 3):
+        for s in ORDER:
             def move(z, x, y, d, s=s):
                 return steps[first_axis if d == 0 else second_axis](z, x, y, d, s)
             parts.append(lax.ppermute(v, AXES, spots(move)))
@@ -275,62 +278,69 @@
     def pick(a, b):
         return jnp.where(is_first > 0.5, a, b)
 
-    low, high, mine, other, is_first = pl.pallas_call(
-        functools.partial(load_kernel, slots, half),
-        out_shape=(kept, kept, vec, vec, vec),
+    *held, mine, other, is_first = pl.pallas_call(
+        functools.partial(load_kernel, slots, part_slots),
+        out_shape=(kept,) * PIECES + (vec, vec, vec),
         in_specs=[smem, pl.BlockSpec(memory_space=pltpu.HBM)],
-        out_specs=(vmem,) * 5,
+        out_specs=(vmem,) * (PIECES + 3),
         scratch_shapes=[acc, acc, pltpu.SemaphoreType.DMA((slots,))],
         compiler_params=params,
         name="load",
     )(meta, pltpu.with_memory_space_constraint(values, pltpu.HBM))
 
-    def stay(v):
-        return pltpu.with_memory_space_constraint(v, pltpu.VMEM)
-
-    def share(v, after):
-        v, after = lax.optimization_barrier((v, after))
-        return swap(v), after
+    def stay(pieces):
+        return [pltpu.with_memory_space_constraint(v, pltpu.VMEM) for v in pieces]
+
+    twins = []
+
+    def share(after):
+        v, after = lax.optimization_barrier((held[len(twins)], after))
+        twins.append(swap(v))
+        return after
+
+    def shared(before):
+        twins[-1], before = lax.optimization_barrier((twins[-1], before))
+        return before
 
     def own(kernel, name):
         def run(*args):
             return pl.pallas_call(
-                functools.partial(kernel, slots, half),
+                functools.partial(kernel, slots, part_slots),
                 out_shape=(vec, vec),
-                in_specs=[smem] + [vmem] * 4,
+                in_specs=[smem] + [vmem] * (PIECES + 2),
                 out_specs=(vmem, vmem),
                 compiler_params=params,
                 name=name,
-            )(meta, stay(low), stay(high), *args)
+            )(meta, *stay(held), *args)
         return run
 
     def chip(kinds, summed, name, s):
         return pl.pallas_call(
-            functools.partial(chip_kernel, slots, half, kinds, summed),
+            functools.partial(chip_kernel, slots, part_slots, kinds, summed),
             out_shape=vec,
-            in_specs=[smem, smem] + [vmem] * 5,
+            in_specs=[smem, smem] + [vmem] * (2 * PIECES + 1),
             out_specs=vmem,
             compiler_params=params,
             name=name,
-        )(meta, twin, stay(low), stay(high), stay(twin_low), stay(twin_high), s)
+        )(meta, twin, *stay(held), *stay(twins), s)
 
     def late_swap(v, parts):
         return swap(lax.optimization_barrier((v, parts[1]))[0])
 
     twin = swap(meta)
     m = jnp.maximum(mine, swap(other))
-    twin_low, m = share(low, m)
+    m = share(m)
     u = top(slot(m, "x", "z"))
     s = pick(u, lax.rsqrt(u + EPS))
-    twin_low, s = lax.optimization_barrier((twin_low, s))
+    s = shared(s)
     part, col_1 = own(row_kernel, "rows")(s, swap(s))
     m = pick(s, jnp.maximum(part, swap(part)))
-    twin_high, m = share(high, m)
+    m = share(m)
     u = top(slot(m, "y", "x"))
     s = pick(lax.rsqrt(u + EPS), u)
-    twin_high, s = lax.optimization_barrier((twin_high, s))
+    s = shared(s)
     part, row_1 = own(col_kernel, "cols")(s, swap(s))
-    m = pick(jnp.maximum(part, swap(part)), s)
+    m = share(pick(jnp.maximum(part, swap(part)), s))
     u = top(slot(m, "z", "y"))
     now_2 = next_factor(pick(col_1, row_1), u)
 
@@ -355,14 +365,14 @@
 
     flat = jax.ShapeDtypeStruct((2 * BLOCKS, size // 2), jnp.float32)
     scaled, row_out, col_out = pl.pallas_call(
-        functools.partial(final_kernel, slots, half),
+        functools.partial(final_kernel, slots, part_slots),
         out_shape=(jax.ShapeDtypeStruct((slots, size, size), jnp.float32), flat, flat),
-        in_specs=[smem] + [vmem] * 4,
+        in_specs=[smem] + [vmem] * (PIECES + 2),
         out_specs=(pl.BlockSpec(memory_space=pltpu.HBM), vmem, vmem),
         scratch_shapes=[pltpu.VMEM((slots, size, size), jnp.float32), pltpu.SemaphoreType.DMA((slots,))],
         compiler_params=pltpu.CompilerParams(vmem_limit_bytes=16 * MIB),
         name="scaled",
-    )(meta, stay(low), stay(high), row_last, col_last)
+    )(meta, *stay(held), row_last, col_last)
     return row_out.reshape(-1), col_out.reshape(-1), scaled[None, None]
 
 

time: 118 us -> 114 us (0.966); the launches traced: 118 us -> 113 us
  starting transfers between devices: 63.7 us -> 54.9 us
  Pallas kernels: 21.9 us -> 25.9 us
    ppermute x24, starting transfers between devices: 40.7 us -> 27.1 us  [slot(): parts.append(lax.ppermute(v, AXES, spots(move)))]
    ppermute x14 -> x15, starting transfers between devices: 23 us -> 27.8 us  [shards(): swap = lambda v: lax.ppermute(v, 'depth', [(0, 1), (1, 0)])]
    pallas_call x8, Pallas kernels: 21.9 us -> 25.9 us  [the longest x4 11.7 us: chip(): pl.pallas_call(functools.partial(chip_kernel, slots, part_slots, kinds, s...]
    ppermute x14 -> x15, waiting for transfers between devices: 8.12 us -> 7.88 us  [shards(): swap = lambda v: lax.ppermute(v, 'depth', [(0, 1), (1, 0)])]
  transfers between devices with their start and end apart: 38 -> 39, of which waited for: 27 -> 22; matrix products, arithmetic and copies ran while one was open for 0% -> 0% of each run, Pallas kernels for 0% -> 0%
where the time goes in v4:
time: 114 us; the launch traced here: 113 us
  starting transfers between devices  54.9 us (48%)
  waiting for transfers between devices  29.1 us (26%)
  Pallas kernels  25.9 us (23%)
  between operations  1.63 us (1%)
  other arithmetic  1.36 us (1%)
    ppermute x15, starting transfers between devices, shards(): swap = lambda v: lax.ppermute(v, 'depth', [(0, 1), (1, 0)])  27.8 us
    ppermute x24, starting transfers between devices, slot(): parts.append(lax.ppermute(v, AXES, spots(move)))  27.1 us
    ppermute x24, waiting for transfers between devices, slot(): parts.append(lax.ppermute(v, AXES, spots(move)))  21.2 us
    pallas_call x4, Pallas kernels, chip(): pl.pallas_call(functools.partial(chip_kernel, slots, part_slots, kinds, s...  11.7 us
    ppermute x15, waiting for transfers between devices, shards(): swap = lambda v: lax.ppermute(v, 'depth', [(0, 1), (1, 0)])  7.88 us
    pallas_call x1, Pallas kernels, shards(): pl.pallas_call(functools.partial(final_kernel, slots, part_slots), out_sh...  6.45 us
    pallas_call x1, Pallas kernels, shards(): pl.pallas_call(functools.partial(load_kernel, slots, part_slots), out_sha...  4.01 us
    pallas_call x2, Pallas kernels, run(): pl.pallas_call(functools.partial(kernel, slots, part_slots), out_shape=(v...  3.67 us
  transfers between devices with their start and end apart: 39, of which 22 were waited for; matrix products, arithmetic and copies ran while one was open for 0% of the time, Pallas kernels for 0%

profile of v4, /device:TPU:1, one launch (start us, length us, event | category | flops | bytes accessed | tf_op | source)
XLA Modules:
  0.0 112.9 jit_solution(16589866674311185732)
XLA Ops:
  2.0 4.0 %load.1 = (f32[16,256,256]{2,1,0:T(8,128)S(1)}, f32[16,256,256]{2,1,0:T(8,128)S(1)}, f32[16,256,256]{2,1,0:T(8,128)S(1)}, f32[128,256]{1,0:T(8,128)S(1)}, f32[12...) custom-call(s32[98]{0:T(128)S(1)} %pad_add_fusion.meta_ref, f32[48,256,256]{2,1,0:T(8,128)} %bitcast.9), custom_call_target="tpu_custom_call" | custom-call | tf_op jit(solution)/shard_map/load/pallas_call | solution.py:281
  6.1 2.9 %collective-permute-start.1 = (f32[128,256]{1,0:T(8,128)S(1)}, f32[128,256]{1,0:T(8,128)S(1)}, u32[]{:S(2)}, u32[]{:S(2)}) collective-permute-start(f32[128,256]{1,0:T(8,128)S(1)} %get-tuple-element.33), channel_id=1, source_target_pairs={{0,1},{1,0},{2,3},{3,2},{4,5},{5,4},{6,7},{7,6},{8,9},{9,8},{10,11... | collective-permute-start | bytes 393224 | tf_op jit(solution)/shard_map/ppermute | solution.py:276
  10.4 2.0 %collective-permute-start.5 = (f32[128,256]{1,0:T(8,128)S(1)}, f32[128,256]{1,0:T(8,128)S(1)}, u32[]{:S(2)}, u32[]{:S(2)}) collective-permute-start(f32[128,256]{1,0:T(8,128)S(1)} %max.63), channel_id=1, source_target_pairs={{0,16},{1,65},{2,18},{3,67},{4,20},{5,69},{6,22},{7,71},{8,24},{9,... | collective-permute-start | bytes 393224 | tf_op jit(solution)/shard_map/ppermute | solution.py:264
  12.4 1.4 %collective-permute-start.4 = (f32[128,256]{1,0:T(8,128)S(1)}, f32[128,256]{1,0:T(8,128)S(1)}, u32[]{:S(2)}, u32[]{:S(2)}) collective-permute-start(f32[128,256]{1,0:T(8,128)S(1)} %max.63), channel_id=1, source_target_pairs={{0,24},{1,97},{2,26},{3,99},{4,28},{5,101},{6,30},{7,103},{8,16},{... | collective-permute-start | bytes 393224 | tf_op jit(solution)/shard_map/ppermute | solution.py:264
  14.2 1.8 %collective-permute-done.5 = f32[128,256]{1,0:T(8,128)S(1)} collective-permute-done((f32[128,256]{1,0:T(8,128)S(1)}, f32[128,256]{1,0:T(8,128)S(1)}, u32[]{:S(2)}, u32[]{:S(2)}) %collective-permute-start.5) | collective-permute-done | bytes 131104 | tf_op jit(solution)/shard_map/ppermute | solution.py:264
  16.0 1.7 %collective-permute-done.4 = f32[128,256]{1,0:T(8,128)S(1)} collective-permute-done((f32[128,256]{1,0:T(8,128)S(1)}, f32[128,256]{1,0:T(8,128)S(1)}, u32[]{:S(2)}, u32[]{:S(2)}) %collective-permute-start.4) | collective-permute-done | bytes 131104 | tf_op jit(solution)/shard_map/ppermute | solution.py:264
  19.7 1.8 %rows.1 = (f32[128,256]{1,0:T(8,128)S(1)}, f32[128,256]{1,0:T(8,128)S(1)}) custom-call(s32[98]{0:T(128)S(1)} %pad_add_fusion.meta_ref, f32[16,256,256]{2,1,0:T(8,128)S(1)} %get-tuple-element.34.refs_0_, f32[16,256,256]{2,1,0:T(8,128)S(1)} %get-tuple-element.39.refs_1_, f32[16,256,256]{2,1,0:T(8,128)S(1)} %get-tuple-element.44.refs_2_, ...), custom_call_target="tpu_custom_call" | custom-call | tf_op jit(solution)/shard_map/rows/pallas_call | solution.py:307
  24.1 2.6 %collective-permute-start.11 = (f32[128,256]{1,0:T(8,128)S(1)}, f32[128,256]{1,0:T(8,128)S(1)}, u32[]{:S(2)}, u32[]{:S(2)}) collective-permute-start(f32[128,256]{1,0:T(8,128)S(1)} %maximum_select_fusion.1), channel_id=1, source_target_pairs={{0,4},{1,17},{2,6},{3,19},{4,0},{5,21},{6,2},{7,23},{8,12},{9,25},... | collective-permute-start | bytes 393224 | tf_op jit(solution)/shard_map/ppermute | solution.py:264
  27.9 1.5 %collective-permute-done.11 = f32[128,256]{1,0:T(8,128)S(1)} collective-permute-done((f32[128,256]{1,0:T(8,128)S(1)}, f32[128,256]{1,0:T(8,128)S(1)}, u32[]{:S(2)}, u32[]{:S(2)}) %collective-permute-start.11) | collective-permute-done | bytes 131104 | tf_op jit(solution)/shard_map/ppermute | solution.py:264
  29.4 2.3 %collective-permute-done.10 = f32[128,256]{1,0:T(8,128)S(1)} collective-permute-done((f32[128,256]{1,0:T(8,128)S(1)}, f32[128,256]{1,0:T(8,128)S(1)}, u32[]{:S(2)}, u32[]{:S(2)}) %collective-permute-start.10) | collective-permute-done | bytes 131104 | tf_op jit(solution)/shard_map/ppermute | solution.py:264
  31.8 3.2 %collective-permute-start.12 = (f32[128,256]{1,0:T(8,128)S(1)}, f32[128,256]{1,0:T(8,128)S(1)}, u32[]{:S(2)}, u32[]{:S(2)}) collective-permute-start(f32[128,256]{1,0:T(8,128)S(1)} %rsqrt_select_fusion.refs_3_), channel_id=1, source_target_pairs={{0,1},{1,0},{2,3},{3,2},{4,5},{5,4},{6,7},{7,6},{8,9},{9,8},{10,11... | collective-permute-start | bytes 393224 | tf_op jit(solution)/shard_map/ppermute | solution.py:276
  36.0 1.8 %cols.1 = (f32[128,256]{1,0:T(8,128)S(1)}, f32[128,256]{1,0:T(8,128)S(1)}) custom-call(s32[98]{0:T(128)S(1)} %pad_add_fusion.meta_ref, f32[16,256,256]{2,1,0:T(8,128)S(1)} %get-tuple-element.34.refs_0_, f32[16,256,256]{2,1,0:T(8,128)S(1)} %get-tuple-element.39.refs_1_, f32[16,256,256]{2,1,0:T(8,128)S(1)} %get-tuple-element.44.refs_2_, ...), custom_call_target="tpu_custom_call" | custom-call | tf_op jit(solution)/shard_map/cols/pallas_call | solution.py:307
  44.1 1.9 %collective-permute-done.17 = f32[128,256]{1,0:T(8,128)S(1)} collective-permute-done((f32[128,256]{1,0:T(8,128)S(1)}, f32[128,256]{1,0:T(8,128)S(1)}, u32[]{:S(2)}, u32[]{:S(2)}) %collective-permute-start.17) | collective-permute-done | bytes 131104 | tf_op jit(solution)/shard_map/ppermute | solution.py:264
  47.2 3.7 %chip_both.1 = f32[128,256]{1,0:T(8,128)S(1)} custom-call(s32[98]{0:T(128)S(1)} %pad_add_fusion.meta_ref, s32[98]{0:T(128)S(1)} %collective-permute-done.twin_ref, f32[16,256,256]{2,1,0:T(8,128)S(1)} %get-tuple-element.34.refs_0_, f32[16,256,256]{2,1,0:T(8,128)S(1)} %get-tuple-element.39.refs_1_, f32[16,256,256]{2,1,0:T(8,128)S(1)} %get-tuple-element.44.refs_2_, ...), custom_call_target="tpu_custom_call" | custom-call | tf_op jit(solution)/shard_map/chip_both/pallas_call | solution.py:318
  52.1 3.0 %collective-permute-start.20 = (f32[128,256]{1,0:T(8,128)S(1)}, f32[128,256]{1,0:T(8,128)S(1)}, u32[]{:S(2)}, u32[]{:S(2)}) collective-permute-start(f32[128,256]{1,0:T(8,128)S(1)} %chip_both.1), channel_id=1, source_target_pairs={{0,16},{1,65},{2,18},{3,67},{4,20},{5,69},{6,22},{7,71},{8,24},{9,... | collective-permute-start | bytes 393224 | tf_op jit(solution)/shard_map/ppermute | solution.py:264
  55.1 3.2 %collective-permute-start.21 = (f32[128,256]{1,0:T(8,128)S(1)}, f32[128,256]{1,0:T(8,128)S(1)}, u32[]{:S(2)}, u32[]{:S(2)}) collective-permute-start(f32[128,256]{1,0:T(8,128)S(1)} %rsqrt_multiply_fusion.2.refs_6_), channel_id=1, source_target_pairs={{0,1},{1,0},{2,3},{3,2},{4,5},{5,4},{6,7},{7,6},{8,9},{9,8},{10,11... | collective-permute-start | bytes 393224 | tf_op jit(solution)/shard_map/ppermute | solution.py:276
  59.1 1.3 %collective-permute-done.19 = f32[128,256]{1,0:T(8,128)S(1)} collective-permute-done((f32[128,256]{1,0:T(8,128)S(1)}, f32[128,256]{1,0:T(8,128)S(1)}, u32[]{:S(2)}, u32[]{:S(2)}) %collective-permute-start.19) | collective-permute-done | bytes 131104 | tf_op jit(solution)/shard_map/ppermute | solution.py:264
  60.5 3.5 %chip_rows.1 = f32[128,256]{1,0:T(8,128)S(1)} custom-call(s32[98]{0:T(128)S(1)} %pad_add_fusion.meta_ref, s32[98]{0:T(128)S(1)} %collective-permute-done.twin_ref, f32[16,256,256]{2,1,0:T(8,128)S(1)} %get-tuple-element.34.refs_0_, f32[16,256,256]{2,1,0:T(8,128)S(1)} %get-tuple-element.39.refs_1_, f32[16,256,256]{2,1,0:T(8,128)S(1)} %get-tuple-element.44.refs_2_, ...), custom_call_target="tpu_custom_call" | custom-call | tf_op jit(solution)/shard_map/chip_rows/pallas_call | solution.py:318
  64.0 1.7 %collective-permute-start.25 = (f32[128,256]{1,0:T(8,128)S(1)}, f32[128,256]{1,0:T(8,128)S(1)}, u32[]{:S(2)}, u32[]{:S(2)}) collective-permute-start(f32[128,256]{1,0:T(8,128)S(1)} %chip_rows.1), channel_id=1, source_target_pairs={{0,4},{1,17},{2,6},{3,19},{4,0},{5,21},{6,2},{7,23},{8,12},{9,25},... | collective-permute-start | bytes 393224 | tf_op jit(solution)/shard_map/ppermute | solution.py:264
  67.3 2.2 %collective-permute-done.25 = f32[128,256]{1,0:T(8,128)S(1)} collective-permute-done((f32[128,256]{1,0:T(8,128)S(1)}, f32[128,256]{1,0:T(8,128)S(1)}, u32[]{:S(2)}, u32[]{:S(2)}) %collective-permute-start.25) | collective-permute-done | bytes 131104 | tf_op jit(solution)/shard_map/ppermute | solution.py:264
  69.5 1.4 %collective-permute-done.24 = f32[128,256]{1,0:T(8,128)S(1)} collective-permute-done((f32[128,256]{1,0:T(8,128)S(1)}, f32[128,256]{1,0:T(8,128)S(1)}, u32[]{:S(2)}, u32[]{:S(2)}) %collective-permute-start.24) | collective-permute-done | bytes 131104 | tf_op jit(solution)/shard_map/ppermute | solution.py:264
  74.6 4.8 %collective-permute-start.26 = (f32[128,256]{1,0:T(8,128)S(1)}, f32[128,256]{1,0:T(8,128)S(1)}, u32[]{:S(2)}, u32[]{:S(2)}) collective-permute-start(f32[128,256]{1,0:T(8,128)S(1)} %multiply_select_fusion.1.refs_6_), channel_id=1, source_target_pairs={{0,1},{1,0},{2,3},{3,2},{4,5},{5,4},{6,7},{7,6},{8,9},{9,8},{10,11... | collective-permute-start | bytes 393224 | tf_op jit(solution)/shard_map/ppermute | solution.py:276
  80.5 4.0 %chip_sums.1 = f32[128,256]{1,0:T(8,128)S(1)} custom-call(s32[98]{0:T(128)S(1)} %pad_add_fusion.meta_ref, s32[98]{0:T(128)S(1)} %collective-permute-done.twin_ref, f32[16,256,256]{2,1,0:T(8,128)S(1)} %get-tuple-element.34.refs_0_, f32[16,256,256]{2,1,0:T(8,128)S(1)} %get-tuple-element.39.refs_1_, f32[16,256,256]{2,1,0:T(8,128)S(1)} %get-tuple-element.44.refs_2_, ...), custom_call_target="tpu_custom_call" | custom-call | tf_op jit(solution)/shard_map/chip_sums/pallas_call | solution.py:318
  84.8 2.1 %collective-permute-start.33 = (f32[128,256]{1,0:T(8,128)S(1)}, f32[128,256]{1,0:T(8,128)S(1)}, u32[]{:S(2)}, u32[]{:S(2)}) collective-permute-start(f32[128,256]{1,0:T(8,128)S(1)} %chip_sums.1), channel_id=1, source_target_pairs={{0,16},{1,65},{2,18},{3,67},{4,20},{5,69},{6,22},{7,71},{8,24},{9,... | collective-permute-start | bytes 393224 | tf_op jit(solution)/shard_map/ppermute | solution.py:264
  86.9 1.6 %collective-permute-start.32 = (f32[128,256]{1,0:T(8,128)S(1)}, f32[128,256]{1,0:T(8,128)S(1)}, u32[]{:S(2)}, u32[]{:S(2)}) collective-permute-start(f32[128,256]{1,0:T(8,128)S(1)} %chip_sums.1), channel_id=1, source_target_pairs={{0,24},{1,97},{2,26},{3,99},{4,28},{5,101},{6,30},{7,103},{8,16},{... | collective-permute-start | bytes 393224 | tf_op jit(solution)/shard_map/ppermute | solution.py:264
  88.4 4.2 %collective-permute-start.31 = (f32[128,256]{1,0:T(8,128)S(1)}, f32[128,256]{1,0:T(8,128)S(1)}, u32[]{:S(2)}, u32[]{:S(2)}) collective-permute-start(f32[128,256]{1,0:T(8,128)S(1)} %rsqrt_multiply_fusion.1.refs_6_), channel_id=1, source_target_pairs={{0,1},{1,0},{2,3},{3,2},{4,5},{5,4},{6,7},{7,6},{8,9},{9,8},{10,11... | collective-permute-start | bytes 393224 | tf_op jit(solution)/shard_map/ppermute | solution.py:276
  93.6 2.6 %collective-permute-start.38 = (f32[128,256]{1,0:T(8,128)S(1)}, f32[128,256]{1,0:T(8,128)S(1)}, u32[]{:S(2)}, u32[]{:S(2)}) collective-permute-start(f32[128,256]{1,0:T(8,128)S(1)} %multiply_select_fusion), channel_id=1, source_target_pairs={{0,1},{1,0},{2,3},{3,2},{4,5},{5,4},{6,7},{7,6},{8,9},{9,8},{10,11... | collective-permute-start | bytes 393224 | tf_op jit(solution)/shard_map/ppermute | solution.py:276
  96.2 1.3 %collective-permute-start.36 = (f32[128,256]{1,0:T(8,128)S(1)}, f32[128,256]{1,0:T(8,128)S(1)}, u32[]{:S(2)}, u32[]{:S(2)}) collective-permute-start(f32[128,256]{1,0:T(8,128)S(1)} %multiply_select_fusion), channel_id=1, source_target_pairs={{0,4},{1,17},{2,6},{3,19},{4,0},{5,21},{6,2},{7,23},{8,12},{9,25},... | collective-permute-start | bytes 393224 | tf_op jit(solution)/shard_map/ppermute | solution.py:264
  99.0 2.9 %collective-permute-done.36 = f32[128,256]{1,0:T(8,128)S(1)} collective-permute-done((f32[128,256]{1,0:T(8,128)S(1)}, f32[128,256]{1,0:T(8,128)S(1)}, u32[]{:S(2)}, u32[]{:S(2)}) %collective-permute-start.36) | collective-permute-done | bytes 131104 | tf_op jit(solution)/shard_map/ppermute | solution.py:264
  101.8 1.4 %collective-permute-done.35 = f32[128,256]{1,0:T(8,128)S(1)} collective-permute-done((f32[128,256]{1,0:T(8,128)S(1)}, f32[128,256]{1,0:T(8,128)S(1)}, u32[]{:S(2)}, u32[]{:S(2)}) %collective-permute-start.35) | collective-permute-done | bytes 131104 | tf_op jit(solution)/shard_map/ppermute | solution.py:264
  103.3 1.9 %collective-permute-start.37 = (f32[128,256]{1,0:T(8,128)S(1)}, f32[128,256]{1,0:T(8,128)S(1)}, u32[]{:S(2)}, u32[]{:S(2)}) collective-permute-start(f32[128,256]{1,0:T(8,128)S(1)} %get-tuple-element.56), channel_id=1, source_target_pairs={{0,1},{1,0},{2,3},{3,2},{4,5},{5,4},{6,7},{7,6},{8,9},{9,8},{10,11... | collective-permute-start | bytes 393224 | tf_op jit(solution)/shard_map/ppermute | solution.py:276
  106.2 6.5 %scaled.1 = (f32[48,256,256]{2,1,0:T(8,128)}, f32[256,128]{1,0:T(8,128)}, f32[256,128]{1,0:T(8,128)}) custom-call(s32[98]{0:T(128)S(1)} %pad_add_fusion.meta_ref, f32[16,256,256]{2,1,0:T(8,128)S(1)} %get-tuple-element.34.refs_0_, f32[16,256,256]{2,1,0:T(8,128)S(1)} %get-tuple-element.39.refs_1_, f32[16,256,256]{2,1,0:T(8,128)S(1)} %get-tuple-element.44.refs_2_, ...), custom_call_target="tpu_custom_call" | custom-call | tf_op jit(solution)/shard_map/scaled/pallas_call | solution.py:367
  (67 shorter events, 29.3 us)
Async XLA Ops:
  10.0 8.3 %collective-permute-start.2 = (f32[16,256,256]{2,1,0:T(8,128)S(1)}, f32[16,256,256]{2,1,0:T(8,128)S(1)}, u32[]{:S(2)}, u32[]{:S(2)}) collective-permute-start(f32[16,256,256]{2,1,0:T(8,128)S(1)} %get-tuple-element.34.refs_0_), channel_id=1, source_target_pairs={{0,1},{1,0},{2,3},{3,2},{4,5},{5,4},{6,7},{7,6},{8,9},{9,8},{10,11... | collective-permute-start | bytes 12582920 | tf_op jit(solution)/shard_map/ppermute | solution.py:276
  10.4 5.6 %collective-permute-start.5 = (f32[128,256]{1,0:T(8,128)S(1)}, f32[128,256]{1,0:T(8,128)S(1)}, u32[]{:S(2)}, u32[]{:S(2)}) collective-permute-start(f32[128,256]{1,0:T(8,128)S(1)} %max.63), channel_id=1, source_target_pairs={{0,16},{1,65},{2,18},{3,67},{4,20},{5,69},{6,22},{7,71},{8,24},{9,... | collective-permute-start | bytes 393224 | tf_op jit(solution)/shard_map/ppermute | solution.py:264
  12.4 5.3 %collective-permute-start.4 = (f32[128,256]{1,0:T(8,128)S(1)}, f32[128,256]{1,0:T(8,128)S(1)}, u32[]{:S(2)}, u32[]{:S(2)}) collective-permute-start(f32[128,256]{1,0:T(8,128)S(1)} %max.63), channel_id=1, source_target_pairs={{0,24},{1,97},{2,26},{3,99},{4,28},{5,101},{6,30},{7,103},{8,16},{... | collective-permute-start | bytes 393224 | tf_op jit(solution)/shard_map/ppermute | solution.py:264
  13.7 4.4 %collective-permute-start.3 = (f32[128,256]{1,0:T(8,128)S(1)}, f32[128,256]{1,0:T(8,128)S(1)}, u32[]{:S(2)}, u32[]{:S(2)}) collective-permute-start(f32[128,256]{1,0:T(8,128)S(1)} %max.63), channel_id=1, source_target_pairs={{0,8},{1,33},{2,10},{3,35},{4,12},{5,37},{6,14},{7,39},{8,0},{9,41... | collective-permute-start | bytes 393224 | tf_op jit(solution)/shard_map/ppermute | solution.py:264
  23.6 8.2 %collective-permute-start.8 = (f32[16,256,256]{2,1,0:T(8,128)S(1)}, f32[16,256,256]{2,1,0:T(8,128)S(1)}, u32[]{:S(2)}, u32[]{:S(2)}) collective-permute-start(f32[16,256,256]{2,1,0:T(8,128)S(1)} %get-tuple-element.39.refs_1_), channel_id=1, source_target_pairs={{0,1},{1,0},{2,3},{3,2},{4,5},{5,4},{6,7},{7,6},{8,9},{9,8},{10,11... | collective-permute-start | bytes 12582920 | tf_op jit(solution)/shard_map/ppermute | solution.py:276
  24.1 5.3 %collective-permute-start.11 = (f32[128,256]{1,0:T(8,128)S(1)}, f32[128,256]{1,0:T(8,128)S(1)}, u32[]{:S(2)}, u32[]{:S(2)}) collective-permute-start(f32[128,256]{1,0:T(8,128)S(1)} %maximum_select_fusion.1), channel_id=1, source_target_pairs={{0,4},{1,17},{2,6},{3,19},{4,0},{5,21},{6,2},{7,23},{8,12},{9,25},... | collective-permute-start | bytes 393224 | tf_op jit(solution)/shard_map/ppermute | solution.py:264
  26.7 5.0 %collective-permute-start.10 = (f32[128,256]{1,0:T(8,128)S(1)}, f32[128,256]{1,0:T(8,128)S(1)}, u32[]{:S(2)}, u32[]{:S(2)}) collective-permute-start(f32[128,256]{1,0:T(8,128)S(1)} %maximum_select_fusion.1), channel_id=1, source_target_pairs={{0,6},{1,25},{2,4},{3,27},{4,2},{5,29},{6,0},{7,31},{8,14},{9,17},... | collective-permute-start | bytes 393224 | tf_op jit(solution)/shard_map/ppermute | solution.py:264
  31.8 4.2 %collective-permute-start.12 = (f32[128,256]{1,0:T(8,128)S(1)}, f32[128,256]{1,0:T(8,128)S(1)}, u32[]{:S(2)}, u32[]{:S(2)}) collective-permute-start(f32[128,256]{1,0:T(8,128)S(1)} %rsqrt_select_fusion.refs_3_), channel_id=1, source_target_pairs={{0,1},{1,0},{2,3},{3,2},{4,5},{5,4},{6,7},{7,6},{8,9},{9,8},{10,11... | collective-permute-start | bytes 393224 | tf_op jit(solution)/shard_map/ppermute | solution.py:276
  39.9 7.3 %collective-permute-start.14 = (f32[16,256,256]{2,1,0:T(8,128)S(1)}, f32[16,256,256]{2,1,0:T(8,128)S(1)}, u32[]{:S(2)}, u32[]{:S(2)}) collective-permute-start(f32[16,256,256]{2,1,0:T(8,128)S(1)} %get-tuple-element.44.refs_2_), channel_id=1, source_target_pairs={{0,1},{1,0},{2,3},{3,2},{4,5},{5,4},{6,7},{7,6},{8,9},{9,8},{10,11... | collective-permute-start | bytes 12582920 | tf_op jit(solution)/shard_map/ppermute | solution.py:276
  40.4 5.6 %collective-permute-start.17 = (f32[128,256]{1,0:T(8,128)S(1)}, f32[128,256]{1,0:T(8,128)S(1)}, u32[]{:S(2)}, u32[]{:S(2)}) collective-permute-start(f32[128,256]{1,0:T(8,128)S(1)} %maximum_select_fusion), channel_id=1, source_target_pairs={{0,64},{1,5},{2,66},{3,7},{4,68},{5,1},{6,70},{7,3},{8,72},{9,13},... | collective-permute-start | bytes 393224 | tf_op jit(solution)/shard_map/ppermute | solution.py:264
  40.9 6.2 %collective-permute-start.16 = (f32[128,256]{1,0:T(8,128)S(1)}, f32[128,256]{1,0:T(8,128)S(1)}, u32[]{:S(2)}, u32[]{:S(2)}) collective-permute-start(f32[128,256]{1,0:T(8,128)S(1)} %maximum_select_fusion), channel_id=1, source_target_pairs={{0,96},{1,7},{2,98},{3,5},{4,100},{5,3},{6,102},{7,1},{8,104},{9,1... | collective-permute-start | bytes 393224 | tf_op jit(solution)/shard_map/ppermute | solution.py:264
  41.8 5.3 %collective-permute-start.15 = (f32[128,256]{1,0:T(8,128)S(1)}, f32[128,256]{1,0:T(8,128)S(1)}, u32[]{:S(2)}, u32[]{:S(2)}) collective-permute-start(f32[128,256]{1,0:T(8,128)S(1)} %maximum_select_fusion), channel_id=1, source_target_pairs={{0,32},{1,3},{2,34},{3,1},{4,36},{5,7},{6,38},{7,5},{8,40},{9,11},... | collective-permute-start | bytes 393224 | tf_op jit(solution)/shard_map/ppermute | solution.py:264
  43.0 4.2 %collective-permute-start = (s32[98]{0:T(128)S(1)}, s32[98]{0:T(128)S(1)}, u32[]{:S(2)}, u32[]{:S(2)}) collective-permute-start(s32[98]{0:T(128)S(1)} %pad_add_fusion.meta_ref), channel_id=1, source_target_pairs={{0,1},{1,0},{2,3},{3,2},{4,5},{5,4},{6,7},{7,6},{8,9},{9,8},{10,11... | collective-permute-start | bytes 1184 | tf_op jit(solution)/shard_map/ppermute | solution.py:276
  50.9 4.2 %collective-permute-start.18 = (f32[128,256]{1,0:T(8,128)S(1)}, f32[128,256]{1,0:T(8,128)S(1)}, u32[]{:S(2)}, u32[]{:S(2)}) collective-permute-start(f32[128,256]{1,0:T(8,128)S(1)} %chip_both.1), channel_id=1, source_target_pairs={{0,8},{1,33},{2,10},{3,35},{4,12},{5,37},{6,14},{7,39},{8,0},{9,41... | collective-permute-start | bytes 393224 | tf_op jit(solution)/shard_map/ppermute | solution.py:264
  52.1 7.0 %collective-permute-start.20 = (f32[128,256]{1,0:T(8,128)S(1)}, f32[128,256]{1,0:T(8,128)S(1)}, u32[]{:S(2)}, u32[]{:S(2)}) collective-permute-start(f32[128,256]{1,0:T(8,128)S(1)} %chip_both.1), channel_id=1, source_target_pairs={{0,16},{1,65},{2,18},{3,67},{4,20},{5,69},{6,22},{7,71},{8,24},{9,... | collective-permute-start | bytes 393224 | tf_op jit(solution)/shard_map/ppermute | solution.py:264
  55.1 5.3 %collective-permute-start.19 = (f32[128,256]{1,0:T(8,128)S(1)}, f32[128,256]{1,0:T(8,128)S(1)}, u32[]{:S(2)}, u32[]{:S(2)}) collective-permute-start(f32[128,256]{1,0:T(8,128)S(1)} %chip_both.1), channel_id=1, source_target_pairs={{0,24},{1,97},{2,26},{3,99},{4,28},{5,101},{6,30},{7,103},{8,16},{... | collective-permute-start | bytes 393224 | tf_op jit(solution)/shard_map/ppermute | solution.py:264
  55.1 5.3 %collective-permute-start.21 = (f32[128,256]{1,0:T(8,128)S(1)}, f32[128,256]{1,0:T(8,128)S(1)}, u32[]{:S(2)}, u32[]{:S(2)}) collective-permute-start(f32[128,256]{1,0:T(8,128)S(1)} %rsqrt_multiply_fusion.2.refs_6_), channel_id=1, source_target_pairs={{0,1},{1,0},{2,3},{3,2},{4,5},{5,4},{6,7},{7,6},{8,9},{9,8},{10,11... | collective-permute-start | bytes 393224 | tf_op jit(solution)/shard_map/ppermute | solution.py:276
  64.0 5.5 %collective-permute-start.25 = (f32[128,256]{1,0:T(8,128)S(1)}, f32[128,256]{1,0:T(8,128)S(1)}, u32[]{:S(2)}, u32[]{:S(2)}) collective-permute-start(f32[128,256]{1,0:T(8,128)S(1)} %chip_rows.1), channel_id=1, source_target_pairs={{0,4},{1,17},{2,6},{3,19},{4,0},{5,21},{6,2},{7,23},{8,12},{9,25},... | collective-permute-start | bytes 393224 | tf_op jit(solution)/shard_map/ppermute | solution.py:264
  65.7 5.2 %collective-permute-start.24 = (f32[128,256]{1,0:T(8,128)S(1)}, f32[128,256]{1,0:T(8,128)S(1)}, u32[]{:S(2)}, u32[]{:S(2)}) collective-permute-start(f32[128,256]{1,0:T(8,128)S(1)} %chip_rows.1), channel_id=1, source_target_pairs={{0,6},{1,25},{2,4},{3,27},{4,2},{5,29},{6,0},{7,31},{8,14},{9,17},... | collective-permute-start | bytes 393224 | tf_op jit(solution)/shard_map/ppermute | solution.py:264
  66.7 4.6 %collective-permute-start.23 = (f32[128,256]{1,0:T(8,128)S(1)}, f32[128,256]{1,0:T(8,128)S(1)}, u32[]{:S(2)}, u32[]{:S(2)}) collective-permute-start(f32[128,256]{1,0:T(8,128)S(1)} %chip_rows.1), channel_id=1, source_target_pairs={{0,2},{1,9},{2,0},{3,11},{4,6},{5,13},{6,4},{7,15},{8,10},{9,1},{1... | collective-permute-start | bytes 393224 | tf_op jit(solution)/shard_map/ppermute | solution.py:264
  67.2 12.2 %collective-permute-start.22 = (f32[128,256]{1,0:T(8,128)S(1)}, f32[128,256]{1,0:T(8,128)S(1)}, u32[]{:S(2)}, u32[]{:S(2)}) collective-permute-start(f32[128,256]{1,0:T(8,128)S(1)} %multiply_select_fusion.2.refs_6_), channel_id=1, source_target_pairs={{0,1},{1,0},{2,3},{3,2},{4,5},{5,4},{6,7},{7,6},{8,9},{9,8},{10,11... | collective-permute-start | bytes 393224 | tf_op jit(solution)/shard_map/ppermute | solution.py:276
  71.9 7.5 %collective-permute-start.29 = (f32[128,256]{1,0:T(8,128)S(1)}, f32[128,256]{1,0:T(8,128)S(1)}, u32[]{:S(2)}, u32[]{:S(2)}) collective-permute-start(f32[128,256]{1,0:T(8,128)S(1)} %chip_cols.1), channel_id=1, source_target_pairs={{0,64},{1,5},{2,66},{3,7},{4,68},{5,1},{6,70},{7,3},{8,72},{9,13},... | collective-permute-start | bytes 393224 | tf_op jit(solution)/shard_map/ppermute | solution.py:264
  73.0 6.4 %collective-permute-start.28 = (f32[128,256]{1,0:T(8,128)S(1)}, f32[128,256]{1,0:T(8,128)S(1)}, u32[]{:S(2)}, u32[]{:S(2)}) collective-permute-start(f32[128,256]{1,0:T(8,128)S(1)} %chip_cols.1), channel_id=1, source_target_pairs={{0,96},{1,7},{2,98},{3,5},{4,100},{5,3},{6,102},{7,1},{8,104},{9,1... | collective-permute-start | bytes 393224 | tf_op jit(solution)/shard_map/ppermute | solution.py:264
  74.1 5.3 %collective-permute-start.27 = (f32[128,256]{1,0:T(8,128)S(1)}, f32[128,256]{1,0:T(8,128)S(1)}, u32[]{:S(2)}, u32[]{:S(2)}) collective-permute-start(f32[128,256]{1,0:T(8,128)S(1)} %chip_cols.1), channel_id=1, source_target_pairs={{0,32},{1,3},{2,34},{3,1},{4,36},{5,7},{6,38},{7,5},{8,40},{9,11},... | collective-permute-start | bytes 393224 | tf_op jit(solution)/shard_map/ppermute | solution.py:264
  74.6 5.7 %collective-permute-start.26 = (f32[128,256]{1,0:T(8,128)S(1)}, f32[128,256]{1,0:T(8,128)S(1)}, u32[]{:S(2)}, u32[]{:S(2)}) collective-permute-start(f32[128,256]{1,0:T(8,128)S(1)} %multiply_select_fusion.1.refs_6_), channel_id=1, source_target_pairs={{0,1},{1,0},{2,3},{3,2},{4,5},{5,4},{6,7},{7,6},{8,9},{9,8},{10,11... | collective-permute-start | bytes 393224 | tf_op jit(solution)/shard_map/ppermute | solution.py:276
  84.8 7.8 %collective-permute-start.33 = (f32[128,256]{1,0:T(8,128)S(1)}, f32[128,256]{1,0:T(8,128)S(1)}, u32[]{:S(2)}, u32[]{:S(2)}) collective-permute-start(f32[128,256]{1,0:T(8,128)S(1)} %chip_sums.1), channel_id=1, source_target_pairs={{0,16},{1,65},{2,18},{3,67},{4,20},{5,69},{6,22},{7,71},{8,24},{9,... | collective-permute-start | bytes 393224 | tf_op jit(solution)/shard_map/ppermute | solution.py:264
  86.9 5.7 %collective-permute-start.32 = (f32[128,256]{1,0:T(8,128)S(1)}, f32[128,256]{1,0:T(8,128)S(1)}, u32[]{:S(2)}, u32[]{:S(2)}) collective-permute-start(f32[128,256]{1,0:T(8,128)S(1)} %chip_sums.1), channel_id=1, source_target_pairs={{0,24},{1,97},{2,26},{3,99},{4,28},{5,101},{6,30},{7,103},{8,16},{... | collective-permute-start | bytes 393224 | tf_op jit(solution)/shard_map/ppermute | solution.py:264
  88.4 5.2 %collective-permute-start.31 = (f32[128,256]{1,0:T(8,128)S(1)}, f32[128,256]{1,0:T(8,128)S(1)}, u32[]{:S(2)}, u32[]{:S(2)}) collective-permute-start(f32[128,256]{1,0:T(8,128)S(1)} %rsqrt_multiply_fusion.1.refs_6_), channel_id=1, source_target_pairs={{0,1},{1,0},{2,3},{3,2},{4,5},{5,4},{6,7},{7,6},{8,9},{9,8},{10,11... | collective-permute-start | bytes 393224 | tf_op jit(solution)/shard_map/ppermute | solution.py:276
  93.6 5.3 %collective-permute-start.38 = (f32[128,256]{1,0:T(8,128)S(1)}, f32[128,256]{1,0:T(8,128)S(1)}, u32[]{:S(2)}, u32[]{:S(2)}) collective-permute-start(f32[128,256]{1,0:T(8,128)S(1)} %multiply_select_fusion), channel_id=1, source_target_pairs={{0,1},{1,0},{2,3},{3,2},{4,5},{5,4},{6,7},{7,6},{8,9},{9,8},{10,11... | collective-permute-start | bytes 393224 | tf_op jit(solution)/shard_map/ppermute | solution.py:276
  96.2 5.6 %collective-permute-start.36 = (f32[128,256]{1,0:T(8,128)S(1)}, f32[128,256]{1,0:T(8,128)S(1)}, u32[]{:S(2)}, u32[]{:S(2)}) collective-permute-start(f32[128,256]{1,0:T(8,128)S(1)} %multiply_select_fusion), channel_id=1, source_target_pairs={{0,4},{1,17},{2,6},{3,19},{4,0},{5,21},{6,2},{7,23},{8,12},{9,25},... | collective-permute-start | bytes 393224 | tf_op jit(solution)/shard_map/ppermute | solution.py:264
  97.5 5.7 %collective-permute-start.35 = (f32[128,256]{1,0:T(8,128)S(1)}, f32[128,256]{1,0:T(8,128)S(1)}, u32[]{:S(2)}, u32[]{:S(2)}) collective-permute-start(f32[128,256]{1,0:T(8,128)S(1)} %multiply_select_fusion), channel_id=1, source_target_pairs={{0,6},{1,25},{2,4},{3,27},{4,2},{5,29},{6,0},{7,31},{8,14},{9,17},... | collective-permute-start | bytes 393224 | tf_op jit(solution)/shard_map/ppermute | solution.py:264
  98.4 4.8 %collective-permute-start.34 = (f32[128,256]{1,0:T(8,128)S(1)}, f32[128,256]{1,0:T(8,128)S(1)}, u32[]{:S(2)}, u32[]{:S(2)}) collective-permute-start(f32[128,256]{1,0:T(8,128)S(1)} %multiply_select_fusion), channel_id=1, source_target_pairs={{0,2},{1,9},{2,0},{3,11},{4,6},{5,13},{6,4},{7,15},{8,10},{9,1},{1... | collective-permute-start | bytes 393224 | tf_op jit(solution)/shard_map/ppermute | solution.py:264
  (7 other events, 20.2 us)

commit v5 on v4

--- a/solution.py
+++ b/solution.py
@@ -11,7 +11,7 @@
 BLOCKS = 128
 EPS = 1e-06
 AXES = ("row", "col", "depth")
-LOAD_GROUP = 8
+LOAD_GROUP = 4
 SWEEP_GROUP = 16
 CHIP_GROUP = 8
 COPY_GROUP = 4
@@ -325,7 +325,7 @@
         )(meta, twin, *stay(held), *stay(twins), s)
 
     def late_swap(v, parts):
-        return swap(lax.optimization_barrier((v, parts[1]))[0])
+        return swap(lax.optimization_barrier((v, parts[2]))[0])
 
     twin = swap(meta)
     m = jnp.maximum(mine, swap(other))

time: 114 us -> 113 us (level); the launches traced: 113 us -> 113 us
  Pallas kernels: 25.9 us -> 20.8 us
  waiting for transfers between devices: 29.1 us -> 31.9 us
  starting transfers between devices: 54.9 us -> 57.5 us
    ppermute x24, starting transfers between devices: 27.1 us -> 30.4 us  [slot(): parts.append(lax.ppermute(v, AXES, spots(move)))]
    pallas_call x4, Pallas kernels: 11.7 us -> 8.43 us  [chip(): pl.pallas_call(functools.partial(chip_kernel, slots, part_slots, kinds, s...]
    ppermute x24, waiting for transfers between devices: 21.2 us -> 24 us  [slot(): parts.append(lax.ppermute(v, AXES, spots(move)))]
    pallas_call x2, Pallas kernels: 3.67 us -> 2.43 us  [run(): pl.pallas_call(functools.partial(kernel, slots, part_slots), out_shape=(v...]
  transfers between devices with their start and end apart: 39 -> 39, of which waited for: 22 -> 24; matrix products, arithmetic and copies ran while one was open for 0% -> 0% of each run, Pallas kernels for 0% -> 0%
where the time goes in v5:
time: 113 us
  starting transfers between devices  57.5 us (51%)
  waiting for transfers between devices  31.9 us (28%)
  Pallas kernels  20.8 us (18%)
  between operations  1.65 us (1%)
  other arithmetic  1.36 us (1%)
    ppermute x24, starting transfers between devices, slot(): parts.append(lax.ppermute(v, AXES, spots(move)))  30.4 us
    ppermute x15, starting transfers between devices, shards(): swap = lambda v: lax.ppermute(v, 'depth', [(0, 1), (1, 0)])  27.1 us
    ppermute x24, waiting for transfers between devices, slot(): parts.append(lax.ppermute(v, AXES, spots(move)))  24 us
    pallas_call x4, Pallas kernels, chip(): pl.pallas_call(functools.partial(chip_kernel, slots, part_slots, kinds, s...  8.43 us
    ppermute x15, waiting for transfers between devices, shards(): swap = lambda v: lax.ppermute(v, 'depth', [(0, 1), (1, 0)])  7.9 us
    pallas_call x1, Pallas kernels, shards(): pl.pallas_call(functools.partial(final_kernel, slots, part_slots), out_sh...  6.45 us
    pallas_call x1, Pallas kernels, shards(): pl.pallas_call(functools.partial(load_kernel, slots, part_slots), out_sha...  3.45 us
    pallas_call x2, Pallas kernels, run(): pl.pallas_call(functools.partial(kernel, slots, part_slots), out_shape=(v...  2.43 us
  transfers between devices with their start and end apart: 39, of which 24 were waited for; matrix products, arithmetic and copies ran while one was open for 0% of the time, Pallas kernels for 0%

profile of v5, /device:TPU:1, one launch (start us, length us, event | category | flops | bytes accessed | tf_op | source)
XLA Modules:
  0.0 113.1 jit_solution(10402048456779360528)
XLA Ops:
  2.0 3.4 %load.1 = (f32[16,256,256]{2,1,0:T(8,128)S(1)}, f32[16,256,256]{2,1,0:T(8,128)S(1)}, f32[16,256,256]{2,1,0:T(8,128)S(1)}, f32[128,256]{1,0:T(8,128)S(1)}, f32[12...) custom-call(s32[98]{0:T(128)S(1)} %pad_add_fusion.meta_ref, f32[48,256,256]{2,1,0:T(8,128)} %bitcast.9), custom_call_target="tpu_custom_call" | custom-call | tf_op jit(solution)/shard_map/load/pallas_call | solution.py:281
  5.5 1.8 %collective-permute-start.1 = (f32[128,256]{1,0:T(8,128)S(1)}, f32[128,256]{1,0:T(8,128)S(1)}, u32[]{:S(2)}, u32[]{:S(2)}) collective-permute-start(f32[128,256]{1,0:T(8,128)S(1)} %get-tuple-element.33), channel_id=1, source_target_pairs={{0,1},{1,0},{2,3},{3,2},{4,5},{5,4},{6,7},{7,6},{8,9},{9,8},{10,11... | collective-permute-start | bytes 393224 | tf_op jit(solution)/shard_map/ppermute | solution.py:276
  8.7 3.4 %collective-permute-start.5 = (f32[128,256]{1,0:T(8,128)S(1)}, f32[128,256]{1,0:T(8,128)S(1)}, u32[]{:S(2)}, u32[]{:S(2)}) collective-permute-start(f32[128,256]{1,0:T(8,128)S(1)} %max.63), channel_id=1, source_target_pairs={{0,16},{1,65},{2,18},{3,67},{4,20},{5,69},{6,22},{7,71},{8,24},{9,... | collective-permute-start | bytes 393224 | tf_op jit(solution)/shard_map/ppermute | solution.py:264
  13.2 1.6 %collective-permute-done.5 = f32[128,256]{1,0:T(8,128)S(1)} collective-permute-done((f32[128,256]{1,0:T(8,128)S(1)}, f32[128,256]{1,0:T(8,128)S(1)}, u32[]{:S(2)}, u32[]{:S(2)}) %collective-permute-start.5) | collective-permute-done | bytes 131104 | tf_op jit(solution)/shard_map/ppermute | solution.py:264
  14.8 2.7 %collective-permute-done.4 = f32[128,256]{1,0:T(8,128)S(1)} collective-permute-done((f32[128,256]{1,0:T(8,128)S(1)}, f32[128,256]{1,0:T(8,128)S(1)}, u32[]{:S(2)}, u32[]{:S(2)}) %collective-permute-start.4) | collective-permute-done | bytes 131104 | tf_op jit(solution)/shard_map/ppermute | solution.py:264
  23.4 2.8 %collective-permute-start.11 = (f32[128,256]{1,0:T(8,128)S(1)}, f32[128,256]{1,0:T(8,128)S(1)}, u32[]{:S(2)}, u32[]{:S(2)}) collective-permute-start(f32[128,256]{1,0:T(8,128)S(1)} %maximum_select_fusion.1), channel_id=1, source_target_pairs={{0,4},{1,17},{2,6},{3,19},{4,0},{5,21},{6,2},{7,23},{8,12},{9,25},... | collective-permute-start | bytes 393224 | tf_op jit(solution)/shard_map/ppermute | solution.py:264
  26.2 1.5 %collective-permute-start.10 = (f32[128,256]{1,0:T(8,128)S(1)}, f32[128,256]{1,0:T(8,128)S(1)}, u32[]{:S(2)}, u32[]{:S(2)}) collective-permute-start(f32[128,256]{1,0:T(8,128)S(1)} %maximum_select_fusion.1), channel_id=1, source_target_pairs={{0,6},{1,25},{2,4},{3,27},{4,2},{5,29},{6,0},{7,31},{8,14},{9,17},... | collective-permute-start | bytes 393224 | tf_op jit(solution)/shard_map/ppermute | solution.py:264
  29.0 2.5 %collective-permute-done.10 = f32[128,256]{1,0:T(8,128)S(1)} collective-permute-done((f32[128,256]{1,0:T(8,128)S(1)}, f32[128,256]{1,0:T(8,128)S(1)}, u32[]{:S(2)}, u32[]{:S(2)}) %collective-permute-start.10) | collective-permute-done | bytes 131104 | tf_op jit(solution)/shard_map/ppermute | solution.py:264
  32.1 2.2 %collective-permute-start.12 = (f32[128,256]{1,0:T(8,128)S(1)}, f32[128,256]{1,0:T(8,128)S(1)}, u32[]{:S(2)}, u32[]{:S(2)}) collective-permute-start(f32[128,256]{1,0:T(8,128)S(1)} %rsqrt_select_fusion.refs_3_), channel_id=1, source_target_pairs={{0,1},{1,0},{2,3},{3,2},{4,5},{5,4},{6,7},{7,6},{8,9},{9,8},{10,11... | collective-permute-start | bytes 393224 | tf_op jit(solution)/shard_map/ppermute | solution.py:276
  35.4 1.2 %cols.1 = (f32[128,256]{1,0:T(8,128)S(1)}, f32[128,256]{1,0:T(8,128)S(1)}) custom-call(s32[98]{0:T(128)S(1)} %pad_add_fusion.meta_ref, f32[16,256,256]{2,1,0:T(8,128)S(1)} %get-tuple-element.34.refs_0_, f32[16,256,256]{2,1,0:T(8,128)S(1)} %get-tuple-element.39.refs_1_, f32[16,256,256]{2,1,0:T(8,128)S(1)} %get-tuple-element.44.refs_2_, ...), custom_call_target="tpu_custom_call" | custom-call | tf_op jit(solution)/shard_map/cols/pallas_call | solution.py:307
  40.2 1.3 %collective-permute-start.16 = (f32[128,256]{1,0:T(8,128)S(1)}, f32[128,256]{1,0:T(8,128)S(1)}, u32[]{:S(2)}, u32[]{:S(2)}) collective-permute-start(f32[128,256]{1,0:T(8,128)S(1)} %maximum_select_fusion), channel_id=1, source_target_pairs={{0,96},{1,7},{2,98},{3,5},{4,100},{5,3},{6,102},{7,1},{8,104},{9,1... | collective-permute-start | bytes 393224 | tf_op jit(solution)/shard_map/ppermute | solution.py:264
  41.8 2.5 %collective-permute-start = (s32[98]{0:T(128)S(1)}, s32[98]{0:T(128)S(1)}, u32[]{:S(2)}, u32[]{:S(2)}) collective-permute-start(s32[98]{0:T(128)S(1)} %pad_add_fusion.meta_ref), channel_id=1, source_target_pairs={{0,1},{1,0},{2,3},{3,2},{4,5},{5,4},{6,7},{7,6},{8,9},{9,8},{10,11... | collective-permute-start | bytes 1184 | tf_op jit(solution)/shard_map/ppermute | solution.py:276
  46.0 2.6 %chip_both.1 = f32[128,256]{1,0:T(8,128)S(1)} custom-call(s32[98]{0:T(128)S(1)} %pad_add_fusion.meta_ref, s32[98]{0:T(128)S(1)} %collective-permute-done.twin_ref, f32[16,256,256]{2,1,0:T(8,128)S(1)} %get-tuple-element.34.refs_0_, f32[16,256,256]{2,1,0:T(8,128)S(1)} %get-tuple-element.39.refs_1_, f32[16,256,256]{2,1,0:T(8,128)S(1)} %get-tuple-element.44.refs_2_, ...), custom_call_target="tpu_custom_call" | custom-call | tf_op jit(solution)/shard_map/chip_both/pallas_call | solution.py:318
  48.6 3.5 %collective-permute-start.19 = (f32[128,256]{1,0:T(8,128)S(1)}, f32[128,256]{1,0:T(8,128)S(1)}, u32[]{:S(2)}, u32[]{:S(2)}) collective-permute-start(f32[128,256]{1,0:T(8,128)S(1)} %chip_both.1), channel_id=1, source_target_pairs={{0,24},{1,97},{2,26},{3,99},{4,28},{5,101},{6,30},{7,103},{8,16},{... | collective-permute-start | bytes 393224 | tf_op jit(solution)/shard_map/ppermute | solution.py:264
  52.8 2.6 %collective-permute-done.19 = f32[128,256]{1,0:T(8,128)S(1)} collective-permute-done((f32[128,256]{1,0:T(8,128)S(1)}, f32[128,256]{1,0:T(8,128)S(1)}, u32[]{:S(2)}, u32[]{:S(2)}) %collective-permute-start.19) | collective-permute-done | bytes 131104 | tf_op jit(solution)/shard_map/ppermute | solution.py:264
  55.4 5.1 %collective-permute-start.21 = (f32[128,256]{1,0:T(8,128)S(1)}, f32[128,256]{1,0:T(8,128)S(1)}, u32[]{:S(2)}, u32[]{:S(2)}) collective-permute-start(f32[128,256]{1,0:T(8,128)S(1)} %rsqrt_multiply_fusion.2.refs_6_), channel_id=1, source_target_pairs={{0,1},{1,0},{2,3},{3,2},{4,5},{5,4},{6,7},{7,6},{8,9},{9,8},{10,11... | collective-permute-start | bytes 393224 | tf_op jit(solution)/shard_map/ppermute | solution.py:276
  61.6 2.4 %chip_rows.1 = f32[128,256]{1,0:T(8,128)S(1)} custom-call(s32[98]{0:T(128)S(1)} %pad_add_fusion.meta_ref, s32[98]{0:T(128)S(1)} %collective-permute-done.twin_ref, f32[16,256,256]{2,1,0:T(8,128)S(1)} %get-tuple-element.34.refs_0_, f32[16,256,256]{2,1,0:T(8,128)S(1)} %get-tuple-element.39.refs_1_, f32[16,256,256]{2,1,0:T(8,128)S(1)} %get-tuple-element.44.refs_2_, ...), custom_call_target="tpu_custom_call" | custom-call | tf_op jit(solution)/shard_map/chip_rows/pallas_call | solution.py:318
  64.1 4.5 %collective-permute-start.24 = (f32[128,256]{1,0:T(8,128)S(1)}, f32[128,256]{1,0:T(8,128)S(1)}, u32[]{:S(2)}, u32[]{:S(2)}) collective-permute-start(f32[128,256]{1,0:T(8,128)S(1)} %chip_rows.1), channel_id=1, source_target_pairs={{0,6},{1,25},{2,4},{3,27},{4,2},{5,29},{6,0},{7,31},{8,14},{9,17},... | collective-permute-start | bytes 393224 | tf_op jit(solution)/shard_map/ppermute | solution.py:264
  69.7 2.2 %collective-permute-done.24 = f32[128,256]{1,0:T(8,128)S(1)} collective-permute-done((f32[128,256]{1,0:T(8,128)S(1)}, f32[128,256]{1,0:T(8,128)S(1)}, u32[]{:S(2)}, u32[]{:S(2)}) %collective-permute-start.24) | collective-permute-done | bytes 131104 | tf_op jit(solution)/shard_map/ppermute | solution.py:264
  74.1 2.1 %collective-permute-start.27 = (f32[128,256]{1,0:T(8,128)S(1)}, f32[128,256]{1,0:T(8,128)S(1)}, u32[]{:S(2)}, u32[]{:S(2)}) collective-permute-start(f32[128,256]{1,0:T(8,128)S(1)} %chip_cols.1), channel_id=1, source_target_pairs={{0,32},{1,3},{2,34},{3,1},{4,36},{5,7},{6,38},{7,5},{8,40},{9,11},... | collective-permute-start | bytes 393224 | tf_op jit(solution)/shard_map/ppermute | solution.py:264
  76.3 1.9 %collective-permute-start.26 = (f32[128,256]{1,0:T(8,128)S(1)}, f32[128,256]{1,0:T(8,128)S(1)}, u32[]{:S(2)}, u32[]{:S(2)}) collective-permute-start(f32[128,256]{1,0:T(8,128)S(1)} %multiply_select_fusion.1.refs_6_), channel_id=1, source_target_pairs={{0,1},{1,0},{2,3},{3,2},{4,5},{5,4},{6,7},{7,6},{8,9},{9,8},{10,11... | collective-permute-start | bytes 393224 | tf_op jit(solution)/shard_map/ppermute | solution.py:276
  80.4 2.8 %chip_sums.1 = f32[128,256]{1,0:T(8,128)S(1)} custom-call(s32[98]{0:T(128)S(1)} %pad_add_fusion.meta_ref, s32[98]{0:T(128)S(1)} %collective-permute-done.twin_ref, f32[16,256,256]{2,1,0:T(8,128)S(1)} %get-tuple-element.34.refs_0_, f32[16,256,256]{2,1,0:T(8,128)S(1)} %get-tuple-element.39.refs_1_, f32[16,256,256]{2,1,0:T(8,128)S(1)} %get-tuple-element.44.refs_2_, ...), custom_call_target="tpu_custom_call" | custom-call | tf_op jit(solution)/shard_map/chip_sums/pallas_call | solution.py:318
  83.3 1.6 %collective-permute-start.30 = (f32[128,256]{1,0:T(8,128)S(1)}, f32[128,256]{1,0:T(8,128)S(1)}, u32[]{:S(2)}, u32[]{:S(2)}) collective-permute-start(f32[128,256]{1,0:T(8,128)S(1)} %chip_sums.1), channel_id=1, source_target_pairs={{0,24},{1,97},{2,26},{3,99},{4,28},{5,101},{6,30},{7,103},{8,16},{... | collective-permute-start | bytes 393224 | tf_op jit(solution)/shard_map/ppermute | solution.py:264
  84.9 2.1 %collective-permute-start.33 = (f32[128,256]{1,0:T(8,128)S(1)}, f32[128,256]{1,0:T(8,128)S(1)}, u32[]{:S(2)}, u32[]{:S(2)}) collective-permute-start(f32[128,256]{1,0:T(8,128)S(1)} %chip_sums.1), channel_id=1, source_target_pairs={{0,16},{1,65},{2,18},{3,67},{4,20},{5,69},{6,22},{7,71},{8,24},{9,... | collective-permute-start | bytes 393224 | tf_op jit(solution)/shard_map/ppermute | solution.py:264
  86.9 1.4 %collective-permute-done.30 = f32[128,256]{1,0:T(8,128)S(1)} collective-permute-done((f32[128,256]{1,0:T(8,128)S(1)}, f32[128,256]{1,0:T(8,128)S(1)}, u32[]{:S(2)}, u32[]{:S(2)}) %collective-permute-start.30) | collective-permute-done | bytes 131104 | tf_op jit(solution)/shard_map/ppermute | solution.py:264
  88.4 5.6 %collective-permute-start.31 = (f32[128,256]{1,0:T(8,128)S(1)}, f32[128,256]{1,0:T(8,128)S(1)}, u32[]{:S(2)}, u32[]{:S(2)}) collective-permute-start(f32[128,256]{1,0:T(8,128)S(1)} %rsqrt_multiply_fusion.1.refs_6_), channel_id=1, source_target_pairs={{0,1},{1,0},{2,3},{3,2},{4,5},{5,4},{6,7},{7,6},{8,9},{9,8},{10,11... | collective-permute-start | bytes 393224 | tf_op jit(solution)/shard_map/ppermute | solution.py:276
  95.1 1.6 %collective-permute-start.38 = (f32[128,256]{1,0:T(8,128)S(1)}, f32[128,256]{1,0:T(8,128)S(1)}, u32[]{:S(2)}, u32[]{:S(2)}) collective-permute-start(f32[128,256]{1,0:T(8,128)S(1)} %multiply_select_fusion), channel_id=1, source_target_pairs={{0,1},{1,0},{2,3},{3,2},{4,5},{5,4},{6,7},{7,6},{8,9},{9,8},{10,11... | collective-permute-start | bytes 393224 | tf_op jit(solution)/shard_map/ppermute | solution.py:276
  96.7 1.7 %collective-permute-start.36 = (f32[128,256]{1,0:T(8,128)S(1)}, f32[128,256]{1,0:T(8,128)S(1)}, u32[]{:S(2)}, u32[]{:S(2)}) collective-permute-start(f32[128,256]{1,0:T(8,128)S(1)} %multiply_select_fusion), channel_id=1, source_target_pairs={{0,4},{1,17},{2,6},{3,19},{4,0},{5,21},{6,2},{7,23},{8,12},{9,25},... | collective-permute-start | bytes 393224 | tf_op jit(solution)/shard_map/ppermute | solution.py:264
  99.5 2.9 %collective-permute-done.36 = f32[128,256]{1,0:T(8,128)S(1)} collective-permute-done((f32[128,256]{1,0:T(8,128)S(1)}, f32[128,256]{1,0:T(8,128)S(1)}, u32[]{:S(2)}, u32[]{:S(2)}) %collective-permute-start.36) | collective-permute-done | bytes 131104 | tf_op jit(solution)/shard_map/ppermute | solution.py:264
  102.3 1.4 %collective-permute-done.35 = f32[128,256]{1,0:T(8,128)S(1)} collective-permute-done((f32[128,256]{1,0:T(8,128)S(1)}, f32[128,256]{1,0:T(8,128)S(1)}, u32[]{:S(2)}, u32[]{:S(2)}) %collective-permute-start.35) | collective-permute-done | bytes 131104 | tf_op jit(solution)/shard_map/ppermute | solution.py:264
  103.8 1.6 %collective-permute-start.37 = (f32[128,256]{1,0:T(8,128)S(1)}, f32[128,256]{1,0:T(8,128)S(1)}, u32[]{:S(2)}, u32[]{:S(2)}) collective-permute-start(f32[128,256]{1,0:T(8,128)S(1)} %get-tuple-element.56), channel_id=1, source_target_pairs={{0,1},{1,0},{2,3},{3,2},{4,5},{5,4},{6,7},{7,6},{8,9},{9,8},{10,11... | collective-permute-start | bytes 393224 | tf_op jit(solution)/shard_map/ppermute | solution.py:276
  106.4 6.5 %scaled.1 = (f32[48,256,256]{2,1,0:T(8,128)}, f32[256,128]{1,0:T(8,128)}, f32[256,128]{1,0:T(8,128)}) custom-call(s32[98]{0:T(128)S(1)} %pad_add_fusion.meta_ref, f32[16,256,256]{2,1,0:T(8,128)S(1)} %get-tuple-element.34.refs_0_, f32[16,256,256]{2,1,0:T(8,128)S(1)} %get-tuple-element.39.refs_1_, f32[16,256,256]{2,1,0:T(8,128)S(1)} %get-tuple-element.44.refs_2_, ...), custom_call_target="tpu_custom_call" | custom-call | tf_op jit(solution)/shard_map/scaled/pallas_call | solution.py:367
  (67 shorter events, 27.9 us)
Async XLA Ops:
  8.3 9.2 %collective-permute-start.2 = (f32[16,256,256]{2,1,0:T(8,128)S(1)}, f32[16,256,256]{2,1,0:T(8,128)S(1)}, u32[]{:S(2)}, u32[]{:S(2)}) collective-permute-start(f32[16,256,256]{2,1,0:T(8,128)S(1)} %get-tuple-element.34.refs_0_), channel_id=1, source_target_pairs={{0,1},{1,0},{2,3},{3,2},{4,5},{5,4},{6,7},{7,6},{8,9},{9,8},{10,11... | collective-permute-start | bytes 12582920 | tf_op jit(solution)/shard_map/ppermute | solution.py:276
  8.7 6.0 %collective-permute-start.5 = (f32[128,256]{1,0:T(8,128)S(1)}, f32[128,256]{1,0:T(8,128)S(1)}, u32[]{:S(2)}, u32[]{:S(2)}) collective-permute-start(f32[128,256]{1,0:T(8,128)S(1)} %max.63), channel_id=1, source_target_pairs={{0,16},{1,65},{2,18},{3,67},{4,20},{5,69},{6,22},{7,71},{8,24},{9,... | collective-permute-start | bytes 393224 | tf_op jit(solution)/shard_map/ppermute | solution.py:264
  12.1 5.3 %collective-permute-start.4 = (f32[128,256]{1,0:T(8,128)S(1)}, f32[128,256]{1,0:T(8,128)S(1)}, u32[]{:S(2)}, u32[]{:S(2)}) collective-permute-start(f32[128,256]{1,0:T(8,128)S(1)} %max.63), channel_id=1, source_target_pairs={{0,24},{1,97},{2,26},{3,99},{4,28},{5,101},{6,30},{7,103},{8,16},{... | collective-permute-start | bytes 393224 | tf_op jit(solution)/shard_map/ppermute | solution.py:264
  13.2 4.3 %collective-permute-start.3 = (f32[128,256]{1,0:T(8,128)S(1)}, f32[128,256]{1,0:T(8,128)S(1)}, u32[]{:S(2)}, u32[]{:S(2)}) collective-permute-start(f32[128,256]{1,0:T(8,128)S(1)} %max.63), channel_id=1, source_target_pairs={{0,8},{1,33},{2,10},{3,35},{4,12},{5,37},{6,14},{7,39},{8,0},{9,41... | collective-permute-start | bytes 393224 | tf_op jit(solution)/shard_map/ppermute | solution.py:264
  22.9 9.2 %collective-permute-start.8 = (f32[16,256,256]{2,1,0:T(8,128)S(1)}, f32[16,256,256]{2,1,0:T(8,128)S(1)}, u32[]{:S(2)}, u32[]{:S(2)}) collective-permute-start(f32[16,256,256]{2,1,0:T(8,128)S(1)} %get-tuple-element.39.refs_1_), channel_id=1, source_target_pairs={{0,1},{1,0},{2,3},{3,2},{4,5},{5,4},{6,7},{7,6},{8,9},{9,8},{10,11... | collective-permute-start | bytes 12582920 | tf_op jit(solution)/shard_map/ppermute | solution.py:276
  23.4 5.6 %collective-permute-start.11 = (f32[128,256]{1,0:T(8,128)S(1)}, f32[128,256]{1,0:T(8,128)S(1)}, u32[]{:S(2)}, u32[]{:S(2)}) collective-permute-start(f32[128,256]{1,0:T(8,128)S(1)} %maximum_select_fusion.1), channel_id=1, source_target_pairs={{0,4},{1,17},{2,6},{3,19},{4,0},{5,21},{6,2},{7,23},{8,12},{9,25},... | collective-permute-start | bytes 393224 | tf_op jit(solution)/shard_map/ppermute | solution.py:264
  26.2 5.3 %collective-permute-start.10 = (f32[128,256]{1,0:T(8,128)S(1)}, f32[128,256]{1,0:T(8,128)S(1)}, u32[]{:S(2)}, u32[]{:S(2)}) collective-permute-start(f32[128,256]{1,0:T(8,128)S(1)} %maximum_select_fusion.1), channel_id=1, source_target_pairs={{0,6},{1,25},{2,4},{3,27},{4,2},{5,29},{6,0},{7,31},{8,14},{9,17},... | collective-permute-start | bytes 393224 | tf_op jit(solution)/shard_map/ppermute | solution.py:264
  27.7 4.3 %collective-permute-start.9 = (f32[128,256]{1,0:T(8,128)S(1)}, f32[128,256]{1,0:T(8,128)S(1)}, u32[]{:S(2)}, u32[]{:S(2)}) collective-permute-start(f32[128,256]{1,0:T(8,128)S(1)} %maximum_select_fusion.1), channel_id=1, source_target_pairs={{0,2},{1,9},{2,0},{3,11},{4,6},{5,13},{6,4},{7,15},{8,10},{9,1},{1... | collective-permute-start | bytes 393224 | tf_op jit(solution)/shard_map/ppermute | solution.py:264
  38.7 7.3 %collective-permute-start.14 = (f32[16,256,256]{2,1,0:T(8,128)S(1)}, f32[16,256,256]{2,1,0:T(8,128)S(1)}, u32[]{:S(2)}, u32[]{:S(2)}) collective-permute-start(f32[16,256,256]{2,1,0:T(8,128)S(1)} %get-tuple-element.44.refs_2_), channel_id=1, source_target_pairs={{0,1},{1,0},{2,3},{3,2},{4,5},{5,4},{6,7},{7,6},{8,9},{9,8},{10,11... | collective-permute-start | bytes 12582920 | tf_op jit(solution)/shard_map/ppermute | solution.py:276
  39.1 5.6 %collective-permute-start.17 = (f32[128,256]{1,0:T(8,128)S(1)}, f32[128,256]{1,0:T(8,128)S(1)}, u32[]{:S(2)}, u32[]{:S(2)}) collective-permute-start(f32[128,256]{1,0:T(8,128)S(1)} %maximum_select_fusion), channel_id=1, source_target_pairs={{0,64},{1,5},{2,66},{3,7},{4,68},{5,1},{6,70},{7,3},{8,72},{9,13},... | collective-permute-start | bytes 393224 | tf_op jit(solution)/shard_map/ppermute | solution.py:264
  40.2 5.6 %collective-permute-start.16 = (f32[128,256]{1,0:T(8,128)S(1)}, f32[128,256]{1,0:T(8,128)S(1)}, u32[]{:S(2)}, u32[]{:S(2)}) collective-permute-start(f32[128,256]{1,0:T(8,128)S(1)} %maximum_select_fusion), channel_id=1, source_target_pairs={{0,96},{1,7},{2,98},{3,5},{4,100},{5,3},{6,102},{7,1},{8,104},{9,1... | collective-permute-start | bytes 393224 | tf_op jit(solution)/shard_map/ppermute | solution.py:264
  41.5 4.4 %collective-permute-start.15 = (f32[128,256]{1,0:T(8,128)S(1)}, f32[128,256]{1,0:T(8,128)S(1)}, u32[]{:S(2)}, u32[]{:S(2)}) collective-permute-start(f32[128,256]{1,0:T(8,128)S(1)} %maximum_select_fusion), channel_id=1, source_target_pairs={{0,32},{1,3},{2,34},{3,1},{4,36},{5,7},{6,38},{7,5},{8,40},{9,11},... | collective-permute-start | bytes 393224 | tf_op jit(solution)/shard_map/ppermute | solution.py:264
  41.8 4.2 %collective-permute-start = (s32[98]{0:T(128)S(1)}, s32[98]{0:T(128)S(1)}, u32[]{:S(2)}, u32[]{:S(2)}) collective-permute-start(s32[98]{0:T(128)S(1)} %pad_add_fusion.meta_ref), channel_id=1, source_target_pairs={{0,1},{1,0},{2,3},{3,2},{4,5},{5,4},{6,7},{7,6},{8,9},{9,8},{10,11... | collective-permute-start | bytes 1184 | tf_op jit(solution)/shard_map/ppermute | solution.py:276
  48.6 6.9 %collective-permute-start.19 = (f32[128,256]{1,0:T(8,128)S(1)}, f32[128,256]{1,0:T(8,128)S(1)}, u32[]{:S(2)}, u32[]{:S(2)}) collective-permute-start(f32[128,256]{1,0:T(8,128)S(1)} %chip_both.1), channel_id=1, source_target_pairs={{0,24},{1,97},{2,26},{3,99},{4,28},{5,101},{6,30},{7,103},{8,16},{... | collective-permute-start | bytes 393224 | tf_op jit(solution)/shard_map/ppermute | solution.py:264
  52.1 8.4 %collective-permute-start.20 = (f32[128,256]{1,0:T(8,128)S(1)}, f32[128,256]{1,0:T(8,128)S(1)}, u32[]{:S(2)}, u32[]{:S(2)}) collective-permute-start(f32[128,256]{1,0:T(8,128)S(1)} %chip_both.1), channel_id=1, source_target_pairs={{0,16},{1,65},{2,18},{3,67},{4,20},{5,69},{6,22},{7,71},{8,24},{9,... | collective-permute-start | bytes 393224 | tf_op jit(solution)/shard_map/ppermute | solution.py:264
  52.5 8.0 %collective-permute-start.18 = (f32[128,256]{1,0:T(8,128)S(1)}, f32[128,256]{1,0:T(8,128)S(1)}, u32[]{:S(2)}, u32[]{:S(2)}) collective-permute-start(f32[128,256]{1,0:T(8,128)S(1)} %chip_both.1), channel_id=1, source_target_pairs={{0,8},{1,33},{2,10},{3,35},{4,12},{5,37},{6,14},{7,39},{8,0},{9,41... | collective-permute-start | bytes 393224 | tf_op jit(solution)/shard_map/ppermute | solution.py:264
  55.4 6.1 %collective-permute-start.21 = (f32[128,256]{1,0:T(8,128)S(1)}, f32[128,256]{1,0:T(8,128)S(1)}, u32[]{:S(2)}, u32[]{:S(2)}) collective-permute-start(f32[128,256]{1,0:T(8,128)S(1)} %rsqrt_multiply_fusion.2.refs_6_), channel_id=1, source_target_pairs={{0,1},{1,0},{2,3},{3,2},{4,5},{5,4},{6,7},{7,6},{8,9},{9,8},{10,11... | collective-permute-start | bytes 393224 | tf_op jit(solution)/shard_map/ppermute | solution.py:276
  64.0 5.7 %collective-permute-start.25 = (f32[128,256]{1,0:T(8,128)S(1)}, f32[128,256]{1,0:T(8,128)S(1)}, u32[]{:S(2)}, u32[]{:S(2)}) collective-permute-start(f32[128,256]{1,0:T(8,128)S(1)} %chip_rows.1), channel_id=1, source_target_pairs={{0,4},{1,17},{2,6},{3,19},{4,0},{5,21},{6,2},{7,23},{8,12},{9,25},... | collective-permute-start | bytes 393224 | tf_op jit(solution)/shard_map/ppermute | solution.py:264
  64.1 7.8 %collective-permute-start.24 = (f32[128,256]{1,0:T(8,128)S(1)}, f32[128,256]{1,0:T(8,128)S(1)}, u32[]{:S(2)}, u32[]{:S(2)}) collective-permute-start(f32[128,256]{1,0:T(8,128)S(1)} %chip_rows.1), channel_id=1, source_target_pairs={{0,6},{1,25},{2,4},{3,27},{4,2},{5,29},{6,0},{7,31},{8,14},{9,17},... | collective-permute-start | bytes 393224 | tf_op jit(solution)/shard_map/ppermute | solution.py:264
  68.6 4.3 %collective-permute-start.23 = (f32[128,256]{1,0:T(8,128)S(1)}, f32[128,256]{1,0:T(8,128)S(1)}, u32[]{:S(2)}, u32[]{:S(2)}) collective-permute-start(f32[128,256]{1,0:T(8,128)S(1)} %chip_rows.1), channel_id=1, source_target_pairs={{0,2},{1,9},{2,0},{3,11},{4,6},{5,13},{6,4},{7,15},{8,10},{9,1},{1... | collective-permute-start | bytes 393224 | tf_op jit(solution)/shard_map/ppermute | solution.py:264
  69.1 9.1 %collective-permute-start.22 = (f32[128,256]{1,0:T(8,128)S(1)}, f32[128,256]{1,0:T(8,128)S(1)}, u32[]{:S(2)}, u32[]{:S(2)}) collective-permute-start(f32[128,256]{1,0:T(8,128)S(1)} %multiply_select_fusion.2.refs_6_), channel_id=1, source_target_pairs={{0,1},{1,0},{2,3},{3,2},{4,5},{5,4},{6,7},{7,6},{8,9},{9,8},{10,11... | collective-permute-start | bytes 393224 | tf_op jit(solution)/shard_map/ppermute | solution.py:276
  73.5 5.7 %collective-permute-start.29 = (f32[128,256]{1,0:T(8,128)S(1)}, f32[128,256]{1,0:T(8,128)S(1)}, u32[]{:S(2)}, u32[]{:S(2)}) collective-permute-start(f32[128,256]{1,0:T(8,128)S(1)} %chip_cols.1), channel_id=1, source_target_pairs={{0,64},{1,5},{2,66},{3,7},{4,68},{5,1},{6,70},{7,3},{8,72},{9,13},... | collective-permute-start | bytes 393224 | tf_op jit(solution)/shard_map/ppermute | solution.py:264
  73.6 6.7 %collective-permute-start.28 = (f32[128,256]{1,0:T(8,128)S(1)}, f32[128,256]{1,0:T(8,128)S(1)}, u32[]{:S(2)}, u32[]{:S(2)}) collective-permute-start(f32[128,256]{1,0:T(8,128)S(1)} %chip_cols.1), channel_id=1, source_target_pairs={{0,96},{1,7},{2,98},{3,5},{4,100},{5,3},{6,102},{7,1},{8,104},{9,1... | collective-permute-start | bytes 393224 | tf_op jit(solution)/shard_map/ppermute | solution.py:264
  74.1 6.2 %collective-permute-start.27 = (f32[128,256]{1,0:T(8,128)S(1)}, f32[128,256]{1,0:T(8,128)S(1)}, u32[]{:S(2)}, u32[]{:S(2)}) collective-permute-start(f32[128,256]{1,0:T(8,128)S(1)} %chip_cols.1), channel_id=1, source_target_pairs={{0,32},{1,3},{2,34},{3,1},{4,36},{5,7},{6,38},{7,5},{8,40},{9,11},... | collective-permute-start | bytes 393224 | tf_op jit(solution)/shard_map/ppermute | solution.py:264
  83.3 5.1 %collective-permute-start.30 = (f32[128,256]{1,0:T(8,128)S(1)}, f32[128,256]{1,0:T(8,128)S(1)}, u32[]{:S(2)}, u32[]{:S(2)}) collective-permute-start(f32[128,256]{1,0:T(8,128)S(1)} %chip_sums.1), channel_id=1, source_target_pairs={{0,24},{1,97},{2,26},{3,99},{4,28},{5,101},{6,30},{7,103},{8,16},{... | collective-permute-start | bytes 393224 | tf_op jit(solution)/shard_map/ppermute | solution.py:264
  84.9 9.2 %collective-permute-start.33 = (f32[128,256]{1,0:T(8,128)S(1)}, f32[128,256]{1,0:T(8,128)S(1)}, u32[]{:S(2)}, u32[]{:S(2)}) collective-permute-start(f32[128,256]{1,0:T(8,128)S(1)} %chip_sums.1), channel_id=1, source_target_pairs={{0,16},{1,65},{2,18},{3,67},{4,20},{5,69},{6,22},{7,71},{8,24},{9,... | collective-permute-start | bytes 393224 | tf_op jit(solution)/shard_map/ppermute | solution.py:264
  86.9 7.1 %collective-permute-start.32 = (f32[128,256]{1,0:T(8,128)S(1)}, f32[128,256]{1,0:T(8,128)S(1)}, u32[]{:S(2)}, u32[]{:S(2)}) collective-permute-start(f32[128,256]{1,0:T(8,128)S(1)} %chip_sums.1), channel_id=1, source_target_pairs={{0,8},{1,33},{2,10},{3,35},{4,12},{5,37},{6,14},{7,39},{8,0},{9,41... | collective-permute-start | bytes 393224 | tf_op jit(solution)/shard_map/ppermute | solution.py:264
  88.4 6.6 %collective-permute-start.31 = (f32[128,256]{1,0:T(8,128)S(1)}, f32[128,256]{1,0:T(8,128)S(1)}, u32[]{:S(2)}, u32[]{:S(2)}) collective-permute-start(f32[128,256]{1,0:T(8,128)S(1)} %rsqrt_multiply_fusion.1.refs_6_), channel_id=1, source_target_pairs={{0,1},{1,0},{2,3},{3,2},{4,5},{5,4},{6,7},{7,6},{8,9},{9,8},{10,11... | collective-permute-start | bytes 393224 | tf_op jit(solution)/shard_map/ppermute | solution.py:276
  95.1 4.4 %collective-permute-start.38 = (f32[128,256]{1,0:T(8,128)S(1)}, f32[128,256]{1,0:T(8,128)S(1)}, u32[]{:S(2)}, u32[]{:S(2)}) collective-permute-start(f32[128,256]{1,0:T(8,128)S(1)} %multiply_select_fusion), channel_id=1, source_target_pairs={{0,1},{1,0},{2,3},{3,2},{4,5},{5,4},{6,7},{7,6},{8,9},{9,8},{10,11... | collective-permute-start | bytes 393224 | tf_op jit(solution)/shard_map/ppermute | solution.py:276
  96.7 5.6 %collective-permute-start.36 = (f32[128,256]{1,0:T(8,128)S(1)}, f32[128,256]{1,0:T(8,128)S(1)}, u32[]{:S(2)}, u32[]{:S(2)}) collective-permute-start(f32[128,256]{1,0:T(8,128)S(1)} %multiply_select_fusion), channel_id=1, source_target_pairs={{0,4},{1,17},{2,6},{3,19},{4,0},{5,21},{6,2},{7,23},{8,12},{9,25},... | collective-permute-start | bytes 393224 | tf_op jit(solution)/shard_map/ppermute | solution.py:264
  98.5 5.3 %collective-permute-start.35 = (f32[128,256]{1,0:T(8,128)S(1)}, f32[128,256]{1,0:T(8,128)S(1)}, u32[]{:S(2)}, u32[]{:S(2)}) collective-permute-start(f32[128,256]{1,0:T(8,128)S(1)} %multiply_select_fusion), channel_id=1, source_target_pairs={{0,6},{1,25},{2,4},{3,27},{4,2},{5,29},{6,0},{7,31},{8,14},{9,17},... | collective-permute-start | bytes 393224 | tf_op jit(solution)/shard_map/ppermute | solution.py:264
  98.9 4.9 %collective-permute-start.34 = (f32[128,256]{1,0:T(8,128)S(1)}, f32[128,256]{1,0:T(8,128)S(1)}, u32[]{:S(2)}, u32[]{:S(2)}) collective-permute-start(f32[128,256]{1,0:T(8,128)S(1)} %multiply_select_fusion), channel_id=1, source_target_pairs={{0,2},{1,9},{2,0},{3,11},{4,6},{5,13},{6,4},{7,15},{8,10},{9,1},{1... | collective-permute-start | bytes 393224 | tf_op jit(solution)/shard_map/ppermute | solution.py:264
  (7 other events, 18.9 us)

commit v6 on v5

--- a/solution.py
+++ b/solution.py
@@ -12,7 +12,7 @@
 EPS = 1e-06
 AXES = ("row", "col", "depth")
 LOAD_GROUP = 4
-SWEEP_GROUP = 16
+SWEEP_GROUP = 8
 CHIP_GROUP = 8
 COPY_GROUP = 4
 PIECES = 3

time: 113 us -> 113 us (level)
  starting transfers between devices: 57.5 us -> 54.3 us
  waiting for transfers between devices: 31.9 us -> 33.6 us
  Pallas kernels: 20.8 us -> 22 us
    ppermute x15, starting transfers between devices: 27.1 us -> 19 us  [shards(): swap = lambda v: lax.ppermute(v, 'depth', [(0, 1), (1, 0)])]
    ppermute x24, starting transfers between devices: 30.4 us -> 35.3 us  [slot(): parts.append(lax.ppermute(v, AXES, spots(move)))]
  transfers between devices with their start and end apart: 39 -> 39, of which waited for: 24 -> 22; matrix products, arithmetic and copies ran while one was open for 0% -> 0% of each run, Pallas kernels for 0% -> 0%
where the time goes in v6:
time: 113 us
  starting transfers between devices  54.3 us (48%)
  waiting for transfers between devices  33.6 us (30%)
  Pallas kernels  22 us (19%)
  between operations  1.65 us (1%)
  other arithmetic  1.36 us (1%)
    ppermute x24, starting transfers between devices, slot(): parts.append(lax.ppermute(v, AXES, spots(move)))  35.3 us
    ppermute x24, waiting for transfers between devices, slot(): parts.append(lax.ppermute(v, AXES, spots(move)))  24.7 us
    ppermute x15, starting transfers between devices, shards(): swap = lambda v: lax.ppermute(v, 'depth', [(0, 1), (1, 0)])  19 us
    ppermute x15, waiting for transfers between devices, shards(): swap = lambda v: lax.ppermute(v, 'depth', [(0, 1), (1, 0)])  8.9 us
    pallas_call x4, Pallas kernels, chip(): pl.pallas_call(functools.partial(chip_kernel, slots, part_slots, kinds, s...  8.22 us
    pallas_call x1, Pallas kernels, shards(): pl.pallas_call(functools.partial(final_kernel, slots, part_slots), out_sh...  6.45 us
    pallas_call x1, Pallas kernels, shards(): pl.pallas_call(functools.partial(load_kernel, slots, part_slots), out_sha...  4.07 us
    pallas_call x2, Pallas kernels, run(): pl.pallas_call(functools.partial(kernel, slots, part_slots), out_shape=(v...  3.31 us
  transfers between devices with their start and end apart: 39, of which 22 were waited for; matrix products, arithmetic and copies ran while one was open for 0% of the time, Pallas kernels for 0%

profile of v6, /device:TPU:1, one launch (start us, length us, event | category | flops | bytes accessed | tf_op | source)
XLA Modules:
  0.0 112.9 jit_solution(3081776249566435925)
XLA Ops:
  2.0 4.1 %load.1 = (f32[16,256,256]{2,1,0:T(8,128)S(1)}, f32[16,256,256]{2,1,0:T(8,128)S(1)}, f32[16,256,256]{2,1,0:T(8,128)S(1)}, f32[128,256]{1,0:T(8,128)S(1)}, f32[12...) custom-call(s32[98]{0:T(128)S(1)} %pad_add_fusion.meta_ref, f32[48,256,256]{2,1,0:T(8,128)} %bitcast.9), custom_call_target="tpu_custom_call" | custom-call | tf_op jit(solution)/shard_map/load/pallas_call | solution.py:281
  8.4 6.1 %collective-permute-start.5 = (f32[128,256]{1,0:T(8,128)S(1)}, f32[128,256]{1,0:T(8,128)S(1)}, u32[]{:S(2)}, u32[]{:S(2)}) collective-permute-start(f32[128,256]{1,0:T(8,128)S(1)} %max.63), channel_id=1, source_target_pairs={{0,16},{1,65},{2,18},{3,67},{4,20},{5,69},{6,22},{7,71},{8,24},{9,... | collective-permute-start | bytes 393224 | tf_op jit(solution)/shard_map/ppermute | solution.py:264
  14.5 2.3 %collective-permute-done.5 = f32[128,256]{1,0:T(8,128)S(1)} collective-permute-done((f32[128,256]{1,0:T(8,128)S(1)}, f32[128,256]{1,0:T(8,128)S(1)}, u32[]{:S(2)}, u32[]{:S(2)}) %collective-permute-start.5) | collective-permute-done | bytes 131104 | tf_op jit(solution)/shard_map/ppermute | solution.py:264
  16.9 2.7 %collective-permute-done.4 = f32[128,256]{1,0:T(8,128)S(1)} collective-permute-done((f32[128,256]{1,0:T(8,128)S(1)}, f32[128,256]{1,0:T(8,128)S(1)}, u32[]{:S(2)}, u32[]{:S(2)}) %collective-permute-start.4) | collective-permute-done | bytes 131104 | tf_op jit(solution)/shard_map/ppermute | solution.py:264
  21.1 1.7 %rows.1 = (f32[128,256]{1,0:T(8,128)S(1)}, f32[128,256]{1,0:T(8,128)S(1)}) custom-call(s32[98]{0:T(128)S(1)} %pad_add_fusion.meta_ref, f32[16,256,256]{2,1,0:T(8,128)S(1)} %get-tuple-element.34.refs_0_, f32[16,256,256]{2,1,0:T(8,128)S(1)} %get-tuple-element.39.refs_1_, f32[16,256,256]{2,1,0:T(8,128)S(1)} %get-tuple-element.44.refs_2_, ...), custom_call_target="tpu_custom_call" | custom-call | tf_op jit(solution)/shard_map/rows/pallas_call | solution.py:307
  24.4 1.9 %collective-permute-start.11 = (f32[128,256]{1,0:T(8,128)S(1)}, f32[128,256]{1,0:T(8,128)S(1)}, u32[]{:S(2)}, u32[]{:S(2)}) collective-permute-start(f32[128,256]{1,0:T(8,128)S(1)} %maximum_select_fusion.1), channel_id=1, source_target_pairs={{0,4},{1,17},{2,6},{3,19},{4,0},{5,21},{6,2},{7,23},{8,12},{9,25},... | collective-permute-start | bytes 393224 | tf_op jit(solution)/shard_map/ppermute | solution.py:264
  27.1 3.0 %collective-permute-done.11 = f32[128,256]{1,0:T(8,128)S(1)} collective-permute-done((f32[128,256]{1,0:T(8,128)S(1)}, f32[128,256]{1,0:T(8,128)S(1)}, u32[]{:S(2)}, u32[]{:S(2)}) %collective-permute-start.11) | collective-permute-done | bytes 131104 | tf_op jit(solution)/shard_map/ppermute | solution.py:264
  30.0 1.6 %collective-permute-done.10 = f32[128,256]{1,0:T(8,128)S(1)} collective-permute-done((f32[128,256]{1,0:T(8,128)S(1)}, f32[128,256]{1,0:T(8,128)S(1)}, u32[]{:S(2)}, u32[]{:S(2)}) %collective-permute-start.10) | collective-permute-done | bytes 131104 | tf_op jit(solution)/shard_map/ppermute | solution.py:264
  31.7 1.8 %collective-permute-start.12 = (f32[128,256]{1,0:T(8,128)S(1)}, f32[128,256]{1,0:T(8,128)S(1)}, u32[]{:S(2)}, u32[]{:S(2)}) collective-permute-start(f32[128,256]{1,0:T(8,128)S(1)} %rsqrt_select_fusion.refs_3_), channel_id=1, source_target_pairs={{0,1},{1,0},{2,3},{3,2},{4,5},{5,4},{6,7},{7,6},{8,9},{9,8},{10,11... | collective-permute-start | bytes 393224 | tf_op jit(solution)/shard_map/ppermute | solution.py:276
  34.5 1.7 %cols.1 = (f32[128,256]{1,0:T(8,128)S(1)}, f32[128,256]{1,0:T(8,128)S(1)}) custom-call(s32[98]{0:T(128)S(1)} %pad_add_fusion.meta_ref, f32[16,256,256]{2,1,0:T(8,128)S(1)} %get-tuple-element.34.refs_0_, f32[16,256,256]{2,1,0:T(8,128)S(1)} %get-tuple-element.39.refs_1_, f32[16,256,256]{2,1,0:T(8,128)S(1)} %get-tuple-element.44.refs_2_, ...), custom_call_target="tpu_custom_call" | custom-call | tf_op jit(solution)/shard_map/cols/pallas_call | solution.py:307
  37.9 2.0 %collective-permute-start.17 = (f32[128,256]{1,0:T(8,128)S(1)}, f32[128,256]{1,0:T(8,128)S(1)}, u32[]{:S(2)}, u32[]{:S(2)}) collective-permute-start(f32[128,256]{1,0:T(8,128)S(1)} %maximum_select_fusion), channel_id=1, source_target_pairs={{0,64},{1,5},{2,66},{3,7},{4,68},{5,1},{6,70},{7,3},{8,72},{9,13},... | collective-permute-start | bytes 393224 | tf_op jit(solution)/shard_map/ppermute | solution.py:264
  41.5 3.3 %collective-permute-start = (s32[98]{0:T(128)S(1)}, s32[98]{0:T(128)S(1)}, u32[]{:S(2)}, u32[]{:S(2)}) collective-permute-start(s32[98]{0:T(128)S(1)} %pad_add_fusion.meta_ref), channel_id=1, source_target_pairs={{0,1},{1,0},{2,3},{3,2},{4,5},{5,4},{6,7},{7,6},{8,9},{9,8},{10,11... | collective-permute-start | bytes 1184 | tf_op jit(solution)/shard_map/ppermute | solution.py:276
  45.7 2.6 %chip_both.1 = f32[128,256]{1,0:T(8,128)S(1)} custom-call(s32[98]{0:T(128)S(1)} %pad_add_fusion.meta_ref, s32[98]{0:T(128)S(1)} %collective-permute-done.twin_ref, f32[16,256,256]{2,1,0:T(8,128)S(1)} %get-tuple-element.34.refs_0_, f32[16,256,256]{2,1,0:T(8,128)S(1)} %get-tuple-element.39.refs_1_, f32[16,256,256]{2,1,0:T(8,128)S(1)} %get-tuple-element.44.refs_2_, ...), custom_call_target="tpu_custom_call" | custom-call | tf_op jit(solution)/shard_map/chip_both/pallas_call | solution.py:318
  48.3 5.5 %collective-permute-start.19 = (f32[128,256]{1,0:T(8,128)S(1)}, f32[128,256]{1,0:T(8,128)S(1)}, u32[]{:S(2)}, u32[]{:S(2)}) collective-permute-start(f32[128,256]{1,0:T(8,128)S(1)} %chip_both.1), channel_id=1, source_target_pairs={{0,24},{1,97},{2,26},{3,99},{4,28},{5,101},{6,30},{7,103},{8,16},{... | collective-permute-start | bytes 393224 | tf_op jit(solution)/shard_map/ppermute | solution.py:264
  54.5 2.6 %collective-permute-done.19 = f32[128,256]{1,0:T(8,128)S(1)} collective-permute-done((f32[128,256]{1,0:T(8,128)S(1)}, f32[128,256]{1,0:T(8,128)S(1)}, u32[]{:S(2)}, u32[]{:S(2)}) %collective-permute-start.19) | collective-permute-done | bytes 131104 | tf_op jit(solution)/shard_map/ppermute | solution.py:264
  57.1 2.0 %collective-permute-start.21 = (f32[128,256]{1,0:T(8,128)S(1)}, f32[128,256]{1,0:T(8,128)S(1)}, u32[]{:S(2)}, u32[]{:S(2)}) collective-permute-start(f32[128,256]{1,0:T(8,128)S(1)} %rsqrt_multiply_fusion.2.refs_6_), channel_id=1, source_target_pairs={{0,1},{1,0},{2,3},{3,2},{4,5},{5,4},{6,7},{7,6},{8,9},{9,8},{10,11... | collective-permute-start | bytes 393224 | tf_op jit(solution)/shard_map/ppermute | solution.py:276
  60.1 2.4 %chip_rows.1 = f32[128,256]{1,0:T(8,128)S(1)} custom-call(s32[98]{0:T(128)S(1)} %pad_add_fusion.meta_ref, s32[98]{0:T(128)S(1)} %collective-permute-done.twin_ref, f32[16,256,256]{2,1,0:T(8,128)S(1)} %get-tuple-element.34.refs_0_, f32[16,256,256]{2,1,0:T(8,128)S(1)} %get-tuple-element.39.refs_1_, f32[16,256,256]{2,1,0:T(8,128)S(1)} %get-tuple-element.44.refs_2_, ...), custom_call_target="tpu_custom_call" | custom-call | tf_op jit(solution)/shard_map/chip_rows/pallas_call | solution.py:318
  63.8 1.7 %collective-permute-start.24 = (f32[128,256]{1,0:T(8,128)S(1)}, f32[128,256]{1,0:T(8,128)S(1)}, u32[]{:S(2)}, u32[]{:S(2)}) collective-permute-start(f32[128,256]{1,0:T(8,128)S(1)} %chip_rows.1), channel_id=1, source_target_pairs={{0,6},{1,25},{2,4},{3,27},{4,2},{5,29},{6,0},{7,31},{8,14},{9,17},... | collective-permute-start | bytes 393224 | tf_op jit(solution)/shard_map/ppermute | solution.py:264
  65.5 1.6 %collective-permute-start.22 = (f32[128,256]{1,0:T(8,128)S(1)}, f32[128,256]{1,0:T(8,128)S(1)}, u32[]{:S(2)}, u32[]{:S(2)}) collective-permute-start(f32[128,256]{1,0:T(8,128)S(1)} %multiply_select_fusion.2.refs_6_), channel_id=1, source_target_pairs={{0,1},{1,0},{2,3},{3,2},{4,5},{5,4},{6,7},{7,6},{8,9},{9,8},{10,11... | collective-permute-start | bytes 393224 | tf_op jit(solution)/shard_map/ppermute | solution.py:276
  68.2 1.4 %collective-permute-done.24 = f32[128,256]{1,0:T(8,128)S(1)} collective-permute-done((f32[128,256]{1,0:T(8,128)S(1)}, f32[128,256]{1,0:T(8,128)S(1)}, u32[]{:S(2)}, u32[]{:S(2)}) %collective-permute-start.24) | collective-permute-done | bytes 131104 | tf_op jit(solution)/shard_map/ppermute | solution.py:264
  70.3 4.0 %collective-permute-start.29 = (f32[128,256]{1,0:T(8,128)S(1)}, f32[128,256]{1,0:T(8,128)S(1)}, u32[]{:S(2)}, u32[]{:S(2)}) collective-permute-start(f32[128,256]{1,0:T(8,128)S(1)} %chip_cols.1), channel_id=1, source_target_pairs={{0,64},{1,5},{2,66},{3,7},{4,68},{5,1},{6,70},{7,3},{8,72},{9,13},... | collective-permute-start | bytes 393224 | tf_op jit(solution)/shard_map/ppermute | solution.py:264
  74.3 2.2 %collective-permute-start.28 = (f32[128,256]{1,0:T(8,128)S(1)}, f32[128,256]{1,0:T(8,128)S(1)}, u32[]{:S(2)}, u32[]{:S(2)}) collective-permute-start(f32[128,256]{1,0:T(8,128)S(1)} %chip_cols.1), channel_id=1, source_target_pairs={{0,96},{1,7},{2,98},{3,5},{4,100},{5,3},{6,102},{7,1},{8,104},{9,1... | collective-permute-start | bytes 393224 | tf_op jit(solution)/shard_map/ppermute | solution.py:264
  77.8 2.0 %collective-permute-done.28 = f32[128,256]{1,0:T(8,128)S(1)} collective-permute-done((f32[128,256]{1,0:T(8,128)S(1)}, f32[128,256]{1,0:T(8,128)S(1)}, u32[]{:S(2)}, u32[]{:S(2)}) %collective-permute-start.28) | collective-permute-done | bytes 131104 | tf_op jit(solution)/shard_map/ppermute | solution.py:264
  81.2 2.6 %chip_sums.1 = f32[128,256]{1,0:T(8,128)S(1)} custom-call(s32[98]{0:T(128)S(1)} %pad_add_fusion.meta_ref, s32[98]{0:T(128)S(1)} %collective-permute-done.twin_ref, f32[16,256,256]{2,1,0:T(8,128)S(1)} %get-tuple-element.34.refs_0_, f32[16,256,256]{2,1,0:T(8,128)S(1)} %get-tuple-element.39.refs_1_, f32[16,256,256]{2,1,0:T(8,128)S(1)} %get-tuple-element.44.refs_2_, ...), custom_call_target="tpu_custom_call" | custom-call | tf_op jit(solution)/shard_map/chip_sums/pallas_call | solution.py:318
  83.8 2.7 %collective-permute-start.30 = (f32[128,256]{1,0:T(8,128)S(1)}, f32[128,256]{1,0:T(8,128)S(1)}, u32[]{:S(2)}, u32[]{:S(2)}) collective-permute-start(f32[128,256]{1,0:T(8,128)S(1)} %chip_sums.1), channel_id=1, source_target_pairs={{0,24},{1,97},{2,26},{3,99},{4,28},{5,101},{6,30},{7,103},{8,16},{... | collective-permute-start | bytes 393224 | tf_op jit(solution)/shard_map/ppermute | solution.py:264
  86.6 1.6 %collective-permute-start.33 = (f32[128,256]{1,0:T(8,128)S(1)}, f32[128,256]{1,0:T(8,128)S(1)}, u32[]{:S(2)}, u32[]{:S(2)}) collective-permute-start(f32[128,256]{1,0:T(8,128)S(1)} %chip_sums.1), channel_id=1, source_target_pairs={{0,16},{1,65},{2,18},{3,67},{4,20},{5,69},{6,22},{7,71},{8,24},{9,... | collective-permute-start | bytes 393224 | tf_op jit(solution)/shard_map/ppermute | solution.py:264
  88.2 1.7 %collective-permute-done.30 = f32[128,256]{1,0:T(8,128)S(1)} collective-permute-done((f32[128,256]{1,0:T(8,128)S(1)}, f32[128,256]{1,0:T(8,128)S(1)}, u32[]{:S(2)}, u32[]{:S(2)}) %collective-permute-start.30) | collective-permute-done | bytes 131104 | tf_op jit(solution)/shard_map/ppermute | solution.py:264
  89.9 3.0 %collective-permute-start.31 = (f32[128,256]{1,0:T(8,128)S(1)}, f32[128,256]{1,0:T(8,128)S(1)}, u32[]{:S(2)}, u32[]{:S(2)}) collective-permute-start(f32[128,256]{1,0:T(8,128)S(1)} %rsqrt_multiply_fusion.1.refs_6_), channel_id=1, source_target_pairs={{0,1},{1,0},{2,3},{3,2},{4,5},{5,4},{6,7},{7,6},{8,9},{9,8},{10,11... | collective-permute-start | bytes 393224 | tf_op jit(solution)/shard_map/ppermute | solution.py:276
  95.3 1.8 %collective-permute-start.36 = (f32[128,256]{1,0:T(8,128)S(1)}, f32[128,256]{1,0:T(8,128)S(1)}, u32[]{:S(2)}, u32[]{:S(2)}) collective-permute-start(f32[128,256]{1,0:T(8,128)S(1)} %multiply_select_fusion), channel_id=1, source_target_pairs={{0,4},{1,17},{2,6},{3,19},{4,0},{5,21},{6,2},{7,23},{8,12},{9,25},... | collective-permute-start | bytes 393224 | tf_op jit(solution)/shard_map/ppermute | solution.py:264
  98.1 2.9 %collective-permute-done.36 = f32[128,256]{1,0:T(8,128)S(1)} collective-permute-done((f32[128,256]{1,0:T(8,128)S(1)}, f32[128,256]{1,0:T(8,128)S(1)}, u32[]{:S(2)}, u32[]{:S(2)}) %collective-permute-start.36) | collective-permute-done | bytes 131104 | tf_op jit(solution)/shard_map/ppermute | solution.py:264
  102.2 3.1 %collective-permute-start.37 = (f32[128,256]{1,0:T(8,128)S(1)}, f32[128,256]{1,0:T(8,128)S(1)}, u32[]{:S(2)}, u32[]{:S(2)}) collective-permute-start(f32[128,256]{1,0:T(8,128)S(1)} %get-tuple-element.56), channel_id=1, source_target_pairs={{0,1},{1,0},{2,3},{3,2},{4,5},{5,4},{6,7},{7,6},{8,9},{9,8},{10,11... | collective-permute-start | bytes 393224 | tf_op jit(solution)/shard_map/ppermute | solution.py:276
  106.3 6.5 %scaled.1 = (f32[48,256,256]{2,1,0:T(8,128)}, f32[256,128]{1,0:T(8,128)}, f32[256,128]{1,0:T(8,128)}) custom-call(s32[98]{0:T(128)S(1)} %pad_add_fusion.meta_ref, f32[16,256,256]{2,1,0:T(8,128)S(1)} %get-tuple-element.34.refs_0_, f32[16,256,256]{2,1,0:T(8,128)S(1)} %get-tuple-element.39.refs_1_, f32[16,256,256]{2,1,0:T(8,128)S(1)} %get-tuple-element.44.refs_2_, ...), custom_call_target="tpu_custom_call" | custom-call | tf_op jit(solution)/shard_map/scaled/pallas_call | solution.py:367
  (67 shorter events, 25.3 us)
Async XLA Ops:
  8.0 11.6 %collective-permute-start.2 = (f32[16,256,256]{2,1,0:T(8,128)S(1)}, f32[16,256,256]{2,1,0:T(8,128)S(1)}, u32[]{:S(2)}, u32[]{:S(2)}) collective-permute-start(f32[16,256,256]{2,1,0:T(8,128)S(1)} %get-tuple-element.34.refs_0_), channel_id=1, source_target_pairs={{0,1},{1,0},{2,3},{3,2},{4,5},{5,4},{6,7},{7,6},{8,9},{9,8},{10,11... | collective-permute-start | bytes 12582920 | tf_op jit(solution)/shard_map/ppermute | solution.py:276
  8.4 8.4 %collective-permute-start.5 = (f32[128,256]{1,0:T(8,128)S(1)}, f32[128,256]{1,0:T(8,128)S(1)}, u32[]{:S(2)}, u32[]{:S(2)}) collective-permute-start(f32[128,256]{1,0:T(8,128)S(1)} %max.63), channel_id=1, source_target_pairs={{0,16},{1,65},{2,18},{3,67},{4,20},{5,69},{6,22},{7,71},{8,24},{9,... | collective-permute-start | bytes 393224 | tf_op jit(solution)/shard_map/ppermute | solution.py:264
  14.5 5.0 %collective-permute-start.4 = (f32[128,256]{1,0:T(8,128)S(1)}, f32[128,256]{1,0:T(8,128)S(1)}, u32[]{:S(2)}, u32[]{:S(2)}) collective-permute-start(f32[128,256]{1,0:T(8,128)S(1)} %max.63), channel_id=1, source_target_pairs={{0,24},{1,97},{2,26},{3,99},{4,28},{5,101},{6,30},{7,103},{8,16},{... | collective-permute-start | bytes 393224 | tf_op jit(solution)/shard_map/ppermute | solution.py:264
  14.5 5.0 %collective-permute-start.3 = (f32[128,256]{1,0:T(8,128)S(1)}, f32[128,256]{1,0:T(8,128)S(1)}, u32[]{:S(2)}, u32[]{:S(2)}) collective-permute-start(f32[128,256]{1,0:T(8,128)S(1)} %max.63), channel_id=1, source_target_pairs={{0,8},{1,33},{2,10},{3,35},{4,12},{5,37},{6,14},{7,39},{8,0},{9,41... | collective-permute-start | bytes 393224 | tf_op jit(solution)/shard_map/ppermute | solution.py:264
  24.2 7.5 %collective-permute-start.8 = (f32[16,256,256]{2,1,0:T(8,128)S(1)}, f32[16,256,256]{2,1,0:T(8,128)S(1)}, u32[]{:S(2)}, u32[]{:S(2)}) collective-permute-start(f32[16,256,256]{2,1,0:T(8,128)S(1)} %get-tuple-element.39.refs_1_), channel_id=1, source_target_pairs={{0,1},{1,0},{2,3},{3,2},{4,5},{5,4},{6,7},{7,6},{8,9},{9,8},{10,11... | collective-permute-start | bytes 12582920 | tf_op jit(solution)/shard_map/ppermute | solution.py:276
  24.4 5.6 %collective-permute-start.11 = (f32[128,256]{1,0:T(8,128)S(1)}, f32[128,256]{1,0:T(8,128)S(1)}, u32[]{:S(2)}, u32[]{:S(2)}) collective-permute-start(f32[128,256]{1,0:T(8,128)S(1)} %maximum_select_fusion.1), channel_id=1, source_target_pairs={{0,4},{1,17},{2,6},{3,19},{4,0},{5,21},{6,2},{7,23},{8,12},{9,25},... | collective-permute-start | bytes 393224 | tf_op jit(solution)/shard_map/ppermute | solution.py:264
  26.3 5.3 %collective-permute-start.10 = (f32[128,256]{1,0:T(8,128)S(1)}, f32[128,256]{1,0:T(8,128)S(1)}, u32[]{:S(2)}, u32[]{:S(2)}) collective-permute-start(f32[128,256]{1,0:T(8,128)S(1)} %maximum_select_fusion.1), channel_id=1, source_target_pairs={{0,6},{1,25},{2,4},{3,27},{4,2},{5,29},{6,0},{7,31},{8,14},{9,17},... | collective-permute-start | bytes 393224 | tf_op jit(solution)/shard_map/ppermute | solution.py:264
  26.7 4.9 %collective-permute-start.9 = (f32[128,256]{1,0:T(8,128)S(1)}, f32[128,256]{1,0:T(8,128)S(1)}, u32[]{:S(2)}, u32[]{:S(2)}) collective-permute-start(f32[128,256]{1,0:T(8,128)S(1)} %maximum_select_fusion.1), channel_id=1, source_target_pairs={{0,2},{1,9},{2,0},{3,11},{4,6},{5,13},{6,4},{7,15},{8,10},{9,1},{1... | collective-permute-start | bytes 393224 | tf_op jit(solution)/shard_map/ppermute | solution.py:264
  37.6 8.0 %collective-permute-start.14 = (f32[16,256,256]{2,1,0:T(8,128)S(1)}, f32[16,256,256]{2,1,0:T(8,128)S(1)}, u32[]{:S(2)}, u32[]{:S(2)}) collective-permute-start(f32[16,256,256]{2,1,0:T(8,128)S(1)} %get-tuple-element.44.refs_2_), channel_id=1, source_target_pairs={{0,1},{1,0},{2,3},{3,2},{4,5},{5,4},{6,7},{7,6},{8,9},{9,8},{10,11... | collective-permute-start | bytes 12582920 | tf_op jit(solution)/shard_map/ppermute | solution.py:276
  37.9 6.9 %collective-permute-start.17 = (f32[128,256]{1,0:T(8,128)S(1)}, f32[128,256]{1,0:T(8,128)S(1)}, u32[]{:S(2)}, u32[]{:S(2)}) collective-permute-start(f32[128,256]{1,0:T(8,128)S(1)} %maximum_select_fusion), channel_id=1, source_target_pairs={{0,64},{1,5},{2,66},{3,7},{4,68},{5,1},{6,70},{7,3},{8,72},{9,13},... | collective-permute-start | bytes 393224 | tf_op jit(solution)/shard_map/ppermute | solution.py:264
  39.8 5.3 %collective-permute-start.16 = (f32[128,256]{1,0:T(8,128)S(1)}, f32[128,256]{1,0:T(8,128)S(1)}, u32[]{:S(2)}, u32[]{:S(2)}) collective-permute-start(f32[128,256]{1,0:T(8,128)S(1)} %maximum_select_fusion), channel_id=1, source_target_pairs={{0,96},{1,7},{2,98},{3,5},{4,100},{5,3},{6,102},{7,1},{8,104},{9,1... | collective-permute-start | bytes 393224 | tf_op jit(solution)/shard_map/ppermute | solution.py:264
  40.9 4.7 %collective-permute-start.15 = (f32[128,256]{1,0:T(8,128)S(1)}, f32[128,256]{1,0:T(8,128)S(1)}, u32[]{:S(2)}, u32[]{:S(2)}) collective-permute-start(f32[128,256]{1,0:T(8,128)S(1)} %maximum_select_fusion), channel_id=1, source_target_pairs={{0,32},{1,3},{2,34},{3,1},{4,36},{5,7},{6,38},{7,5},{8,40},{9,11},... | collective-permute-start | bytes 393224 | tf_op jit(solution)/shard_map/ppermute | solution.py:264
  41.5 4.2 %collective-permute-start = (s32[98]{0:T(128)S(1)}, s32[98]{0:T(128)S(1)}, u32[]{:S(2)}, u32[]{:S(2)}) collective-permute-start(s32[98]{0:T(128)S(1)} %pad_add_fusion.meta_ref), channel_id=1, source_target_pairs={{0,1},{1,0},{2,3},{3,2},{4,5},{5,4},{6,7},{7,6},{8,9},{9,8},{10,11... | collective-permute-start | bytes 1184 | tf_op jit(solution)/shard_map/ppermute | solution.py:276
  48.3 8.8 %collective-permute-start.19 = (f32[128,256]{1,0:T(8,128)S(1)}, f32[128,256]{1,0:T(8,128)S(1)}, u32[]{:S(2)}, u32[]{:S(2)}) collective-permute-start(f32[128,256]{1,0:T(8,128)S(1)} %chip_both.1), channel_id=1, source_target_pairs={{0,24},{1,97},{2,26},{3,99},{4,28},{5,101},{6,30},{7,103},{8,16},{... | collective-permute-start | bytes 393224 | tf_op jit(solution)/shard_map/ppermute | solution.py:264
  53.8 5.3 %collective-permute-start.20 = (f32[128,256]{1,0:T(8,128)S(1)}, f32[128,256]{1,0:T(8,128)S(1)}, u32[]{:S(2)}, u32[]{:S(2)}) collective-permute-start(f32[128,256]{1,0:T(8,128)S(1)} %chip_both.1), channel_id=1, source_target_pairs={{0,16},{1,65},{2,18},{3,67},{4,20},{5,69},{6,22},{7,71},{8,24},{9,... | collective-permute-start | bytes 393224 | tf_op jit(solution)/shard_map/ppermute | solution.py:264
  54.5 4.6 %collective-permute-start.18 = (f32[128,256]{1,0:T(8,128)S(1)}, f32[128,256]{1,0:T(8,128)S(1)}, u32[]{:S(2)}, u32[]{:S(2)}) collective-permute-start(f32[128,256]{1,0:T(8,128)S(1)} %chip_both.1), channel_id=1, source_target_pairs={{0,8},{1,33},{2,10},{3,35},{4,12},{5,37},{6,14},{7,39},{8,0},{9,41... | collective-permute-start | bytes 393224 | tf_op jit(solution)/shard_map/ppermute | solution.py:264
  62.5 5.7 %collective-permute-start.25 = (f32[128,256]{1,0:T(8,128)S(1)}, f32[128,256]{1,0:T(8,128)S(1)}, u32[]{:S(2)}, u32[]{:S(2)}) collective-permute-start(f32[128,256]{1,0:T(8,128)S(1)} %chip_rows.1), channel_id=1, source_target_pairs={{0,4},{1,17},{2,6},{3,19},{4,0},{5,21},{6,2},{7,23},{8,12},{9,25},... | collective-permute-start | bytes 393224 | tf_op jit(solution)/shard_map/ppermute | solution.py:264
  63.8 5.9 %collective-permute-start.24 = (f32[128,256]{1,0:T(8,128)S(1)}, f32[128,256]{1,0:T(8,128)S(1)}, u32[]{:S(2)}, u32[]{:S(2)}) collective-permute-start(f32[128,256]{1,0:T(8,128)S(1)} %chip_rows.1), channel_id=1, source_target_pairs={{0,6},{1,25},{2,4},{3,27},{4,2},{5,29},{6,0},{7,31},{8,14},{9,17},... | collective-permute-start | bytes 393224 | tf_op jit(solution)/shard_map/ppermute | solution.py:264
  65.5 4.2 %collective-permute-start.23 = (f32[128,256]{1,0:T(8,128)S(1)}, f32[128,256]{1,0:T(8,128)S(1)}, u32[]{:S(2)}, u32[]{:S(2)}) collective-permute-start(f32[128,256]{1,0:T(8,128)S(1)} %chip_rows.1), channel_id=1, source_target_pairs={{0,2},{1,9},{2,0},{3,11},{4,6},{5,13},{6,4},{7,15},{8,10},{9,1},{1... | collective-permute-start | bytes 393224 | tf_op jit(solution)/shard_map/ppermute | solution.py:264
  65.5 12.3 %collective-permute-start.22 = (f32[128,256]{1,0:T(8,128)S(1)}, f32[128,256]{1,0:T(8,128)S(1)}, u32[]{:S(2)}, u32[]{:S(2)}) collective-permute-start(f32[128,256]{1,0:T(8,128)S(1)} %multiply_select_fusion.2.refs_6_), channel_id=1, source_target_pairs={{0,1},{1,0},{2,3},{3,2},{4,5},{5,4},{6,7},{7,6},{8,9},{9,8},{10,11... | collective-permute-start | bytes 393224 | tf_op jit(solution)/shard_map/ppermute | solution.py:276
  70.3 7.6 %collective-permute-start.29 = (f32[128,256]{1,0:T(8,128)S(1)}, f32[128,256]{1,0:T(8,128)S(1)}, u32[]{:S(2)}, u32[]{:S(2)}) collective-permute-start(f32[128,256]{1,0:T(8,128)S(1)} %chip_cols.1), channel_id=1, source_target_pairs={{0,64},{1,5},{2,66},{3,7},{4,68},{5,1},{6,70},{7,3},{8,72},{9,13},... | collective-permute-start | bytes 393224 | tf_op jit(solution)/shard_map/ppermute | solution.py:264
  74.3 5.5 %collective-permute-start.28 = (f32[128,256]{1,0:T(8,128)S(1)}, f32[128,256]{1,0:T(8,128)S(1)}, u32[]{:S(2)}, u32[]{:S(2)}) collective-permute-start(f32[128,256]{1,0:T(8,128)S(1)} %chip_cols.1), channel_id=1, source_target_pairs={{0,96},{1,7},{2,98},{3,5},{4,100},{5,3},{6,102},{7,1},{8,104},{9,1... | collective-permute-start | bytes 393224 | tf_op jit(solution)/shard_map/ppermute | solution.py:264
  76.5 4.6 %collective-permute-start.27 = (f32[128,256]{1,0:T(8,128)S(1)}, f32[128,256]{1,0:T(8,128)S(1)}, u32[]{:S(2)}, u32[]{:S(2)}) collective-permute-start(f32[128,256]{1,0:T(8,128)S(1)} %chip_cols.1), channel_id=1, source_target_pairs={{0,32},{1,3},{2,34},{3,1},{4,36},{5,7},{6,38},{7,5},{8,40},{9,11},... | collective-permute-start | bytes 393224 | tf_op jit(solution)/shard_map/ppermute | solution.py:264
  77.0 4.1 %collective-permute-start.26 = (f32[128,256]{1,0:T(8,128)S(1)}, f32[128,256]{1,0:T(8,128)S(1)}, u32[]{:S(2)}, u32[]{:S(2)}) collective-permute-start(f32[128,256]{1,0:T(8,128)S(1)} %multiply_select_fusion.1.refs_6_), channel_id=1, source_target_pairs={{0,1},{1,0},{2,3},{3,2},{4,5},{5,4},{6,7},{7,6},{8,9},{9,8},{10,11... | collective-permute-start | bytes 393224 | tf_op jit(solution)/shard_map/ppermute | solution.py:276
  83.8 6.0 %collective-permute-start.30 = (f32[128,256]{1,0:T(8,128)S(1)}, f32[128,256]{1,0:T(8,128)S(1)}, u32[]{:S(2)}, u32[]{:S(2)}) collective-permute-start(f32[128,256]{1,0:T(8,128)S(1)} %chip_sums.1), channel_id=1, source_target_pairs={{0,24},{1,97},{2,26},{3,99},{4,28},{5,101},{6,30},{7,103},{8,16},{... | collective-permute-start | bytes 393224 | tf_op jit(solution)/shard_map/ppermute | solution.py:264
  86.6 6.4 %collective-permute-start.33 = (f32[128,256]{1,0:T(8,128)S(1)}, f32[128,256]{1,0:T(8,128)S(1)}, u32[]{:S(2)}, u32[]{:S(2)}) collective-permute-start(f32[128,256]{1,0:T(8,128)S(1)} %chip_sums.1), channel_id=1, source_target_pairs={{0,16},{1,65},{2,18},{3,67},{4,20},{5,69},{6,22},{7,71},{8,24},{9,... | collective-permute-start | bytes 393224 | tf_op jit(solution)/shard_map/ppermute | solution.py:264
  88.2 4.7 %collective-permute-start.32 = (f32[128,256]{1,0:T(8,128)S(1)}, f32[128,256]{1,0:T(8,128)S(1)}, u32[]{:S(2)}, u32[]{:S(2)}) collective-permute-start(f32[128,256]{1,0:T(8,128)S(1)} %chip_sums.1), channel_id=1, source_target_pairs={{0,8},{1,33},{2,10},{3,35},{4,12},{5,37},{6,14},{7,39},{8,0},{9,41... | collective-permute-start | bytes 393224 | tf_op jit(solution)/shard_map/ppermute | solution.py:264
  94.0 4.1 %collective-permute-start.38 = (f32[128,256]{1,0:T(8,128)S(1)}, f32[128,256]{1,0:T(8,128)S(1)}, u32[]{:S(2)}, u32[]{:S(2)}) collective-permute-start(f32[128,256]{1,0:T(8,128)S(1)} %multiply_select_fusion), channel_id=1, source_target_pairs={{0,1},{1,0},{2,3},{3,2},{4,5},{5,4},{6,7},{7,6},{8,9},{9,8},{10,11... | collective-permute-start | bytes 393224 | tf_op jit(solution)/shard_map/ppermute | solution.py:276
  95.3 5.6 %collective-permute-start.36 = (f32[128,256]{1,0:T(8,128)S(1)}, f32[128,256]{1,0:T(8,128)S(1)}, u32[]{:S(2)}, u32[]{:S(2)}) collective-permute-start(f32[128,256]{1,0:T(8,128)S(1)} %multiply_select_fusion), channel_id=1, source_target_pairs={{0,4},{1,17},{2,6},{3,19},{4,0},{5,21},{6,2},{7,23},{8,12},{9,25},... | collective-permute-start | bytes 393224 | tf_op jit(solution)/shard_map/ppermute | solution.py:264
  97.1 5.0 %collective-permute-start.35 = (f32[128,256]{1,0:T(8,128)S(1)}, f32[128,256]{1,0:T(8,128)S(1)}, u32[]{:S(2)}, u32[]{:S(2)}) collective-permute-start(f32[128,256]{1,0:T(8,128)S(1)} %multiply_select_fusion), channel_id=1, source_target_pairs={{0,6},{1,25},{2,4},{3,27},{4,2},{5,29},{6,0},{7,31},{8,14},{9,17},... | collective-permute-start | bytes 393224 | tf_op jit(solution)/shard_map/ppermute | solution.py:264
  98.0 4.0 %collective-permute-start.34 = (f32[128,256]{1,0:T(8,128)S(1)}, f32[128,256]{1,0:T(8,128)S(1)}, u32[]{:S(2)}, u32[]{:S(2)}) collective-permute-start(f32[128,256]{1,0:T(8,128)S(1)} %multiply_select_fusion), channel_id=1, source_target_pairs={{0,2},{1,9},{2,0},{3,11},{4,6},{5,13},{6,4},{7,15},{8,10},{9,1},{1... | collective-permute-start | bytes 393224 | tf_op jit(solution)/shard_map/ppermute | solution.py:264
  102.2 4.1 %collective-permute-start.37 = (f32[128,256]{1,0:T(8,128)S(1)}, f32[128,256]{1,0:T(8,128)S(1)}, u32[]{:S(2)}, u32[]{:S(2)}) collective-permute-start(f32[128,256]{1,0:T(8,128)S(1)} %get-tuple-element.56), channel_id=1, source_target_pairs={{0,1},{1,0},{2,3},{3,2},{4,5},{5,4},{6,7},{7,6},{8,9},{9,8},{10,11... | collective-permute-start | bytes 393224 | tf_op jit(solution)/shard_map/ppermute | solution.py:276
  (7 other events, 15.9 us)
